TPU v7x, 256 devices: a whole 4x4x8 slice. The times are simulated.
256 devices in a mesh: row: 16 (over z, core), col: 16 (over y, x).
Axes of the slice: x: 4, y: 4, z: 8, core: 2. Of those that a mesh axis runs over, the one named last changes fastest.
Arguments:
- vectors: float32 [2048, 48, 512], P(('row', 'col')), may hold values from -6 to 6
- factor_one: float32 [2048, 47, 2048], P('row', None, 'col'), may hold values from -0.125 to 0.125
- factor_two: float32 [2048, 46, 2048], P('row', None, 'col'), may hold values from -0.125 to 0.125
- block_inverse: float32 [2, 2048, 2048], P(None, 'row', 'col'), may hold values from -1 to 2, as said below
- lumped_mass: float32 [2048, 48], P(('row', 'col')), may hold values from 0.25 to 9.5
Outputs:
- solved: float32 [2048, 48, 512], P(('row', 'col'))
- rotated: float32 [2048, 48, 512], P(('row', 'col'))
Inputs may be any that keep to these rules, and one draw needn't show every extreme that they name: Each block of block_inverse is lower triangular with diagonal entries between 0.5 and 2.
All inputs are finite; a program needn't handle non-finite values.
Results may differ from a plain program's by a relative error of at most 0.00013.
Values sent between devices are 32-bit elements; how exact they have to be, the bound alone decides.
No kernel may reach another device: no remote copies, remote signals or barrier semaphores. Data moves between devices by JAX's collectives and lax.ppermute only.
A program may use at most 128 MiB of HBM per device.

v0:
```python
import jax
import jax.numpy as jnp
from jax import lax
from jax.sharding import PartitionSpec as P

ORDER = 98304


def spread(block, axis, holder):
    block = jnp.where(lax.axis_index(axis) == holder, block, jnp.zeros_like(block))
    return lax.psum(block, axis)


def spread_rows(panel_rows):
    grid_block = lax.all_gather(panel_rows, "col", axis=0, tiled=True)
    per_column = lax.axis_size("row") // lax.axis_size("col")
    column = lax.axis_index("col")
    gathered = spread(grid_block, "row", column * per_column + 0)
    return gathered


def solve_panel(panel_rows, inverse_tile):
    needed = spread_rows(panel_rows)
    partial_value = jnp.dot(
        inverse_tile, needed, precision=lax.Precision.HIGHEST, preferred_element_type=jnp.float32
    )
    return lax.psum_scatter(partial_value, "col", scatter_dimension=0, tiled=True)


def trailing(lower_tile, solved_cols):
    return lax.psum_scatter(
        jnp.einsum(
            "jtq,qk->jtk",
            lower_tile,
            solved_cols,
            precision=lax.Precision.HIGHEST,
            preferred_element_type=jnp.float32,
        ),
        "col",
        scatter_dimension=0,
        tiled=True,
    )


def body(vectors, factor_one, factor_two, block_inverse, lumped_mass):
    highest = lax.Precision.HIGHEST
    panel_one = solve_panel(vectors[:, 0, :], block_inverse[0])
    one_cols = spread_rows(panel_one)
    remain = vectors[:, 1:, :] - trailing(factor_one, one_cols)
    panel_two = solve_panel(remain[:, 0, :], block_inverse[1])
    two_cols = spread_rows(panel_two)
    remaining = remain[:, 1:, :] - trailing(factor_two, two_cols)
    solved = jnp.concatenate([panel_one[:, None, :], panel_two[:, None, :], remaining], axis=1)
    weighted = solved * lumped_mass[:, :, None]
    local_gram = jnp.einsum(
        "jtk,jtl->kl", weighted, solved, precision=highest, preferred_element_type=jnp.float32
    )
    mass_gram = lax.psum(local_gram, ("row", "col")) / ORDER
    factor = jnp.linalg.cholesky(mass_gram)
    flattened = solved.reshape(-1, solved.shape[2])
    rotated = jax.scipy.linalg.solve_triangular(factor, flattened.T, lower=True).T
    return (solved, rotated.reshape(solved.shape))


def solution(mesh):
    placed = (
        P(("row", "col"), None, None),
        P("row", None, "col"),
        P("row", None, "col"),
        P(None, "row", "col"),
        P(("row", "col"), None),
    )
    return jax.shard_map(
        body,
        mesh=mesh,
        in_specs=placed,
        out_specs=(P(("row", "col"), None, None), P(("row", "col"), None, None)),
        check_vma=False,
    )
```

profile of v0, /device:TPU:1, one launch (start us, length us, event | category | flops | bytes accessed | tf_op | source)
XLA Modules:
  0.0 1414.6 jit_solution(13320057616582228687)
XLA Ops:
  8.3 19.7 %all-gather = f32[128,1,512]{2,1,0:T(1,128)S(1)} all-gather(f32[8,1,512]{2,1,0:T(1,128)S(1)} %slice.132), channel_id=2, replica_groups=mesh['row'=16,'col'=16] {'col'}, dimensions={0}, use_global_device_ids=true | all-gather | bytes 278528 | tf_op jit(solution)/shard_map/all_gather | solution.py:15
  29.0 114.5 %all-reduce.11.cloned.1.call-done = f32[128,512]{1,0:T(8,128)} async-done(((f32[128,512]{1,0:T(8,128)}), f32[128,512]{1,0:T(8,128)}) %all-reduce.11.cloned.1.call-update) | async-done | bytes 262160 | tf_op jit(solution)/shard_map/psum | solution.py:11
  147.8 93.3 %all-reduce.21.cloned.1.call-done = f32[128,512]{0,1:T(8,128)} async-done(((f32[128,512]{0,1:T(8,128)}), f32[128,512]{0,1:T(8,128)}) %all-reduce.21.cloned.1.call-update) | async-done | bytes 262160
  242.2 18.8 %all_gather.13 = f32[128,512]{1,0:T(8,128)} all-gather(f32[8,512]{1,0:T(8,128)S(1)} %copy.41), channel_id=1, replica_groups=mesh['row'=16,'col'=16] {'col'}, dimensions={0}, use_global_device_ids=true | all-gather | bytes 278528 | tf_op jit(solution)/shard_map/all_gather | solution.py:15
  262.9 114.6 %all-reduce.13.cloned.1.call-done = f32[128,512]{0,1:T(8,128)} async-done(((f32[128,512]{0,1:T(8,128)}), f32[128,512]{0,1:T(8,128)}) %all-reduce.13.cloned.1.call-update) | async-done | bytes 262160 | tf_op jit(solution)/shard_map/psum | solution.py:11
  377.5 13.6 convolution_bitcast_fusion
  391.1 12.7 copy.43
  403.9 99.6 %reduce-scatter.5.cloned.1.call-done = f32[8,47,512]{2,1,0:T(8,128)} async-done(((f32[128,47,512]{2,1,0:T(8,128)}), f32[8,47,512]{2,1,0:T(8,128)}) %reduce-scatter.5.cloned.1.call-update) | async-done | bytes 770064 | tf_op jit(solution)/shard_map/reduce_scatter | solution.py:31
  506.0 16.3 %all-gather.1 = f32[128,1,512]{2,1,0:T(1,128)S(1)} all-gather(f32[8,1,512]{2,1,0:T(1,128)S(1)} %slice.149), channel_id=3, replica_groups=mesh['row'=16,'col'=16] {'col'}, dimensions={0}, use_global_device_ids=true | all-gather | bytes 278528 | tf_op jit(solution)/shard_map/all_gather | solution.py:15
  523.3 114.2 %all-reduce.15.cloned.1.call-done = f32[128,512]{1,0:T(8,128)} async-done(((f32[128,512]{1,0:T(8,128)}), f32[128,512]{1,0:T(8,128)}) %all-reduce.15.cloned.1.call-update) | async-done | bytes 262160 | tf_op jit(solution)/shard_map/psum | solution.py:11
  639.8 94.7 %all-reduce.23.cloned.1.call-done = f32[128,512]{0,1:T(8,128)} async-done(((f32[128,512]{0,1:T(8,128)}), f32[128,512]{0,1:T(8,128)}) %all-reduce.23.cloned.1.call-update) | async-done | bytes 262160
  735.7 18.8 %all_gather.15 = f32[128,512]{1,0:T(8,128)} all-gather(f32[8,512]{1,0:T(8,128)S(1)} %copy.45), channel_id=1, replica_groups=mesh['row'=16,'col'=16] {'col'}, dimensions={0}, use_global_device_ids=true | all-gather | bytes 278528 | tf_op jit(solution)/shard_map/all_gather | solution.py:15
  756.5 114.4 %all-reduce.17.cloned.1.call-done = f32[128,512]{0,1:T(8,128)} async-done(((f32[128,512]{0,1:T(8,128)}), f32[128,512]{0,1:T(8,128)}) %all-reduce.17.cloned.1.call-update) | async-done | bytes 262160 | tf_op jit(solution)/shard_map/psum | solution.py:11
  870.9 13.5 convolution_bitcast_fusion.1
  884.4 12.6 copy.47
  898.4 98.5 %reduce-scatter.7.cloned.1.call-done = f32[8,46,512]{2,1,0:T(8,128)} async-done(((f32[128,46,512]{2,1,0:T(8,128)}), f32[8,46,512]{2,1,0:T(8,128)}) %reduce-scatter.7.cloned.1.call-update) | async-done | bytes 753680 | tf_op jit(solution)/shard_map/reduce_scatter | solution.py:31
  1002.7 253.5 %all-reduce.19.cloned.1.call-done = f32[512,512]{0,1:T(8,128)} async-done(((f32[512,512]{0,1:T(8,128)}), f32[512,512]{0,1:T(8,128)}) %all-reduce.19.cloned.1.call-update) | async-done | bytes 1048592 | tf_op jit(solution)/shard_map/psum | solution.py:58
  1261.5 11.7 cholesky.104
  1285.8 12.1 cholesky.217
  1297.9 9.8 custom-call.32
  1309.3 11.7 cholesky.238
  1333.0 11.9 cholesky.255
  1348.9 10.5 while.1
  1359.5 40.2 %custom-call.34 = f32[4,128,128]{1,2,0:T(8,128)S(1)} custom-call(f32[4,128,128]{2,1,0:T(8,128)} %get-tuple-element.9), custom_call_target="InvertDiagBlocksLowerTriangular" | custom-call | tf_op jit(solution)/shard_map/jit(_solve_triangular)/triangular_solve | solution.py:61
  (119 shorter events, 76.3 us)
Async XLA Ops:
  7.2 370.3 %copy-start = (f32[128,47,128]{2,0,1:T(8,128)S(1)}, f32[128,47,128]{2,0,1:T(8,128)}, u32[]{:S(2)}) copy-start(f32[128,47,128]{2,0,1:T(8,128)} %param.6) | copy-start | bytes 9240580
  7.2 136.4 %all-reduce.11.cloned.1.call-start = ((), (), s32[]{:S(2)}) async-start(), calls=%async_computation.2 | async-start | bytes 524288 | tf_op jit(solution)/shard_map/psum | solution.py:11
  29.0 212.1 %all-reduce.21.cloned.1.call-start = ((), (), s32[]{:S(2)}) async-start(), calls=%async_computation.9 | async-start | bytes 524288
  145.8 231.7 %all-reduce.13.cloned.1.call-start = ((), (), s32[]{:S(2)}) async-start(), calls=%async_computation.3 | async-start | bytes 524288 | tf_op jit(solution)/shard_map/psum | solution.py:11
  262.9 240.7 %reduce-scatter.5.cloned.1.call-start = ((), (), s32[]{:S(2)}) async-start(), calls=%async_computation.4 | async-start | bytes 13369344 | tf_op jit(solution)/shard_map/reduce_scatter | solution.py:31
  403.8 233.6 %copy-start.12 = (f32[2,128,128]{2,1,0:T(8,128)S(1)}, f32[2,128,128]{2,1,0:T(8,128)}, u32[]{:S(2)}) copy-start(f32[2,128,128]{2,1,0:T(8,128)} %param.8) | copy-start | bytes 393220
  403.8 467.1 %copy-start.3 = (f32[128,46,128]{2,0,1:T(8,128)S(1)}, f32[128,46,128]{2,0,1:T(8,128)}, u32[]{:S(2)}) copy-start(f32[128,46,128]{2,0,1:T(8,128)} %param.7) | copy-start | bytes 9043972
  403.8 233.6 %all-reduce.15.cloned.1.call-start = ((), (), s32[]{:S(2)}) async-start(), calls=%async_computation.5 | async-start | bytes 524288 | tf_op jit(solution)/shard_map/psum | solution.py:11
  505.1 0.9 copy-start.5
  523.2 211.3 %all-reduce.23.cloned.1.call-start = ((), (), s32[]{:S(2)}) async-start(), calls=%async_computation.10 | async-start | bytes 524288
  639.7 231.2 %all-reduce.17.cloned.1.call-start = ((), (), s32[]{:S(2)}) async-start(), calls=%async_computation.6 | async-start | bytes 524288 | tf_op jit(solution)/shard_map/psum | solution.py:11
  756.3 240.7 %reduce-scatter.7.cloned.1.call-start = ((), (), s32[]{:S(2)}) async-start(), calls=%async_computation.7 | async-start | bytes 13369344 | tf_op jit(solution)/shard_map/reduce_scatter | solution.py:31
  897.0 0.9 copy-start.10
  897.0 1.2 copy-start.11
  897.0 100.0 %copy-start.6 = (f32[8,47,512]{2,1,0:T(8,128)S(1)}, f32[8,47,512]{2,1,0:T(8,128)}, u32[]{:S(2)}) copy-start(f32[8,47,512]{2,1,0:T(8,128)} %copy-done.5) | copy-start | bytes 2310148
  897.0 101.4 %copy-start.13 = (f32[8,48]{1,0:T(8,128)S(1)}, f32[8,48]{1,0:T(8,128)}, u32[]{:S(2)}) copy-start(f32[8,48]{1,0:T(8,128)} %param.9) | copy-start | bytes 4612
  897.0 359.2 %all-reduce.19.cloned.1.call-start = ((), (), s32[]{:S(2)}) async-start(), calls=%async_computation.8 | async-start | bytes 2097152 | tf_op jit(solution)/shard_map/psum | solution.py:58
  998.4 260.2 %copy-start.2 = (f32[8,48,512]{2,1,0:T(8,128)}, f32[8,48,512]{2,1,0:T(8,128)S(1)}, u32[]{:S(2)}) copy-start(f32[8,48,512]{2,1,0:T(8,128)S(1)} %pad_maximum_fusion) | copy-start | bytes 2359300
  1256.2 4.0 copy-start.4
  1260.5 1.0 copy-start.9
  1284.4 115.3 %copy-start.7 = (f32[384,512]{0,1:T(8,128)S(1)}, f32[384,512]{0,1:T(8,128)}, u32[]{:S(2)}) copy-start(f32[384,512]{0,1:T(8,128)} %copy.50) | copy-start | bytes 2359300
  1359.5 40.6 %copy-start.8 = (f32[512,512]{1,0:T(8,128)}, f32[512,512]{1,0:T(8,128)S(1)}, u32[]{:S(2)}) copy-start(f32[512,512]{1,0:T(8,128)S(1)} %get-tuple-element.98) | copy-start | bytes 3145732
  1400.4 7.5 copy-start.1
Sparse Core Ops, SparseCore 0:
  29.1 114.4 all-reduce.10
  147.6 93.4 all-reduce.20
  263.0 114.4 all-reduce.12
  403.9 99.5 reduce-scatter.4
  523.3 114.0 all-reduce.14
  641.1 93.3 all-reduce.22
  756.4 114.4 all-reduce.16
  897.1 99.7 reduce-scatter.6
  1002.4 253.7 all-reduce.18
where the time goes:
time: 1420 us; the launch traced here: 1410 us
  waiting for transfers between devices  1100 us (77%)
  other arithmetic  128 us (9%)
  blocking collectives  73.5 us (5%)
  local copies, waits for them, and re-layouts  52.5 us (4%)
  matrix products  45.1 us (3%)
  between operations  17.6 us (1%)
    psum x4, waiting for transfers between devices, spread(): return lax.psum(block, axis)  458 us
    psum x1, waiting for transfers between devices, body(): mass_gram = lax.psum(local_gram, ('row', 'col')) / ORDER  254 us
    reduce_scatter x2, waiting for transfers between devices, trailing(): lax.psum_scatter(jnp.einsum('jtq,qk->jtk', lower_tile, solved_cols, preci...  198 us
    unnamed x11, waiting for transfers between devices  188 us
    another operation x14, other arithmetic, body(): factor = jnp.linalg.cholesky(mass_gram)  79 us
    all_gather x4, blocking collectives, spread_rows(): grid_block = lax.all_gather(panel_rows, 'col', axis=0, tiled=True)  73.5 us
    another operation x3, other arithmetic, body(): jax.scipy.linalg.solve_triangular(factor, flattened.T, lower=True)  40.3 us
  transfers between devices with their start and end apart: 9, of which 9 were waited for; matrix products, arithmetic and copies ran while one was open for 0% of the time, Pallas kernels for 0%

commit v1 on v0

v1 whole, which is shorter than its diff:
```python
import jax
import jax.numpy as jnp
from jax import lax
from jax.sharding import PartitionSpec as P

ORDER = 98304
HIGHEST = lax.Precision.HIGHEST


def exchange(blocks, axis):
    return lax.all_to_all(blocks, axis, 0, 0)


def share(block, axis):
    size = lax.axis_size(axis)
    return exchange(jnp.broadcast_to(block[None], (size,) + block.shape), axis)


def product(rows, tiles):
    return jnp.einsum("rkq,riq->ki", rows, tiles, precision=HIGHEST, preferred_element_type=jnp.float32)


def trailing(factor, panel):
    out = jnp.einsum("rjtq,crkq->jtck", factor, panel, precision=HIGHEST, preferred_element_type=jnp.float32)
    return out.reshape(out.shape[:2] + (-1,))


def body(vectors, factor_one, factor_two, block_inverse, lumped_mass):
    rows_n, cols_n = lax.axis_size("row"), lax.axis_size("col")
    row, col = lax.axis_index("row"), lax.axis_index("col")
    core, place = row % 2, row // 2
    own, rounds, k_all = vectors.shape
    tile = own * cols_n
    k_part = k_all // cols_n
    swap = [(i, i ^ 1) for i in range(rows_n)]

    heads = vectors[:, :2, :].reshape(own, 2, cols_n, k_part).transpose(2, 1, 0, 3)
    heads = exchange(heads, "col")
    heads = heads.transpose(1, 3, 0, 2).reshape(2, k_part, tile)
    head_rows = share(heads[0], "row")

    mats = jnp.stack([block_inverse[0], factor_one[:, 0, :], block_inverse[1]])
    mats = share(mats, "col")

    def whole(panel_rows):
        mine = lax.dynamic_index_in_dim(
            panel_rows.reshape((rows_n // 2, 2) + panel_rows.shape[1:]), core, 1, keepdims=False
        )
        mine = share(mine, "col")
        return mine, lax.ppermute(mine, "row", swap)

    def owned(mine):
        block = lax.dynamic_index_in_dim(mine, place, 1, keepdims=False)
        block = lax.dynamic_slice_in_dim(block, col * own, own, 2)
        return block.transpose(2, 0, 1).reshape(own, k_all)

    def halves(factor):
        parts = exchange(factor.reshape((cols_n, own) + factor.shape[1:]), "col")
        parts = parts.reshape((rows_n // 2, 2) + parts.shape[1:])
        return (
            lax.dynamic_index_in_dim(parts, core, 1, keepdims=False),
            lax.dynamic_index_in_dim(parts, 1 - core, 1, keepdims=False),
        )

    one_rows = share(product(head_rows, mats[:, 0]), "row")
    remain_head = heads[1] - product(one_rows, mats[:, 1])
    remain_rows = share(remain_head, "row")
    two_rows = share(product(remain_rows, mats[:, 2]), "row")

    one_mine, one_other = whole(one_rows)
    f_mine, f_other = halves(factor_one)
    remain = vectors[:, 1:, :] - trailing(f_mine, one_mine) - trailing(f_other, one_other)

    two_mine, two_other = whole(two_rows)
    f_mine, f_other = halves(factor_two)
    remaining = remain[:, 1:, :] - trailing(f_mine, two_mine) - trailing(f_other, two_other)

    solved = jnp.concatenate([owned(one_mine)[:, None, :], owned(two_mine)[:, None, :], remaining], axis=1)
    weighted = solved * lumped_mass[:, :, None]
    gram = jnp.einsum("jtk,jtl->kl", weighted, solved, precision=HIGHEST, preferred_element_type=jnp.float32)

    lanes = k_all // 4
    gram = gram.reshape(cols_n, 4, own, 4, lanes).transpose(0, 1, 3, 2, 4)
    gram = exchange(gram, "col").sum(axis=0)
    gram = exchange(gram.reshape(rows_n, own, lanes), "row").sum(axis=0)
    gram = share(share(gram, "row"), "col")
    gram = gram.reshape(cols_n, 4, 4, own, lanes).transpose(0, 1, 3, 2, 4).reshape(k_all, k_all)

    factor = jnp.linalg.cholesky(gram / ORDER)
    flattened = solved.reshape(-1, k_all)
    rotated = jax.scipy.linalg.solve_triangular(factor, flattened.T, lower=True).T
    return (solved, rotated.reshape(solved.shape))


def solution(mesh):
    placed = (
        P(("row", "col"), None, None),
        P("row", None, "col"),
        P("row", None, "col"),
        P(None, "row", "col"),
        P(("row", "col"), None),
    )
    return jax.shard_map(
        body,
        mesh=mesh,
        in_specs=placed,
        out_specs=(P(("row", "col"), None, None), P(("row", "col"), None, None)),
        check_vma=False,
    )
```

time: 1420 us -> 545 us (0.38)
  waiting for transfers between devices: 1100 us -> 203 us
  starting transfers between devices: 0.55 us -> 44.4 us
  blocking collectives: 73.5 us -> 99.2 us
  matrix products: 45.1 us -> 24.2 us
    psum x5 -> x0, waiting for transfers between devices: 711 us -> none  [the longest x4 458 us: spread(): return lax.psum(block, axis)]
    all_to_all x0 -> x9, waiting for transfers between devices: none -> 203 us  [exchange(): return lax.all_to_all(blocks, axis, 0, 0)]
    reduce_scatter x2 -> x0, waiting for transfers between devices: 198 us -> none  [trailing(): lax.psum_scatter(jnp.einsum('jtq,qk->jtk', lower_tile, solved_cols, preci...]
    unnamed x11 -> x0, waiting for transfers between devices: 188 us -> none
    all_to_all x0 -> x5, blocking collectives: none -> 99.2 us  [exchange(): return lax.all_to_all(blocks, axis, 0, 0)]
    all_gather x4 -> x0, blocking collectives: 73.5 us -> none  [spread_rows(): grid_block = lax.all_gather(panel_rows, 'col', axis=0, tiled=True)]
    all_to_all x0 -> x9, starting transfers between devices: none -> 42.5 us  [exchange(): return lax.all_to_all(blocks, axis, 0, 0)]
    dot_general x2 -> x4, local copies, waits for them, and re-layouts: 25.3 us -> 4.2 us  [trailing(): jnp.einsum('rjtq,crkq->jtck', factor, panel, precision=HIGHEST, preferred...]
  transfers between devices with their start and end apart: 9 -> 11, of which waited for: 9 -> 9; matrix products, arithmetic and copies ran while one was open for 0% -> 6% of each run, Pallas kernels for 0% -> 0%
where the time goes in v1:
time: 545 us; the launch traced here: 538 us
  waiting for transfers between devices  203 us (37%)
  other arithmetic  120 us (22%)
  blocking collectives  99.2 us (18%)
  starting transfers between devices  44.4 us (8%)
  local copies, waits for them, and re-layouts  43.5 us (8%)
  matrix products  24.2 us (4%)
    all_to_all x9, waiting for transfers between devices, exchange(): return lax.all_to_all(blocks, axis, 0, 0)  203 us
    all_to_all x5, blocking collectives, exchange(): return lax.all_to_all(blocks, axis, 0, 0)  99.2 us
    another operation x14, other arithmetic, body(): factor = jnp.linalg.cholesky(gram / ORDER)  78.8 us
    all_to_all x9, starting transfers between devices, exchange(): return lax.all_to_all(blocks, axis, 0, 0)  42.5 us
    another operation x3, other arithmetic, body(): jax.scipy.linalg.solve_triangular(factor, flattened.T, lower=True)  39.4 us
    dot_general x4, matrix products, trailing(): jnp.einsum('rjtq,crkq->jtck', factor, panel, precision=HIGHEST, preferred...  13 us
  transfers between devices with their start and end apart: 11, of which 9 were waited for; matrix products, arithmetic and copies ran while one was open for 6% of the time, Pallas kernels for 0%

profile of v1, /device:TPU:1, one launch (start us, length us, event | category | flops | bytes accessed | tf_op | source)
XLA Modules:
  0.0 537.8 jit_solution(17462230371553008969)
XLA Ops:
  1.9 13.9 %all_to_all.70 = f32[16,1,512]{2,1,0:T(1,128)S(1)} all-to-all(f32[16,1,512]{2,1,0:T(1,128)S(1)} %reshape.150), channel_id=1, replica_groups=mesh['row'=16,'col'=16] {'col'}, dimensions={0} | all-to-all | bytes 65536 | tf_op jit(solution)/shard_map/all_to_all | solution.py:11
  17.9 10.6 %all-to-all-start.2 = ((f32[16,32,128]{2,1,0:T(8,128)}), f32[16,32,128]{2,1,0:T(8,128)S(1)}, u32[]{:S(2)}, u32[]{:S(2)}) async-start(f32[16,32,128]{2,1,0:T(8,128)} %broadcast_in_dim.27), calls=%async_computation.2 | async-start | bytes 524288 | tf_op jit(solution)/shard_map/all_to_all | solution.py:11
  29.3 10.8 %all-to-all-done.2 = f32[16,32,128]{2,1,0:T(8,128)S(1)} async-done(((f32[16,32,128]{2,1,0:T(8,128)}), f32[16,32,128]{2,1,0:T(8,128)S(1)}, u32[]{:S(2)}, u32[]{:S(2)}) %all-to-all-start.2) | async-done | bytes 262176 | tf_op jit(solution)/shard_map/all_to_all | solution.py:11
  40.5 43.0 %all_to_all.71 = f32[16,3,128,128]{3,2,1,0:T(8,128)S(1)} all-to-all(f32[16,3,128,128]{3,2,1,0:T(8,128)S(1)} %broadcast_in_dim.25), channel_id=1, replica_groups=mesh['row'=16,'col'=16] {'col'}, dimensions={0} | all-to-all | bytes 6291456 | tf_op jit(solution)/shard_map/all_to_all | solution.py:11
  89.5 11.8 %all-to-all-done.3 = f32[16,32,128]{2,1,0:T(8,128)S(1)} async-done(((f32[16,32,128]{2,1,0:T(8,128)}), f32[16,32,128]{2,1,0:T(8,128)S(1)}, u32[]{:S(2)}, u32[]{:S(2)}) %all-to-all-start.3) | async-done | bytes 262176 | tf_op jit(solution)/shard_map/all_to_all | solution.py:11
  110.9 7.2 %all-to-all-done.5 = f32[16,32,128]{2,1,0:T(8,128)} async-done(((f32[16,32,128]{2,1,0:T(8,128)}), f32[16,32,128]{2,1,0:T(8,128)}, u32[]{:S(2)}, u32[]{:S(2)}) %all-to-all-start.5) | async-done | bytes 262176 | tf_op jit(solution)/shard_map/all_to_all | solution.py:11
  124.7 45.5 %all-to-all-done.9 = f32[16,8,46,128]{3,1,2,0:T(8,128)} async-done(((f32[16,8,46,128]{3,1,2,0:T(8,128)}), f32[16,8,46,128]{3,1,2,0:T(8,128)}, u32[]{:S(2)}, u32[]{:S(2)}) %all-to-all-start.9) | async-done | bytes 3014688 | tf_op jit(solution)/shard_map/all_to_all | solution.py:11
  174.9 11.8 %all-to-all-done.6 = f32[16,32,128]{2,1,0:T(8,128)S(1)} async-done(((f32[16,32,128]{2,1,0:T(8,128)}), f32[16,32,128]{2,1,0:T(8,128)S(1)}, u32[]{:S(2)}, u32[]{:S(2)}) %all-to-all-start.6) | async-done | bytes 262176 | tf_op jit(solution)/shard_map/all_to_all | solution.py:11
  192.6 34.5 %all-to-all-done.4 = f32[16,8,32,128]{3,2,1,0:T(8,128)S(1)} async-done(((f32[16,8,32,128]{3,2,1,0:T(8,128)}), f32[16,8,32,128]{3,2,1,0:T(8,128)S(1)}, u32[]{:S(2)}, u32[]{:S(2)}) %all-to-all-start.4) | async-done | bytes 2097184 | tf_op jit(solution)/shard_map/all_to_all | solution.py:11
  236.5 27.8 %all-to-all-done.7 = f32[16,8,32,128]{3,2,1,0:T(8,128)S(1)} async-done(((f32[16,8,32,128]{3,2,1,0:T(8,128)}), f32[16,8,32,128]{3,2,1,0:T(8,128)S(1)}, u32[]{:S(2)}, u32[]{:S(2)}) %all-to-all-start.7) | async-done | bytes 2097184 | tf_op jit(solution)/shard_map/all_to_all | solution.py:11
  277.0 36.1 %all-to-all-done.8 = f32[16,8,47,128]{3,1,2,0:T(8,128)S(1)} async-done(((f32[16,8,47,128]{3,1,2,0:T(8,128)}), f32[16,8,47,128]{3,1,2,0:T(8,128)S(1)}, u32[]{:S(2)}, u32[]{:S(2)}) %all-to-all-start.8) | async-done | bytes 3080224 | tf_op jit(solution)/shard_map/all_to_all | solution.py:11
  336.3 18.8 %all_to_all.72 = f32[16,4,4,8,128]{4,3,2,1,0:T(8,128)S(1)} all-to-all(f32[16,4,4,8,128]{4,3,2,1,0:T(8,128)S(1)} %bitcast.202), channel_id=1, replica_groups=mesh['row'=16,'col'=16] {'col'}, dimensions={0} | all-to-all | bytes 2097152 | tf_op jit(solution)/shard_map/all_to_all | solution.py:11
  355.2 13.2 %all_to_all.73 = f32[16,8,128]{2,1,0:T(8,128)S(1)} all-to-all(f32[16,8,128]{2,1,0:T(8,128)S(1)} %bitcast.209), channel_id=1, replica_groups=mesh['row'=16,'col'=16] {'row'}, dimensions={0} | all-to-all | bytes 131072 | tf_op jit(solution)/shard_map/all_to_all | solution.py:11
  368.4 10.4 %all_to_all.74 = f32[16,8,128]{2,1,0:T(8,128)S(1)} all-to-all(f32[16,8,128]{2,1,0:T(8,128)S(1)} %broadcast_in_dim.35), channel_id=1, replica_groups=mesh['row'=16,'col'=16] {'row'}, dimensions={0} | all-to-all | bytes 131072 | tf_op jit(solution)/shard_map/all_to_all | solution.py:11
  384.7 17.2 %all-to-all-done.13 = f32[16,16,8,128]{3,2,1,0:T(8,128)S(1)} async-done(((f32[16,16,8,128]{3,2,1,0:T(8,128)}), f32[16,16,8,128]{3,2,1,0:T(8,128)S(1)}, u32[]{:S(2)}, u32[]{:S(2)}) %all-to-all-start.13) | async-done | bytes 1048608 | tf_op jit(solution)/shard_map/all_to_all | solution.py:11
  402.6 11.7 %cholesky.104 = f32[128,128]{1,0:T(8,128)S(1)} custom-call(f32[128,128]{1,0:T(8,128)S(1)} %cholesky.266), custom_call_target="Cholesky" | custom-call | tf_op jit(solution)/shard_map/jit(cholesky)/cholesky | solution.py:89
  414.4 9.8 %custom-call.31 = f32[1,128,128]{1,2,0:T(8,128)S(1)} custom-call(f32[1,128,128]{2,1,0:T(8,128)S(1)} %get-tuple-element.39), custom_call_target="InvertDiagBlocksLowerTriangular" | custom-call | tf_op jit(solution)/shard_map/jit(cholesky)/cholesky | solution.py:89
  424.9 11.7 %cholesky.217 = f32[128,128]{1,0:T(8,128)S(1)} custom-call(f32[128,128]{1,0:T(8,128)S(1)} %cholesky.270), custom_call_target="Cholesky" | custom-call | tf_op jit(solution)/shard_map/jit(cholesky)/cholesky | solution.py:89
  436.7 10.0 %custom-call.32 = f32[1,128,128]{1,2,0:T(8,128)S(1)} custom-call(f32[1,128,128]{2,1,0:T(8,128)S(1)} %get-tuple-element.36), custom_call_target="InvertDiagBlocksLowerTriangular" | custom-call | tf_op jit(solution)/shard_map/jit(cholesky)/cholesky | solution.py:89
  447.3 11.7 %cholesky.238 = f32[128,128]{1,0:T(8,128)S(1)} custom-call(f32[128,128]{1,0:T(8,128)S(1)} %cholesky.275), custom_call_target="Cholesky" | custom-call | tf_op jit(solution)/shard_map/jit(cholesky)/cholesky | solution.py:89
  459.8 9.8 %custom-call.33 = f32[1,128,128]{1,2,0:T(8,128)S(1)} custom-call(f32[1,128,128]{2,1,0:T(8,128)S(1)} %get-tuple-element.33), custom_call_target="InvertDiagBlocksLowerTriangular" | custom-call | tf_op jit(solution)/shard_map/jit(cholesky)/cholesky | solution.py:89
  470.2 11.9 %cholesky.255 = f32[128,128]{1,0:T(8,128)S(1)} custom-call(f32[128,128]{1,0:T(8,128)S(1)} %convolution_subtract_fusion.5), custom_call_target="Cholesky" | custom-call | tf_op jit(solution)/shard_map/jit(cholesky)/cholesky | solution.py:89
  486.1 8.1 %while.1 = (s32[]{:T(128)}, f32[512,512]{1,0:T(8,128)S(1)}, s32[4,2]{0,1:T(2,128)S(1)}, f32[4,128,128]{2,1,0:T(8,128)S(1)}, s32[]{:T(128)}) while((s32[]{:T(128)}, f32[512,512]{1,0:T(8,128)S(1)}, s32[4,2]{0,1:T(2,128)S(1)}, f32[4,128,128]{2,1,0:T(8,128)S(1)}, s32[]{:T(128)}) %tuple.36), condition=%wide.while_cond, body=%wide.while_body.sunk | while | flops 2 | bytes 131181 | solution.py:91
  494.2 39.3 %custom-call.34 = f32[4,128,128]{1,2,0:T(8,128)S(1)} custom-call(f32[4,128,128]{2,1,0:T(8,128)S(1)} %get-tuple-element.9), custom_call_target="InvertDiagBlocksLowerTriangular" | custom-call | tf_op jit(solution)/shard_map/jit(_solve_triangular)/triangular_solve | solution.py:91
  (131 shorter events, 105.3 us)
Async XLA Ops:
  0.6 28.7 %copy-start.10 = (f32[2,128,128]{2,1,0:T(8,128)S(1)}, f32[2,128,128]{2,1,0:T(8,128)}, u32[]{:S(2)}) copy-start(f32[2,128,128]{2,1,0:T(8,128)} %param.8) | copy-start | bytes 393220
  17.9 22.3 %all-to-all-start.2 = ((f32[16,32,128]{2,1,0:T(8,128)}), f32[16,32,128]{2,1,0:T(8,128)S(1)}, u32[]{:S(2)}, u32[]{:S(2)}) async-start(f32[16,32,128]{2,1,0:T(8,128)} %broadcast_in_dim.27), calls=%async_computation.2 | async-start | bytes 524288 | tf_op jit(solution)/shard_map/all_to_all | solution.py:11
  85.4 15.9 %all-to-all-start.3 = ((f32[16,32,128]{2,1,0:T(8,128)}), f32[16,32,128]{2,1,0:T(8,128)S(1)}, u32[]{:S(2)}, u32[]{:S(2)}) async-start(f32[16,32,128]{2,1,0:T(8,128)} %broadcast_in_dim.28), calls=%async_computation.3 | async-start | bytes 524288 | tf_op jit(solution)/shard_map/all_to_all | solution.py:11
  103.1 15.0 %all-to-all-start.5 = ((f32[16,32,128]{2,1,0:T(8,128)}), f32[16,32,128]{2,1,0:T(8,128)}, u32[]{:S(2)}, u32[]{:S(2)}) async-start(f32[16,32,128]{2,1,0:T(8,128)} %broadcast_in_dim.31), calls=%async_computation.5 | async-start | bytes 524288 | tf_op jit(solution)/shard_map/all_to_all | solution.py:11
  118.1 52.0 %all-to-all-start.9 = ((f32[16,8,46,128]{3,1,2,0:T(8,128)}), f32[16,8,46,128]{3,1,2,0:T(8,128)}, u32[]{:S(2)}, u32[]{:S(2)}) async-start(f32[16,8,46,128]{3,1,2,0:T(8,128)} %copy.108), calls=%async_computation.9 | async-start | bytes 6029312 | tf_op jit(solution)/shard_map/all_to_all | solution.py:11
  170.9 15.8 %all-to-all-start.6 = ((f32[16,32,128]{2,1,0:T(8,128)}), f32[16,32,128]{2,1,0:T(8,128)S(1)}, u32[]{:S(2)}, u32[]{:S(2)}) async-start(f32[16,32,128]{2,1,0:T(8,128)} %broadcast_in_dim.32), calls=%async_computation.6 | async-start | bytes 524288 | tf_op jit(solution)/shard_map/all_to_all | solution.py:11
  188.3 38.8 %all-to-all-start.4 = ((f32[16,8,32,128]{3,2,1,0:T(8,128)}), f32[16,8,32,128]{3,2,1,0:T(8,128)S(1)}, u32[]{:S(2)}, u32[]{:S(2)}) async-start(f32[16,8,32,128]{3,2,1,0:T(8,128)} %broadcast_in_dim.30), calls=%async_computation.4 | async-start | bytes 4194304 | tf_op jit(solution)/shard_map/all_to_all | solution.py:11
  227.1 2.0 copy-start.2
  229.1 35.2 %all-to-all-start.7 = ((f32[16,8,32,128]{3,2,1,0:T(8,128)}), f32[16,8,32,128]{3,2,1,0:T(8,128)S(1)}, u32[]{:S(2)}, u32[]{:S(2)}) async-start(f32[16,8,32,128]{3,2,1,0:T(8,128)} %broadcast_in_dim.34), calls=%async_computation.7 | async-start | bytes 4194304 | tf_op jit(solution)/shard_map/all_to_all | solution.py:11
  264.3 1.3 copy-start
  265.6 47.6 %all-to-all-start.8 = ((f32[16,8,47,128]{3,1,2,0:T(8,128)}), f32[16,8,47,128]{3,1,2,0:T(8,128)S(1)}, u32[]{:S(2)}, u32[]{:S(2)}) async-start(f32[16,8,47,128]{3,1,2,0:T(8,128)} %copy.103), calls=%async_computation.8 | async-start | bytes 6160384 | tf_op jit(solution)/shard_map/all_to_all | solution.py:11
  269.4 51.7 %collective-permute-start = (f32[16,8,32,128]{3,2,1,0:T(8,128)}, f32[16,8,32,128]{3,2,1,0:T(8,128)}, u32[]{:S(2)}, u32[]{:S(2)}) collective-permute-start(f32[16,8,32,128]{3,2,1,0:T(8,128)} %copy-done.2), channel_id=1, source_target_pairs={{0,16},{16,0},{32,48},{48,32},{64,80},{80,64},{96,112},{112,96},{1... | collective-permute-start | bytes 6291464 | tf_op jit(solution)/shard_map/ppermute | solution.py:50
  271.0 57.9 %collective-permute-start.1 = (f32[16,8,32,128]{3,2,1,0:T(8,128)}, f32[16,8,32,128]{3,2,1,0:T(8,128)}, u32[]{:S(2)}, u32[]{:S(2)}) collective-permute-start(f32[16,8,32,128]{3,2,1,0:T(8,128)} %copy-done), channel_id=1, source_target_pairs={{0,16},{16,0},{32,48},{48,32},{64,80},{80,64},{96,112},{112,96},{1... | collective-permute-start | bytes 6291464 | tf_op jit(solution)/shard_map/ppermute | solution.py:50
  313.2 2.6 copy-start.3
  316.2 4.4 copy-start.1
  321.1 2.0 copy-start.6
  323.1 2.8 copy-start.5
  323.1 2.9 copy-start.9
  329.0 2.0 copy-start.4
  331.0 3.0 copy-start.11
  334.0 49.5 %copy-start.7 = (f32[8,48,512]{2,1,0:T(8,128)}, f32[8,48,512]{2,1,0:T(8,128)S(1)}, u32[]{:S(2)}) copy-start(f32[8,48,512]{2,1,0:T(8,128)S(1)} %pad_maximum_fusion) | copy-start | bytes 2359300
  379.8 22.1 %all-to-all-start.13 = ((f32[16,16,8,128]{3,2,1,0:T(8,128)}), f32[16,16,8,128]{3,2,1,0:T(8,128)S(1)}, u32[]{:S(2)}, u32[]{:S(2)}) async-start(f32[16,16,8,128]{3,2,1,0:T(8,128)} %broadcast_in_dim.36), calls=%async_computation.13 | async-start | bytes 2097152 | tf_op jit(solution)/shard_map/all_to_all | solution.py:11
  447.3 86.2 %copy-start.8 = (f32[384,512]{0,1:T(8,128)S(1)}, f32[384,512]{0,1:T(8,128)}, u32[]{:S(2)}) copy-start(f32[384,512]{0,1:T(8,128)} %copy.114) | copy-start | bytes 2359300

commit v2 on v1

--- a/solution.py
+++ b/solution.py
@@ -1,10 +1,89 @@
+import functools
 import jax
 import jax.numpy as jnp
 from jax import lax
+from jax.experimental import pallas as pl
+from jax.experimental.pallas import tpu as pltpu
 from jax.sharding import PartitionSpec as P
 
 ORDER = 98304
 HIGHEST = lax.Precision.HIGHEST
+
+
+G=8
+def small_dot(a,b,ca,cb):
+    return lax.dot_general(a,b,(((ca,),(cb,)),((),())),precision=HIGHEST,preferred_element_type=jnp.float32)
+
+def invert_block(a_ref, b_ref):
+    n=a_ref.shape[0]
+    full=(G,n)
+    for g in range(n//G):
+        lo=g*G
+        block=a_ref[lo:lo+G,:]
+        d={(i,j): jnp.broadcast_to(block[i:i+1,lo+j:lo+j+1],full) for i in range(G) for j in range(i+1)}
+        a=[jnp.broadcast_to(block[j:j+1,:],full) for j in range(G)]
+        bb=b_ref[lo:lo+G,:]
+        b=[jnp.broadcast_to(bb[j:j+1,:],full) for j in range(G)]
+        r={}
+        for j in range(G):
+            r[j]=lax.rsqrt(d[j,j])
+            for i in range(j+1,G):
+                d[i,j]=d[i,j]*r[j]
+            for i in range(j+1,G):
+                for k in range(i,G):
+                    d[k,i]=d[k,i]-d[k,j]*d[i,j]
+            a[j]=a[j]*r[j]; b[j]=b[j]*r[j]
+            for i in range(j+1,G):
+                a[i]=a[i]-d[i,j]*a[j]; b[i]=b[i]-d[i,j]*b[j]
+        sub=lax.broadcasted_iota(jnp.int32,full,0)
+        outb=b[0]
+        for j in range(1,G): outb=jnp.where(sub==j,b[j],outb)
+        b_ref[lo:lo+G,:]=outb
+        for h in range(g+1,n//G):
+            hs=slice(h*G,h*G+G)
+            ah=a_ref[hs,:]; bh=b_ref[hs,:]
+            c=[jnp.broadcast_to(ah[:,lo+j:lo+j+1],full) for j in range(G)]
+            for j in range(G):
+                c[j]=c[j]*r[j]
+                for i in range(j+1,G):
+                    c[i]=c[i]-d[i,j]*c[j]
+                ah=ah-c[j]*a[j]; bh=bh-c[j]*b[j]
+            a_ref[hs,:]=ah; b_ref[hs,:]=bh
+
+def kernel(scale, gram_ref, out_ref, a_ref, s_ref, t_ref):
+    n=gram_ref.shape[0]; nb=128
+    a_ref[...]=gram_ref[...]*scale
+    out_ref[...]=jnp.where(lax.broadcasted_iota(jnp.int32,(n,n),0)==lax.broadcasted_iota(jnp.int32,(n,n),1),1.0,0.0)
+    def one(b,_):
+        at=pl.multiple_of(b*nb,nb)
+        rows=pl.ds(at,nb)
+        s_ref[...]=a_ref[rows,rows]
+        t_ref[...]=jnp.where(lax.broadcasted_iota(jnp.int32,(nb,nb),0)==lax.broadcasted_iota(jnp.int32,(nb,nb),1),1.0,0.0)
+        invert_block(s_ref,t_ref)
+        inv=t_ref[...]
+        u=small_dot(inv,a_ref[rows,:],1,0)
+        x=small_dot(inv,out_ref[rows,:],1,0)
+        out_ref[rows,:]=x
+        below=lax.broadcasted_iota(jnp.int32,(nb,n),1)>=at+nb
+        uu=jnp.where(below,u,0.0)
+        def rest(i,_):
+            r2=pl.ds(pl.multiple_of(i*nb,nb),nb)
+            ui=small_dot(inv,a_ref[rows,r2],1,0)
+            a_ref[r2,:]=a_ref[r2,:]-small_dot(ui,uu,0,0)
+            out_ref[r2,:]=out_ref[r2,:]-small_dot(ui,x,0,0)
+            return 0
+        lax.fori_loop(b+1,n//nb,rest,0)
+        return 0
+    lax.fori_loop(0,n//nb,one,0)
+
+def inverse_factor(gram, scale):
+    n=gram.shape[0]
+    return pl.pallas_call(functools.partial(kernel,scale),
+        out_shape=jax.ShapeDtypeStruct((n,n),jnp.float32),
+        in_specs=[pl.BlockSpec(memory_space=pltpu.VMEM)],
+        out_specs=pl.BlockSpec(memory_space=pltpu.VMEM),
+        scratch_shapes=[pltpu.VMEM((n,n),jnp.float32),pltpu.VMEM((128,128),jnp.float32),pltpu.VMEM((128,128),jnp.float32)],
+        compiler_params=pltpu.CompilerParams(vmem_limit_bytes=16*1024*1024))(gram)
 
 
 def exchange(blocks, axis):
@@ -40,13 +119,13 @@
     head_rows = share(heads[0], "row")
 
     mats = jnp.stack([block_inverse[0], factor_one[:, 0, :], block_inverse[1]])
-    mats = share(mats, "col")
+    mats = lax.all_gather(mats, "col")
 
     def whole(panel_rows):
         mine = lax.dynamic_index_in_dim(
             panel_rows.reshape((rows_n // 2, 2) + panel_rows.shape[1:]), core, 1, keepdims=False
         )
-        mine = share(mine, "col")
+        mine = lax.all_gather(mine, "col")
         return mine, lax.ppermute(mine, "row", swap)
 
     def owned(mine):
@@ -62,18 +141,17 @@
             lax.dynamic_index_in_dim(parts, 1 - core, 1, keepdims=False),
         )
 
+    f_one = halves(factor_one)
+    mats, f_one = lax.optimization_barrier((mats, f_one))
     one_rows = share(product(head_rows, mats[:, 0]), "row")
+    one_mine, one_other = whole(one_rows)
     remain_head = heads[1] - product(one_rows, mats[:, 1])
     remain_rows = share(remain_head, "row")
     two_rows = share(product(remain_rows, mats[:, 2]), "row")
-
-    one_mine, one_other = whole(one_rows)
-    f_mine, f_other = halves(factor_one)
-    remain = vectors[:, 1:, :] - trailing(f_mine, one_mine) - trailing(f_other, one_other)
-
     two_mine, two_other = whole(two_rows)
-    f_mine, f_other = halves(factor_two)
-    remaining = remain[:, 1:, :] - trailing(f_mine, two_mine) - trailing(f_other, two_other)
+    f_two = halves(factor_two)
+    remain = vectors[:, 1:, :] - trailing(f_one[0], one_mine) - trailing(f_one[1], one_other)
+    remaining = remain[:, 1:, :] - trailing(f_two[0], two_mine) - trailing(f_two[1], two_other)
 
     solved = jnp.concatenate([owned(one_mine)[:, None, :], owned(two_mine)[:, None, :], remaining], axis=1)
     weighted = solved * lumped_mass[:, :, None]
@@ -86,10 +164,9 @@
     gram = share(share(gram, "row"), "col")
     gram = gram.reshape(cols_n, 4, 4, own, lanes).transpose(0, 1, 3, 2, 4).reshape(k_all, k_all)
 
-    factor = jnp.linalg.cholesky(gram / ORDER)
-    flattened = solved.reshape(-1, k_all)
-    rotated = jax.scipy.linalg.solve_triangular(factor, flattened.T, lower=True).T
-    return (solved, rotated.reshape(solved.shape))
+    inverse = inverse_factor(gram, 1.0 / ORDER)
+    rotated = jnp.einsum("jtk,lk->jtl", solved, inverse, precision=HIGHEST, preferred_element_type=jnp.float32)
+    return (solved, rotated)
 
 
 def solution(mesh):

time: 545 us -> 388 us (0.71)
  other arithmetic: 120 us -> 2.96 us
  waiting for transfers between devices: 203 us -> 137 us
  Pallas kernels: 0 us -> 26.8 us
  local copies, waits for them, and re-layouts: 43.5 us -> 32.1 us
  between operations: 3.9 us -> 14.5 us
  matrix products: 24.2 us -> 34.1 us
  blocking collectives: 99.2 us -> 90.8 us
    all_to_all x9 -> x5, waiting for transfers between devices: 203 us -> 72.6 us  [exchange(): return lax.all_to_all(blocks, axis, 0, 0)]
    another operation x17 -> x0, other arithmetic: 118 us -> none  [the longest x14 78.8 us: body(): factor = jnp.linalg.cholesky(gram / ORDER)]
    all_gather x0 -> x3, waiting for transfers between devices: none -> 63.9 us  [the longest x2 60.3 us: whole(): mine = lax.all_gather(mine, 'col')]
    pallas_call x0 -> x1, Pallas kernels: none -> 26.8 us  [inverse_factor(): pl.pallas_call(functools.partial(kernel, scale), out_shape=jax.ShapeDtype...]
    all_to_all x9 -> x5, starting transfers between devices: 42.5 us -> 28.5 us  [exchange(): return lax.all_to_all(blocks, axis, 0, 0)]
    ppermute x2, starting transfers between devices: 1.93 us -> 15 us  [whole(): return (mine, lax.ppermute(mine, 'row', swap))]
    dot_general x4, matrix products: 13 us -> 22.4 us  [trailing(): jnp.einsum('rjtq,crkq->jtck', factor, panel, precision=HIGHEST, preferred...]
    all_to_all x5 -> x6, blocking collectives: 99.2 us -> 90.8 us  [exchange(): return lax.all_to_all(blocks, axis, 0, 0)]
  transfers between devices with their start and end apart: 11 -> 10, of which waited for: 9 -> 7; matrix products, arithmetic and copies ran while one was open for 6% -> 13% of each run, Pallas kernels for 0% -> 0%
where the time goes in v2:
time: 388 us; the launch traced here: 382 us
  waiting for transfers between devices  137 us (35%)
  blocking collectives  90.8 us (23%)
  starting transfers between devices  43.7 us (11%)
  matrix products  34.1 us (9%)
  local copies, waits for them, and re-layouts  32.1 us (8%)
  Pallas kernels  26.8 us (7%)
  between operations  14.5 us (4%)
    all_to_all x6, blocking collectives, exchange(): return lax.all_to_all(blocks, axis, 0, 0)  90.8 us
    all_to_all x5, waiting for transfers between devices, exchange(): return lax.all_to_all(blocks, axis, 0, 0)  72.6 us
    all_gather x2, waiting for transfers between devices, whole(): mine = lax.all_gather(mine, 'col')  60.3 us
    all_to_all x5, starting transfers between devices, exchange(): return lax.all_to_all(blocks, axis, 0, 0)  28.5 us
    pallas_call x1, Pallas kernels, inverse_factor(): pl.pallas_call(functools.partial(kernel, scale), out_shape=jax.ShapeDtype...  26.8 us
    dot_general x4, matrix products, trailing(): jnp.einsum('rjtq,crkq->jtck', factor, panel, precision=HIGHEST, preferred...  22.4 us
    ppermute x2, starting transfers between devices, whole(): return (mine, lax.ppermute(mine, 'row', swap))  15 us
  transfers between devices with their start and end apart: 10, of which 7 were waited for; matrix products, arithmetic and copies ran while one was open for 13% of the time, Pallas kernels for 0%

profile of v2, /device:TPU:1, one launch (start us, length us, event | category | flops | bytes accessed | tf_op | source)
XLA Modules:
  0.0 381.5 jit_solution(1921036103569391543)
XLA Ops:
  11.5 7.6 %all-to-all-start.1 = ((f32[16,1,512]{2,1,0:T(1,128)}), f32[16,1,512]{2,1,0:T(1,128)S(1)}, u32[]{:S(2)}, u32[]{:S(2)}) async-start(f32[16,1,512]{2,1,0:T(1,128)} %reshape.93), calls=%async_computation.1 | async-start | bytes 65536 | tf_op jit(solution)/shard_map/all_to_all | solution.py:90
  19.1 3.7 copy.144
  22.8 2.8 all-to-all-done.1
  25.5 3.9 %all-to-all-start = ((f32[16,8,47,128]{3,1,2,0:T(8,128)}), f32[16,8,47,128]{3,1,2,0:T(8,128)S(1)}, u32[]{:S(2)}, u32[]{:S(2)}) async-start(f32[16,8,47,128]{3,1,2,0:T(8,128)} %copy.144), calls=%async_computation | async-start | bytes 6160384 | tf_op jit(solution)/shard_map/all_to_all | solution.py:90
  30.9 46.5 %all-to-all-done = f32[16,8,47,128]{3,1,2,0:T(8,128)S(1)} async-done(((f32[16,8,47,128]{3,1,2,0:T(8,128)}), f32[16,8,47,128]{3,1,2,0:T(8,128)S(1)}, u32[]{:S(2)}, u32[]{:S(2)}) %all-to-all-start) | async-done | bytes 3080224 | tf_op jit(solution)/shard_map/all_to_all | solution.py:90
  78.1 9.2 %all-to-all-start.2 = ((f32[16,32,128]{2,1,0:T(8,128)}), f32[16,32,128]{2,1,0:T(8,128)S(1)}, u32[]{:S(2)}, u32[]{:S(2)}) async-start(f32[16,32,128]{2,1,0:T(8,128)} %broadcast_in_dim.15), calls=%async_computation.2 | async-start | bytes 524288 | tf_op jit(solution)/shard_map/all_to_all | solution.py:90
  90.0 3.6 all-gather.7.cloned.1.call-done
  93.6 5.5 %all-to-all-done.2 = f32[16,32,128]{2,1,0:T(8,128)S(1)} async-done(((f32[16,32,128]{2,1,0:T(8,128)}), f32[16,32,128]{2,1,0:T(8,128)S(1)}, u32[]{:S(2)}, u32[]{:S(2)}) %all-to-all-start.2) | async-done | bytes 262176 | tf_op jit(solution)/shard_map/all_to_all | solution.py:90
  101.4 14.4 %all_to_all.55 = f32[16,32,128]{2,1,0:T(8,128)S(1)} all-to-all(f32[16,32,128]{2,1,0:T(8,128)S(1)} %broadcast_in_dim.16), channel_id=1, replica_groups=mesh['row'=16,'col'=16] {'row'}, dimensions={0} | all-to-all | bytes 524288 | tf_op jit(solution)/shard_map/all_to_all | solution.py:90
  119.2 14.4 %all_to_all.56 = f32[16,32,128]{2,1,0:T(8,128)S(1)} all-to-all(f32[16,32,128]{2,1,0:T(8,128)S(1)} %broadcast_in_dim.17), channel_id=1, replica_groups=mesh['row'=16,'col'=16] {'row'}, dimensions={0} | all-to-all | bytes 524288 | tf_op jit(solution)/shard_map/all_to_all | solution.py:90
  136.0 14.4 %all_to_all.57 = f32[16,32,128]{2,1,0:T(8,128)S(1)} all-to-all(f32[16,32,128]{2,1,0:T(8,128)S(1)} %broadcast_in_dim.18), channel_id=1, replica_groups=mesh['row'=16,'col'=16] {'row'}, dimensions={0} | all-to-all | bytes 524288 | tf_op jit(solution)/shard_map/all_to_all | solution.py:90
  152.9 4.1 %all-to-all-start.6 = ((f32[16,8,46,128]{3,1,2,0:T(8,128)}), f32[16,8,46,128]{3,1,2,0:T(8,128)S(1)}, u32[]{:S(2)}, u32[]{:S(2)}) async-start(f32[16,8,46,128]{3,1,2,0:T(8,128)} %copy.161), calls=%async_computation.6 | async-start | bytes 6029312 | tf_op jit(solution)/shard_map/all_to_all | solution.py:90
  159.7 13.4 %collective-permute-start = (f32[16,8,32,128]{3,2,1,0:T(8,128)}, f32[16,8,32,128]{3,2,1,0:T(8,128)}, u32[]{:S(2)}, u32[]{:S(2)}) collective-permute-start(f32[16,8,32,128]{3,2,1,0:T(8,128)} %bitcast.144), channel_id=1, source_target_pairs={{0,16},{16,0},{32,48},{48,32},{64,80},{80,64},{96,112},{112,96},{1... | collective-permute-start | bytes 6291464 | tf_op jit(solution)/shard_map/ppermute | solution.py:129
  173.1 57.6 %all-gather.11.cloned.1.call-done = f32[128,1,32,128]{3,2,1,0:T(8,128)} async-done(((f32[8,1,32,128]{3,2,1,0:T(8,128)}), f32[128,1,32,128]{3,2,1,0:T(8,128)}) %all-gather.11.cloned.1.call-update) | async-done | bytes 2097168 | tf_op jit(solution)/shard_map/all_gather | solution.py:128
  237.7 6.7 %fusion.3 = f32[8,47,16,32,1]{1,3,4,2,0:T(8,128)S(1)} fusion(f32[16,8,32,128,1]{3,2,1,0,4:T(8,128)S(1)} %bitcast.146, f32[8,8,47,128]{3,2,0,1:T(8,128)S(1)} %copy-done.7), kind=kOutput, calls=%fused_computation.3 | convolution fusion | flops 2365587456 | bytes 4407296 | tf_op jit(solution)/shard_map/rjtq,crkq->jtck/dot_general | solution.py:103
  250.9 4.3 %fusion.11 = f32[8,46,512]{2,1,0:T(8,128)S(1)} fusion(f32[512,128,8,1]{1,0,2,3:T(8,128)S(1)} %bitcast.124, f32[8,1,8,46,128]{4,2,3,1,0:T(8,128)} %get-tuple-element.14), kind=kOutput, calls=%fused_computation.13 | convolution fusion | flops 2315255808 | bytes 4358144 | tf_op jit(solution)/shard_map/rjtq,crkq->jtck/dot_general | solution.py:103
  255.3 8.5 %fusion = f32[8,47,16,32,1]{1,3,4,2,0:T(8,128)S(1)} fusion(f32[16,8,32,128]{3,2,1,0:T(8,128)} %collective-permute-done, f32[8,8,47,128]{3,2,0,1:T(8,128)S(1)} %copy-done.6), kind=kOutput, calls=%fused_computation | convolution fusion | flops 2365587456 | bytes 4407296 | tf_op jit(solution)/shard_map/rjtq,crkq->jtck/dot_general | solution.py:103
  268.0 2.8 fusion.14
  274.5 21.2 %all_to_all.58 = f32[16,4,4,8,128]{4,3,2,1,0:T(8,128)S(1)} all-to-all(f32[16,4,4,8,128]{4,3,2,1,0:T(8,128)S(1)} %bitcast.137), channel_id=1, replica_groups=mesh['row'=16,'col'=16] {'col'}, dimensions={0} | all-to-all | bytes 2097152 | tf_op jit(solution)/shard_map/all_to_all | solution.py:90
  295.8 16.0 %all_to_all.59 = f32[16,8,128]{2,1,0:T(8,128)S(1)} all-to-all(f32[16,8,128]{2,1,0:T(8,128)S(1)} %bitcast.143), channel_id=1, replica_groups=mesh['row'=16,'col'=16] {'row'}, dimensions={0} | all-to-all | bytes 131072 | tf_op jit(solution)/shard_map/all_to_all | solution.py:90
  311.8 10.4 %all_to_all.60 = f32[16,8,128]{2,1,0:T(8,128)S(1)} all-to-all(f32[16,8,128]{2,1,0:T(8,128)S(1)} %broadcast_in_dim.19), channel_id=1, replica_groups=mesh['row'=16,'col'=16] {'row'}, dimensions={0} | all-to-all | bytes 131072 | tf_op jit(solution)/shard_map/all_to_all | solution.py:90
  323.4 3.7 all-to-all-start.10
  327.6 17.9 %all-to-all-done.10 = f32[16,16,8,128]{3,2,1,0:T(8,128)S(1)} async-done(((f32[16,16,8,128]{3,2,1,0:T(8,128)}), f32[16,16,8,128]{3,2,1,0:T(8,128)S(1)}, u32[]{:S(2)}, u32[]{:S(2)}) %all-to-all-start.10) | async-done | bytes 1048608 | tf_op jit(solution)/shard_map/all_to_all | solution.py:90
  345.4 26.8 %shard_map.68 = f32[512,512]{1,0:T(8,128)S(1)} custom-call(f32[512,512]{1,0:T(8,128)S(1)} %bitcast.121), custom_call_target="tpu_custom_call" | custom-call | tf_op jit(solution)/shard_map/pallas_call | solution.py:81
  (79 shorter events, 47.5 us)
Async XLA Ops:
  7.2 86.5 %all-gather.7.cloned.1.call-start = ((), (), s32[]{:S(2)}) async-start(), calls=%async_computation.11 | async-start | bytes 3342336 | tf_op jit(solution)/shard_map/all_gather | solution.py:122
  11.5 14.1 %all-to-all-start.1 = ((f32[16,1,512]{2,1,0:T(1,128)}), f32[16,1,512]{2,1,0:T(1,128)S(1)}, u32[]{:S(2)}, u32[]{:S(2)}) async-start(f32[16,1,512]{2,1,0:T(1,128)} %reshape.93), calls=%async_computation.1 | async-start | bytes 65536 | tf_op jit(solution)/shard_map/all_to_all | solution.py:90
  25.5 51.9 %all-to-all-start = ((f32[16,8,47,128]{3,1,2,0:T(8,128)}), f32[16,8,47,128]{3,1,2,0:T(8,128)S(1)}, u32[]{:S(2)}, u32[]{:S(2)}) async-start(f32[16,8,47,128]{3,1,2,0:T(8,128)} %copy.144), calls=%async_computation | async-start | bytes 6160384 | tf_op jit(solution)/shard_map/all_to_all | solution.py:90
  78.1 21.0 %all-to-all-start.2 = ((f32[16,32,128]{2,1,0:T(8,128)}), f32[16,32,128]{2,1,0:T(8,128)S(1)}, u32[]{:S(2)}, u32[]{:S(2)}) async-start(f32[16,32,128]{2,1,0:T(8,128)} %broadcast_in_dim.15), calls=%async_computation.2 | async-start | bytes 524288 | tf_op jit(solution)/shard_map/all_to_all | solution.py:90
  87.4 72.3 %all-gather.9.cloned.1.call-start = ((), (), s32[]{:S(2)}) async-start(), calls=%async_computation.12 | async-start | bytes 2228224 | tf_op jit(solution)/shard_map/all_gather | solution.py:128
  116.5 114.2 %all-gather.11.cloned.1.call-start = ((), (), s32[]{:S(2)}) async-start(), calls=%async_computation.13 | async-start | bytes 2228224 | tf_op jit(solution)/shard_map/all_gather | solution.py:128
  116.6 34.4 %copy-start.3 = (f32[128,46,128]{2,0,1:T(8,128)S(1)}, f32[128,46,128]{2,0,1:T(8,128)}, u32[]{:S(2)}) copy-start(f32[128,46,128]{2,0,1:T(8,128)} %param.7) | copy-start | bytes 9043972
  152.9 81.6 %copy-start.9 = (f32[8,48]{1,0:T(8,128)S(1)}, f32[8,48]{1,0:T(8,128)}, u32[]{:S(2)}) copy-start(f32[8,48]{1,0:T(8,128)} %param.9) | copy-start | bytes 4612
  152.9 81.7 %all-to-all-start.6 = ((f32[16,8,46,128]{3,1,2,0:T(8,128)}), f32[16,8,46,128]{3,1,2,0:T(8,128)S(1)}, u32[]{:S(2)}, u32[]{:S(2)}) async-start(f32[16,8,46,128]{3,1,2,0:T(8,128)} %copy.161), calls=%async_computation.6 | async-start | bytes 6029312 | tf_op jit(solution)/shard_map/all_to_all | solution.py:90
  159.7 95.5 %collective-permute-start = (f32[16,8,32,128]{3,2,1,0:T(8,128)}, f32[16,8,32,128]{3,2,1,0:T(8,128)}, u32[]{:S(2)}, u32[]{:S(2)}) collective-permute-start(f32[16,8,32,128]{3,2,1,0:T(8,128)} %bitcast.144), channel_id=1, source_target_pairs={{0,16},{16,0},{32,48},{48,32},{64,80},{80,64},{96,112},{112,96},{1... | collective-permute-start | bytes 6291464 | tf_op jit(solution)/shard_map/ppermute | solution.py:129
  230.7 35.3 %collective-permute-start.1 = (f32[16,8,32,128]{3,2,1,0:T(8,128)}, f32[16,8,32,128]{3,2,1,0:T(8,128)}, u32[]{:S(2)}, u32[]{:S(2)}) collective-permute-start(f32[16,8,32,128]{3,2,1,0:T(8,128)} %bitcast.131), channel_id=1, source_target_pairs={{0,16},{16,0},{32,48},{48,32},{64,80},{80,64},{96,112},{112,96},{1... | collective-permute-start | bytes 6291464 | tf_op jit(solution)/shard_map/ppermute | solution.py:129
  234.6 2.0 copy-start.7
  234.6 3.2 copy-start.8
  250.9 4.3 %copy-start.6 = (f32[8,8,47,128]{3,2,0,1:T(8,128)S(1)}, f32[8,8,47,128]{3,2,0,1:T(8,128)}, u32[]{:S(2)}) copy-start(f32[8,8,47,128]{3,2,0,1:T(8,128)} %get-tuple-element.7) | copy-start | bytes 4620292
  266.0 2.0 copy-start
  268.0 2.8 copy-start.1
  268.0 2.9 copy-start.4
  268.0 2.9 copy-start.5
  323.4 22.1 %all-to-all-start.10 = ((f32[16,16,8,128]{3,2,1,0:T(8,128)}), f32[16,16,8,128]{3,2,1,0:T(8,128)S(1)}, u32[]{:S(2)}, u32[]{:S(2)}) async-start(f32[16,16,8,128]{3,2,1,0:T(8,128)} %broadcast_in_dim.20), calls=%async_computation.10 | async-start | bytes 2097152 | tf_op jit(solution)/shard_map/all_to_all | solution.py:90
  327.5 47.0 %copy-start.2 = (f32[8,48,512]{2,1,0:T(8,128)}, f32[8,48,512]{2,1,0:T(8,128)S(1)}, u32[]{:S(2)}) copy-start(f32[8,48,512]{2,1,0:T(8,128)S(1)} %copy.170) | copy-start | bytes 2359300
Sparse Core Ops, SparseCore 0:
  11.0 82.5 all-gather.6
  116.6 43.0 all-gather.8
  162.7 67.9 all-gather.10

commit v3 on v1

--- a/solution.py
+++ b/solution.py
@@ -1,10 +1,129 @@
+import functools
 import jax
 import jax.numpy as jnp
 from jax import lax
+from jax.experimental import pallas as pl
+from jax.experimental.pallas import tpu as pltpu
 from jax.sharding import PartitionSpec as P
 
 ORDER = 98304
 HIGHEST = lax.Precision.HIGHEST
+
+
+PIVOTS = 8
+BLOCK = 128
+
+
+def small_dot(a, b, a_dim, b_dim):
+    return lax.dot_general(
+        a, b, (((a_dim,), (b_dim,)), ((), ())), precision=HIGHEST, preferred_element_type=jnp.float32
+    )
+
+
+def identity(n):
+    rows = lax.broadcasted_iota(jnp.int32, (n, n), 0)
+    return jnp.where(rows == lax.broadcasted_iota(jnp.int32, (n, n), 1), 1.0, 0.0)
+
+
+def invert_block(a_ref, b_ref):
+    n = a_ref.shape[0]
+    full = (PIVOTS, n)
+    for lo in range(0, n, PIVOTS):
+        block = a_ref[lo : lo + PIVOTS, :]
+        other = b_ref[lo : lo + PIVOTS, :]
+        d = {
+            (i, j): jnp.broadcast_to(block[i : i + 1, lo + j : lo + j + 1], full)
+            for i in range(PIVOTS)
+            for j in range(i + 1)
+        }
+        a = [jnp.broadcast_to(block[j : j + 1, :], full) for j in range(PIVOTS)]
+        b = [jnp.broadcast_to(other[j : j + 1, :], full) for j in range(PIVOTS)]
+        r = {}
+        for j in range(PIVOTS):
+            r[j] = lax.rsqrt(d[j, j])
+            for i in range(j + 1, PIVOTS):
+                d[i, j] = d[i, j] * r[j]
+            for i in range(j + 1, PIVOTS):
+                for k in range(i, PIVOTS):
+                    d[k, i] = d[k, i] - d[k, j] * d[i, j]
+            a[j] = a[j] * r[j]
+            b[j] = b[j] * r[j]
+            for i in range(j + 1, PIVOTS):
+                a[i] = a[i] - d[i, j] * a[j]
+                b[i] = b[i] - d[i, j] * b[j]
+        sub = lax.broadcasted_iota(jnp.int32, full, 0)
+        done = b[0]
+        for j in range(1, PIVOTS):
+            done = jnp.where(sub == j, b[j], done)
+        b_ref[lo : lo + PIVOTS, :] = done
+        for at in range(lo + PIVOTS, n, PIVOTS):
+            ah = a_ref[at : at + PIVOTS, :]
+            bh = b_ref[at : at + PIVOTS, :]
+            c = [jnp.broadcast_to(ah[:, lo + j : lo + j + 1], full) for j in range(PIVOTS)]
+            for j in range(PIVOTS):
+                c[j] = c[j] * r[j]
+                for i in range(j + 1, PIVOTS):
+                    c[i] = c[i] - d[i, j] * c[j]
+                ah = ah - c[j] * a[j]
+                bh = bh - c[j] * b[j]
+            a_ref[at : at + PIVOTS, :] = ah
+            b_ref[at : at + PIVOTS, :] = bh
+
+
+def block_pairs(n):
+    return [(i, j) for i in range(n // BLOCK) for j in range(i, n // BLOCK)]
+
+
+def inverse_kernel(scale, core_ref, mine_ref, other_ref, out_ref, a_ref, s_ref, t_ref):
+    n = out_ref.shape[0]
+    pairs = block_pairs(n)
+    half = len(pairs) // 2
+    core = core_ref[0]
+    for side in range(2):
+        for at, (i, j) in enumerate(pairs[side * half : (side + 1) * half]):
+            rows, cols = slice(i * BLOCK, (i + 1) * BLOCK), slice(j * BLOCK, (j + 1) * BLOCK)
+            part = jnp.where(core == side, mine_ref[at], other_ref[at])
+            a_ref[rows, cols] = part * scale
+    out_ref[...] = identity(n)
+
+    def one(b, _):
+        at = pl.multiple_of(b * BLOCK, BLOCK)
+        rows = pl.ds(at, BLOCK)
+        s_ref[...] = a_ref[rows, rows]
+        t_ref[...] = identity(BLOCK)
+        invert_block(s_ref, t_ref)
+        inv = t_ref[...]
+        below = lax.broadcasted_iota(jnp.int32, (BLOCK, n), 1) >= at + BLOCK
+        u = small_dot(inv, jnp.where(below, a_ref[rows, :], 0.0), 1, 0)
+        x = small_dot(inv, out_ref[rows, :], 1, 0)
+        out_ref[rows, :] = x
+
+        def rest(i, _):
+            later = pl.ds(pl.multiple_of(i * BLOCK, BLOCK), BLOCK)
+            ui = small_dot(inv, a_ref[rows, later], 1, 0)
+            a_ref[later, :] = a_ref[later, :] - small_dot(ui, u, 0, 0)
+            out_ref[later, :] = out_ref[later, :] - small_dot(ui, x, 0, 0)
+            return 0
+
+        lax.fori_loop(b + 1, n // BLOCK, rest, 0)
+        return 0
+
+    lax.fori_loop(0, n // BLOCK, one, 0)
+
+
+def inverse_factor(core, mine, other, n, scale):
+    return pl.pallas_call(
+        functools.partial(inverse_kernel, scale),
+        out_shape=jax.ShapeDtypeStruct((n, n), jnp.float32),
+        in_specs=[pl.BlockSpec(memory_space=pltpu.SMEM)] + [pl.BlockSpec(memory_space=pltpu.VMEM)] * 2,
+        out_specs=pl.BlockSpec(memory_space=pltpu.VMEM),
+        scratch_shapes=[
+            pltpu.VMEM((n, n), jnp.float32),
+            pltpu.VMEM((BLOCK, BLOCK), jnp.float32),
+            pltpu.VMEM((BLOCK, BLOCK), jnp.float32),
+        ],
+        compiler_params=pltpu.CompilerParams(vmem_limit_bytes=16 * 1024 * 1024),
+    )(jnp.full((1,), core, jnp.int32), mine, other)
 
 
 def exchange(blocks, axis):
@@ -40,14 +159,13 @@
     head_rows = share(heads[0], "row")
 
     mats = jnp.stack([block_inverse[0], factor_one[:, 0, :], block_inverse[1]])
-    mats = share(mats, "col")
-
-    def whole(panel_rows):
+    mats = lax.all_gather(mats, "col")
+
+    def gather_half(panel_rows):
         mine = lax.dynamic_index_in_dim(
             panel_rows.reshape((rows_n // 2, 2) + panel_rows.shape[1:]), core, 1, keepdims=False
         )
-        mine = share(mine, "col")
-        return mine, lax.ppermute(mine, "row", swap)
+        return lax.all_gather(mine, "col")
 
     def owned(mine):
         block = lax.dynamic_index_in_dim(mine, place, 1, keepdims=False)
@@ -62,34 +180,42 @@
             lax.dynamic_index_in_dim(parts, 1 - core, 1, keepdims=False),
         )
 
+    f_one = halves(factor_one)
+    mats, f_one = lax.optimization_barrier((mats, f_one))
     one_rows = share(product(head_rows, mats[:, 0]), "row")
+    one_mine = gather_half(one_rows)
+    one_other = lax.ppermute(one_mine, "row", swap)
     remain_head = heads[1] - product(one_rows, mats[:, 1])
     remain_rows = share(remain_head, "row")
     two_rows = share(product(remain_rows, mats[:, 2]), "row")
-
-    one_mine, one_other = whole(one_rows)
-    f_mine, f_other = halves(factor_one)
-    remain = vectors[:, 1:, :] - trailing(f_mine, one_mine) - trailing(f_other, one_other)
-
-    two_mine, two_other = whole(two_rows)
-    f_mine, f_other = halves(factor_two)
-    remaining = remain[:, 1:, :] - trailing(f_mine, two_mine) - trailing(f_other, two_other)
+    two_mine = gather_half(two_rows)
+    f_two = halves(factor_two)
+    remain = vectors[:, 1:, :] - trailing(f_one[0], one_mine) - trailing(f_one[1], one_other)
+    remain, two_mine = lax.optimization_barrier((remain, two_mine))
+    two_other = lax.ppermute(two_mine, "row", swap)
+    remaining = remain[:, 1:, :] - trailing(f_two[0], two_mine) - trailing(f_two[1], two_other)
 
     solved = jnp.concatenate([owned(one_mine)[:, None, :], owned(two_mine)[:, None, :], remaining], axis=1)
     weighted = solved * lumped_mass[:, :, None]
     gram = jnp.einsum("jtk,jtl->kl", weighted, solved, precision=HIGHEST, preferred_element_type=jnp.float32)
 
-    lanes = k_all // 4
-    gram = gram.reshape(cols_n, 4, own, 4, lanes).transpose(0, 1, 3, 2, 4)
-    gram = exchange(gram, "col").sum(axis=0)
-    gram = exchange(gram.reshape(rows_n, own, lanes), "row").sum(axis=0)
-    gram = share(share(gram, "row"), "col")
-    gram = gram.reshape(cols_n, 4, 4, own, lanes).transpose(0, 1, 3, 2, 4).reshape(k_all, k_all)
-
-    factor = jnp.linalg.cholesky(gram / ORDER)
-    flattened = solved.reshape(-1, k_all)
-    rotated = jax.scipy.linalg.solve_triangular(factor, flattened.T, lower=True).T
-    return (solved, rotated.reshape(solved.shape))
+    blocks = jnp.stack(
+        [gram[i * BLOCK : (i + 1) * BLOCK, j * BLOCK : (j + 1) * BLOCK] for i, j in block_pairs(k_all)]
+    )
+    blocks = blocks.reshape((2, -1, BLOCK))
+    there = lax.ppermute(lax.dynamic_index_in_dim(blocks, 1 - core, 0, keepdims=False), "row", swap)
+    part = lax.dynamic_index_in_dim(blocks, core, 0, keepdims=False) + there
+    part = exchange(part.reshape(cols_n, -1, BLOCK), "col").sum(axis=0)
+    step = 2
+    while step < rows_n:
+        part = part + lax.ppermute(part, "row", [(i, i ^ step) for i in range(rows_n)])
+        step *= 2
+    mine = share(part, "col").reshape(-1, BLOCK, BLOCK)
+    other = lax.ppermute(mine, "row", swap)
+
+    inverse = inverse_factor(core, mine, other, k_all, 1.0 / ORDER)
+    rotated = jnp.einsum("jtk,lk->jtl", solved, inverse, precision=HIGHEST, preferred_element_type=jnp.float32)
+    return (solved, rotated)
 
 
 def solution(mesh):

time: 545 us -> 337 us (0.62); the launches traced: 538 us -> 336 us
  other arithmetic: 120 us -> 4.36 us
  waiting for transfers between devices: 203 us -> 113 us
  blocking collectives: 99.2 us -> 67.3 us
  Pallas kernels: 0 us -> 26.8 us
  local copies, waits for them, and re-layouts: 43.5 us -> 30.4 us
  matrix products: 24.2 us -> 36.6 us
  between operations: 3.9 us -> 14.1 us
    all_to_all x9 -> x4, waiting for transfers between devices: 203 us -> 54.7 us  [exchange(): return lax.all_to_all(blocks, axis, 0, 0)]
    another operation x17 -> x0, other arithmetic: 118 us -> none  [the longest x14 78.8 us: body(): factor = jnp.linalg.cholesky(gram / ORDER)]
    all_gather x0 -> x3, waiting for transfers between devices: none -> 51 us  [the longest x2 47.3 us: gather_half(): return lax.all_gather(mine, 'col')]
    all_to_all x5, blocking collectives: 99.2 us -> 67.3 us  [exchange(): return lax.all_to_all(blocks, axis, 0, 0)]
    pallas_call x0 -> x1, Pallas kernels: none -> 26.8 us  [inverse_factor(): pl.pallas_call(functools.partial(inverse_kernel, scale), out_shape=jax.Sh...]
    all_to_all x9 -> x4, starting transfers between devices: 42.5 us -> 25.4 us  [exchange(): return lax.all_to_all(blocks, axis, 0, 0)]
    ppermute x2 -> x7, starting transfers between devices: 1.93 us -> 18.1 us  [the longest x3 9.28 us: body(): lax.ppermute(part, 'row', [(i, i ^ step) for i in range(rows_n)])]
    dot_general x4, matrix products: 13 us -> 25.2 us  [trailing(): jnp.einsum('rjtq,crkq->jtck', factor, panel, precision=HIGHEST, preferred...]
  transfers between devices with their start and end apart: 11 -> 14, of which waited for: 9 -> 11; matrix products, arithmetic and copies ran while one was open for 6% -> 17% of each run, Pallas kernels for 0% -> 0%
where the time goes in v3:
time: 337 us; the launch traced here: 336 us
  waiting for transfers between devices  113 us (34%)
  blocking collectives  67.3 us (20%)
  starting transfers between devices  43.6 us (13%)
  matrix products  36.6 us (11%)
  local copies, waits for them, and re-layouts  30.4 us (9%)
  Pallas kernels  26.8 us (8%)
  between operations  14.1 us (4%)
  other arithmetic  4.36 us (1%)
    all_to_all x5, blocking collectives, exchange(): return lax.all_to_all(blocks, axis, 0, 0)  67.3 us
    all_to_all x4, waiting for transfers between devices, exchange(): return lax.all_to_all(blocks, axis, 0, 0)  54.7 us
    all_gather x2, waiting for transfers between devices, gather_half(): return lax.all_gather(mine, 'col')  47.3 us
    pallas_call x1, Pallas kernels, inverse_factor(): pl.pallas_call(functools.partial(inverse_kernel, scale), out_shape=jax.Sh...  26.8 us
    all_to_all x4, starting transfers between devices, exchange(): return lax.all_to_all(blocks, axis, 0, 0)  25.4 us
    dot_general x4, matrix products, trailing(): jnp.einsum('rjtq,crkq->jtck', factor, panel, precision=HIGHEST, preferred...  25.2 us
    ppermute x3, starting transfers between devices, body(): lax.ppermute(part, 'row', [(i, i ^ step) for i in range(rows_n)])  9.28 us
    dot_general x3, matrix products, product(): jnp.einsum('rkq,riq->ki', rows, tiles, precision=HIGHEST, preferred_eleme...  7.17 us
  transfers between devices with their start and end apart: 14, of which 11 were waited for; matrix products, arithmetic and copies ran while one was open for 17% of the time, Pallas kernels for 0%

profile of v3, /device:TPU:1, one launch (start us, length us, event | category | flops | bytes accessed | tf_op | source)
XLA Modules:
  0.0 335.7 jit_solution(3545412051732288296)
XLA Ops:
  11.5 7.6 %all-to-all-start.1 = ((f32[16,1,512]{2,1,0:T(1,128)}), f32[16,1,512]{2,1,0:T(1,128)S(1)}, u32[]{:S(2)}, u32[]{:S(2)}) async-start(f32[16,1,512]{2,1,0:T(1,128)} %reshape.88), calls=%async_computation.1 | async-start | bytes 65536 | tf_op jit(solution)/shard_map/all_to_all | solution.py:130
  19.1 3.7 %copy.73 = f32[16,8,47,128]{3,1,2,0:T(8,128)} copy(f32[16,8,47,128]{3,1,0,2:T(8,128)} %bitcast.178) | data formatting | bytes 6160384 | tf_op jit(solution)/shard_map/reshape | solution.py:176
  25.5 3.9 %all-to-all-start = ((f32[16,8,47,128]{3,1,2,0:T(8,128)}), f32[16,8,47,128]{3,1,2,0:T(8,128)S(1)}, u32[]{:S(2)}, u32[]{:S(2)}) async-start(f32[16,8,47,128]{3,1,2,0:T(8,128)} %copy.73), calls=%async_computation | async-start | bytes 6160384 | tf_op jit(solution)/shard_map/all_to_all | solution.py:130
  30.9 46.5 %all-to-all-done = f32[16,8,47,128]{3,1,2,0:T(8,128)S(1)} async-done(((f32[16,8,47,128]{3,1,2,0:T(8,128)}), f32[16,8,47,128]{3,1,2,0:T(8,128)S(1)}, u32[]{:S(2)}, u32[]{:S(2)}) %all-to-all-start) | async-done | bytes 3080224 | tf_op jit(solution)/shard_map/all_to_all | solution.py:130
  78.1 9.2 %all-to-all-start.2 = ((f32[16,32,128]{2,1,0:T(8,128)}), f32[16,32,128]{2,1,0:T(8,128)S(1)}, u32[]{:S(2)}, u32[]{:S(2)}) async-start(f32[16,32,128]{2,1,0:T(8,128)} %broadcast_in_dim.15), calls=%async_computation.2 | async-start | bytes 524288 | tf_op jit(solution)/shard_map/all_to_all | solution.py:130
  90.0 3.6 %all-gather.7.cloned.1.call-done = f32[48,128,128]{2,1,0:T(8,128)} async-done(((f32[3,128,128]{2,1,0:T(8,128)}), f32[48,128,128]{2,1,0:T(8,128)}) %all-gather.7.cloned.1.call-update) | async-done | bytes 3145744 | tf_op jit(solution)/shard_map/all_gather | solution.py:162
  93.6 5.5 %all-to-all-done.2 = f32[16,32,128]{2,1,0:T(8,128)S(1)} async-done(((f32[16,32,128]{2,1,0:T(8,128)}), f32[16,32,128]{2,1,0:T(8,128)S(1)}, u32[]{:S(2)}, u32[]{:S(2)}) %all-to-all-start.2) | async-done | bytes 262176 | tf_op jit(solution)/shard_map/all_to_all | solution.py:130
  101.4 14.4 %all_to_all.45 = f32[16,32,128]{2,1,0:T(8,128)S(1)} all-to-all(f32[16,32,128]{2,1,0:T(8,128)S(1)} %broadcast_in_dim.16), channel_id=1, replica_groups=mesh['row'=16,'col'=16] {'row'}, dimensions={0} | all-to-all | bytes 524288 | tf_op jit(solution)/shard_map/all_to_all | solution.py:130
  119.2 14.4 %all_to_all.46 = f32[16,32,128]{2,1,0:T(8,128)S(1)} all-to-all(f32[16,32,128]{2,1,0:T(8,128)S(1)} %broadcast_in_dim.17), channel_id=1, replica_groups=mesh['row'=16,'col'=16] {'row'}, dimensions={0} | all-to-all | bytes 524288 | tf_op jit(solution)/shard_map/all_to_all | solution.py:130
  136.0 14.4 %all_to_all.47 = f32[16,32,128]{2,1,0:T(8,128)S(1)} all-to-all(f32[16,32,128]{2,1,0:T(8,128)S(1)} %broadcast_in_dim.18), channel_id=1, replica_groups=mesh['row'=16,'col'=16] {'row'}, dimensions={0} | all-to-all | bytes 524288 | tf_op jit(solution)/shard_map/all_to_all | solution.py:130
  151.0 8.7 %all-gather.9.cloned.1.call-done = f32[128,1,32,128]{3,2,1,0:T(8,128)} async-done(((f32[8,1,32,128]{3,2,1,0:T(8,128)}), f32[128,1,32,128]{3,2,1,0:T(8,128)}) %all-gather.9.cloned.1.call-update) | async-done | bytes 2097168 | tf_op jit(solution)/shard_map/all_gather | solution.py:168
  163.0 4.7 %all-to-all-start.6 = ((f32[16,8,46,128]{3,1,2,0:T(8,128)}), f32[16,8,46,128]{3,1,2,0:T(8,128)S(1)}, u32[]{:S(2)}, u32[]{:S(2)}) async-start(f32[16,8,46,128]{3,1,2,0:T(8,128)} %copy.89), calls=%async_computation.6 | async-start | bytes 6029312 | tf_op jit(solution)/shard_map/all_to_all | solution.py:130
  167.7 9.7 %fusion.6 = f32[8,47,16,32,1]{1,3,4,2,0:T(8,128)} fusion(f32[16,8,32,128,1]{3,2,1,0,4:T(8,128)} %bitcast.198, f32[8,8,47,128]{3,2,0,1:T(8,128)} %get-tuple-element.8), kind=kOutput, calls=%fused_computation.6 | convolution fusion | flops 2365587456 | bytes 4407296 | tf_op jit(solution)/shard_map/rjtq,crkq->jtck/dot_general | solution.py:143
  177.3 3.1 copy.82
  180.4 9.6 %fusion.2 = f32[8,47,16,32,1]{1,3,4,2,0:T(8,128)} fusion(f32[16,8,32,128]{3,2,1,0:T(8,128)} %collective-permute-done, f32[8,8,47,128]{3,2,0,1:T(8,128)} %get-tuple-element.9), kind=kOutput, calls=%fused_computation.2 | convolution fusion | flops 2365587456 | bytes 4407296 | tf_op jit(solution)/shard_map/rjtq,crkq->jtck/dot_general | solution.py:143
  190.1 3.1 copy.83
  195.9 38.7 %all-gather.11.cloned.1.call-done = f32[128,1,32,128]{3,2,1,0:T(8,128)} async-done(((f32[8,1,32,128]{3,2,1,0:T(8,128)}), f32[128,1,32,128]{3,2,1,0:T(8,128)}) %all-gather.11.cloned.1.call-update) | async-done | bytes 2097168 | tf_op jit(solution)/shard_map/all_gather | solution.py:168
  240.3 3.4 %copy.91 = f32[16,32,128,8]{2,3,1,0:T(8,128)S(1)} copy(f32[16,32,128,8]{2,1,3,0:T(8,128)} %bitcast.185) | data formatting | bytes 4194304 | tf_op jit(solution)/shard_map/rjtq,crkq->jtck/dot_general | solution.py:143
  243.7 3.1 fusion.21
  255.7 13.5 %all_to_all.48 = f32[16,40,128]{2,1,0:T(8,128)S(1)} all-to-all(f32[16,40,128]{2,1,0:T(8,128)S(1)} %bitcast.189), channel_id=1, replica_groups=mesh['row'=16,'col'=16] {'col'}, dimensions={0} | all-to-all | bytes 655360 | tf_op jit(solution)/shard_map/all_to_all | solution.py:130
  275.5 5.7 %collective-permute-start.5 = (f32[40,128]{1,0:T(8,128)S(1)}, f32[40,128]{1,0:T(8,128)S(1)}, u32[]{:S(2)}, u32[]{:S(2)}) collective-permute-start(f32[40,128]{1,0:T(8,128)S(1)} %add.58), channel_id=1, source_target_pairs={{0,128},{16,144},{32,160},{48,176},{64,192},{80,208},{96,224},{112... | collective-permute-start | bytes 61448 | tf_op jit(solution)/shard_map/ppermute | solution.py:211
  282.5 10.5 %all_to_all.49 = f32[16,40,128]{2,1,0:T(8,128)S(1)} all-to-all(f32[16,40,128]{2,1,0:T(8,128)S(1)} %broadcast_in_dim.20), channel_id=1, replica_groups=mesh['row'=16,'col'=16] {'col'}, dimensions={0} | all-to-all | bytes 655360 | tf_op jit(solution)/shard_map/all_to_all | solution.py:130
  293.1 5.7 %collective-permute-start.6 = (f32[5,128,128]{2,1,0:T(8,128)S(1)}, f32[5,128,128]{2,1,0:T(8,128)S(1)}, u32[]{:S(2)}, u32[]{:S(2)}) collective-permute-start(f32[5,128,128]{2,1,0:T(8,128)S(1)} %bitcast.172), channel_id=1, source_target_pairs={{0,16},{16,0},{32,48},{48,32},{64,80},{80,64},{96,112},{112,96},{1... | collective-permute-start | bytes 983048 | tf_op jit(solution)/shard_map/ppermute | solution.py:214
  300.0 26.8 %shard_map.68 = f32[512,512]{1,0:T(8,128)S(1)} custom-call(s32[1]{0:T(128)} %bitcast.55.core_ref, f32[5,128,128]{2,1,0:T(8,128)S(1)} %bitcast.173, f32[5,128,128]{2,1,0:T(8,128)S(1)} %collective-permute-done.6.other_ref), custom_call_target="tpu_custom_call" | custom-call | tf_op jit(solution)/shard_map/pallas_call | solution.py:115
  (86 shorter events, 52.1 us)
Async XLA Ops:
  7.2 86.5 %all-gather.7.cloned.1.call-start = ((), (), s32[]{:S(2)}) async-start(), calls=%async_computation.9 | async-start | bytes 3342336 | tf_op jit(solution)/shard_map/all_gather | solution.py:162
  11.5 14.1 %all-to-all-start.1 = ((f32[16,1,512]{2,1,0:T(1,128)}), f32[16,1,512]{2,1,0:T(1,128)S(1)}, u32[]{:S(2)}, u32[]{:S(2)}) async-start(f32[16,1,512]{2,1,0:T(1,128)} %reshape.88), calls=%async_computation.1 | async-start | bytes 65536 | tf_op jit(solution)/shard_map/all_to_all | solution.py:130
  25.5 51.9 %all-to-all-start = ((f32[16,8,47,128]{3,1,2,0:T(8,128)}), f32[16,8,47,128]{3,1,2,0:T(8,128)S(1)}, u32[]{:S(2)}, u32[]{:S(2)}) async-start(f32[16,8,47,128]{3,1,2,0:T(8,128)} %copy.73), calls=%async_computation | async-start | bytes 6160384 | tf_op jit(solution)/shard_map/all_to_all | solution.py:130
  78.1 21.0 %all-to-all-start.2 = ((f32[16,32,128]{2,1,0:T(8,128)}), f32[16,32,128]{2,1,0:T(8,128)S(1)}, u32[]{:S(2)}, u32[]{:S(2)}) async-start(f32[16,32,128]{2,1,0:T(8,128)} %broadcast_in_dim.15), calls=%async_computation.2 | async-start | bytes 524288 | tf_op jit(solution)/shard_map/all_to_all | solution.py:130
  87.4 72.3 %all-gather.9.cloned.1.call-start = ((), (), s32[]{:S(2)}) async-start(), calls=%async_computation.10 | async-start | bytes 2228224 | tf_op jit(solution)/shard_map/all_gather | solution.py:168
  116.5 118.1 %all-gather.11.cloned.1.call-start = ((), (), s32[]{:S(2)}) async-start(), calls=%async_computation.11 | async-start | bytes 2228224 | tf_op jit(solution)/shard_map/all_gather | solution.py:168
  116.6 44.6 %copy-start.4 = (f32[128,46,128]{2,0,1:T(8,128)S(1)}, f32[128,46,128]{2,0,1:T(8,128)}, u32[]{:S(2)}) copy-start(f32[128,46,128]{2,0,1:T(8,128)} %param.7) | copy-start | bytes 9043972
  159.7 20.7 %collective-permute-start = (f32[16,8,32,128]{3,2,1,0:T(8,128)}, f32[16,8,32,128]{3,2,1,0:T(8,128)}, u32[]{:S(2)}, u32[]{:S(2)}) collective-permute-start(f32[16,8,32,128]{3,2,1,0:T(8,128)} %bitcast.197), channel_id=1, source_target_pairs={{0,16},{16,0},{32,48},{48,32},{64,80},{80,64},{96,112},{112,96},{1... | collective-permute-start | bytes 6291464 | tf_op jit(solution)/shard_map/ppermute | solution.py:187
  163.0 73.1 %all-to-all-start.6 = ((f32[16,8,46,128]{3,1,2,0:T(8,128)}), f32[16,8,46,128]{3,1,2,0:T(8,128)S(1)}, u32[]{:S(2)}, u32[]{:S(2)}) async-start(f32[16,8,46,128]{3,1,2,0:T(8,128)} %copy.89), calls=%async_computation.6 | async-start | bytes 6029312 | tf_op jit(solution)/shard_map/all_to_all | solution.py:130
  234.6 12.2 %collective-permute-start.1 = (f32[16,8,32,128]{3,2,1,0:T(8,128)}, f32[16,8,32,128]{3,2,1,0:T(8,128)}, u32[]{:S(2)}, u32[]{:S(2)}) collective-permute-start(f32[16,8,32,128]{3,2,1,0:T(8,128)} %bitcast.183), channel_id=1, source_target_pairs={{0,16},{16,0},{32,48},{48,32},{64,80},{80,64},{96,112},{112,96},{1... | collective-permute-start | bytes 6291464 | tf_op jit(solution)/shard_map/ppermute | solution.py:195
  240.3 3.4 %copy-start.1 = (f32[8,1,8,46,128]{4,2,3,1,0:T(8,128)S(1)}, f32[8,1,8,46,128]{4,2,3,1,0:T(8,128)}, u32[]{:S(2)}) copy-start(f32[8,1,8,46,128]{4,2,3,1,0:T(8,128)} %get-tuple-element.15) | copy-start | bytes 4521988
  240.3 3.4 %copy-start.2 = (f32[8,47,512]{2,1,0:T(8,128)S(1)}, f32[8,47,512]{2,1,0:T(8,128)}, u32[]{:S(2)}) copy-start(f32[8,47,512]{2,1,0:T(8,128)} %subtract_subtract_fusion) | copy-start | bytes 2310148
  246.8 2.0 copy-start
  248.8 3.0 copy-start.5
  251.8 75.1 %copy-start.3 = (f32[8,48,512]{2,1,0:T(8,128)}, f32[8,48,512]{2,1,0:T(8,128)S(1)}, u32[]{:S(2)}) copy-start(f32[8,48,512]{2,1,0:T(8,128)S(1)} %pad_maximum_fusion) | copy-start | bytes 2359300
  254.0 1.7 collective-permute-start.2
  269.3 2.7 collective-permute-start.3
  272.0 3.5 %collective-permute-start.4 = (f32[40,128]{1,0:T(8,128)S(1)}, f32[40,128]{1,0:T(8,128)S(1)}, u32[]{:S(2)}, u32[]{:S(2)}) collective-permute-start(f32[40,128]{1,0:T(8,128)S(1)} %add.57), channel_id=1, source_target_pairs={{0,64},{16,80},{32,96},{48,112},{64,0},{80,16},{96,32},{112,48},{1... | collective-permute-start | bytes 61448 | tf_op jit(solution)/shard_map/ppermute | solution.py:211
  275.5 7.0 %collective-permute-start.5 = (f32[40,128]{1,0:T(8,128)S(1)}, f32[40,128]{1,0:T(8,128)S(1)}, u32[]{:S(2)}, u32[]{:S(2)}) collective-permute-start(f32[40,128]{1,0:T(8,128)S(1)} %add.58), channel_id=1, source_target_pairs={{0,128},{16,144},{32,160},{48,176},{64,192},{80,208},{96,224},{112... | collective-permute-start | bytes 61448 | tf_op jit(solution)/shard_map/ppermute | solution.py:211
  293.1 7.0 %collective-permute-start.6 = (f32[5,128,128]{2,1,0:T(8,128)S(1)}, f32[5,128,128]{2,1,0:T(8,128)S(1)}, u32[]{:S(2)}, u32[]{:S(2)}) collective-permute-start(f32[5,128,128]{2,1,0:T(8,128)S(1)} %bitcast.172), channel_id=1, source_target_pairs={{0,16},{16,0},{32,48},{48,32},{64,80},{80,64},{96,112},{112,96},{1... | collective-permute-start | bytes 983048 | tf_op jit(solution)/shard_map/ppermute | solution.py:214
Sparse Core Ops, SparseCore 0:
  11.0 82.5 all-gather.6
  116.6 43.0 all-gather.8
  162.1 72.3 all-gather.10

commit v4 on v3

--- a/solution.py
+++ b/solution.py
@@ -126,6 +126,115 @@
     )(jnp.full((1,), core, jnp.int32), mine, other)
 
 
+def pack_kernel(one_ref, two_ref, out_ref):
+    for which, ref in enumerate((one_ref, two_ref)):
+        lead = which + 1
+        out_ref[0, which, :lead] = jnp.zeros((lead,) + ref.shape[1:], jnp.float32)
+        out_ref[0, which, lead:] = ref[...]
+
+
+def pack(one, two, own):
+    rows, steps, tile = one.shape
+    blocks = rows // own
+    specs = [pl.BlockSpec((f.shape[1], own, tile), lambda c: (0, c, 0)) for f in (one, two)]
+    shape = (blocks, 2, steps + 1, own, tile)
+    return pl.pallas_call(
+        pack_kernel,
+        out_shape=jax.ShapeDtypeStruct(shape, jnp.float32),
+        grid=(blocks,),
+        in_specs=specs,
+        out_specs=pl.BlockSpec((1,) + shape[1:], lambda c: (c, 0, 0, 0, 0)),
+        compiler_params=pltpu.CompilerParams(vmem_limit_bytes=56 * 1024 * 1024),
+        cost_estimate=pl.CostEstimate(flops=0, bytes_accessed=16 * one.size, transcendentals=0),
+    )(one.transpose(1, 0, 2), two.transpose(1, 0, 2))
+
+
+def pair(ref, first, second, rows):
+    return jnp.concatenate([ref[first].reshape(rows, BLOCK), ref[second].reshape(rows, BLOCK)], axis=1)
+
+
+def update_kernel(parity_ref, start_ref, factor_ref, panel_ref, after_ref, out_ref):
+    @pl.when(pl.program_id(0) == 0)
+    def _():
+        out_ref[...] = start_ref[...]
+
+    rows, cols = out_ref.shape
+    f = pair(factor_ref, (0, 0, 0), (1, 0, 0), rows)
+    p = pair(panel_ref, (slice(None), 0, 0), (slice(None), 1, 0), cols)
+    out_ref[...] -= small_dot(f, p, 1, 1)
+
+
+def update(start, factors, panel, parity, which, after):
+    chips = factors.shape[0]
+    last = panel.shape[2] - 1
+    return pl.pallas_call(
+        update_kernel,
+        out_shape=jax.ShapeDtypeStruct(start.shape, jnp.float32),
+        grid_spec=pltpu.PrefetchScalarGridSpec(
+            num_scalar_prefetch=1,
+            grid=(chips // 2,),
+            in_specs=[
+                pl.BlockSpec(start.shape, lambda s, p: (0, 0)),
+                pl.BlockSpec((2, 1, 1) + factors.shape[3:], lambda s, p: (s, p[0], which, 0, 0, 0)),
+                pl.BlockSpec((panel.shape[0], 2, 1) + panel.shape[3:], lambda s, p: (0, s, p[0] * last, 0, 0)),
+                pl.BlockSpec(memory_space=pl.ANY),
+            ],
+            out_specs=pl.BlockSpec(start.shape, lambda s, p: (0, 0)),
+        ),
+        compiler_params=pltpu.CompilerParams(vmem_limit_bytes=56 * 1024 * 1024),
+        cost_estimate=pl.CostEstimate(
+            flops=12 * start.size * chips * BLOCK, bytes_accessed=8 * start.size + 8 * start.size, transcendentals=0
+        ),
+    )(jnp.full((1,), parity, jnp.int32), start, factors, panel, after)
+
+
+def finish_kernel(at_ref, update_ref, one_ref, two_ref, mass_ref, solved_ref, blocks_ref):
+    rounds, own, k_all = solved_ref.shape
+    lanes = lax.broadcasted_iota(jnp.int32, (own, BLOCK), 1)
+    rows = lax.broadcasted_iota(jnp.int32, (own, BLOCK), 0)
+    take = jnp.where(lanes == rows + at_ref[1] * own, 1.0, 0.0)
+    solved_ref[0] = small_dot(take, one_ref[:, 0].reshape(k_all, BLOCK), 1, 1)
+    solved_ref[1] = small_dot(take, two_ref[:, 0].reshape(k_all, BLOCK), 1, 1)
+    solved_ref[2:] = update_ref[2 * own :, :].reshape(rounds - 2, own, k_all)
+    all_rows = solved_ref[...].reshape(own * rounds, k_all)
+    weighted = all_rows * mass_ref[...]
+    at = 0
+    for i in range(k_all // BLOCK):
+        got = small_dot(weighted[:, i * BLOCK : (i + 1) * BLOCK], all_rows[:, i * BLOCK :], 0, 0)
+        for j in range(k_all // BLOCK - i):
+            blocks_ref[at] = got[:, j * BLOCK : (j + 1) * BLOCK]
+            at += 1
+
+
+def finish(updated, one, two, mass, row, col, shape):
+    rounds, own, k_all = shape
+    count = len(block_pairs(k_all))
+    panel = (one.shape[0], 1) + one.shape[2:]
+    return pl.pallas_call(
+        finish_kernel,
+        out_shape=(
+            jax.ShapeDtypeStruct(shape, jnp.float32),
+            jax.ShapeDtypeStruct((count, BLOCK, BLOCK), jnp.float32),
+        ),
+        grid_spec=pltpu.PrefetchScalarGridSpec(
+            num_scalar_prefetch=1,
+            grid=(1,),
+            in_specs=[
+                pl.BlockSpec(updated.shape, lambda s, at: (0, 0)),
+                pl.BlockSpec(panel, lambda s, at: (0, at[0], 0, 0)),
+                pl.BlockSpec(panel, lambda s, at: (0, at[0] // 2, 0, 0)),
+                pl.BlockSpec((own * rounds, 1), lambda s, at: (0, 0)),
+            ],
+            out_specs=(
+                pl.BlockSpec(shape, lambda s, at: (0, 0, 0)),
+                pl.BlockSpec((count, BLOCK, BLOCK), lambda s, at: (0, 0, 0)),
+            ),
+        ),
+        compiler_params=pltpu.CompilerParams(vmem_limit_bytes=24 * 1024 * 1024),
+        cost_estimate=pl.CostEstimate(flops=8 * updated.size * k_all, bytes_accessed=12 * updated.size, transcendentals=0),
+    )(jnp.stack([row, col]).astype(jnp.int32), updated, one, two, mass.T.reshape(-1, 1))
+
+
 def exchange(blocks, axis):
     return lax.all_to_all(blocks, axis, 0, 0)
 
@@ -139,69 +248,51 @@
     return jnp.einsum("rkq,riq->ki", rows, tiles, precision=HIGHEST, preferred_element_type=jnp.float32)
 
 
-def trailing(factor, panel):
-    out = jnp.einsum("rjtq,crkq->jtck", factor, panel, precision=HIGHEST, preferred_element_type=jnp.float32)
-    return out.reshape(out.shape[:2] + (-1,))
-
-
 def body(vectors, factor_one, factor_two, block_inverse, lumped_mass):
     rows_n, cols_n = lax.axis_size("row"), lax.axis_size("col")
     row, col = lax.axis_index("row"), lax.axis_index("col")
-    core, place = row % 2, row // 2
+    core = row % 2
     own, rounds, k_all = vectors.shape
     tile = own * cols_n
     k_part = k_all // cols_n
     swap = [(i, i ^ 1) for i in range(rows_n)]
 
+    mats = jnp.stack([block_inverse[0], factor_one[:, 0, :], block_inverse[1]])
     heads = vectors[:, :2, :].reshape(own, 2, cols_n, k_part).transpose(2, 1, 0, 3)
+    mats, heads, factor_one = lax.optimization_barrier((mats, heads, factor_one))
     heads = exchange(heads, "col")
     heads = heads.transpose(1, 3, 0, 2).reshape(2, k_part, tile)
     head_rows = share(heads[0], "row")
 
-    mats = jnp.stack([block_inverse[0], factor_one[:, 0, :], block_inverse[1]])
     mats = lax.all_gather(mats, "col")
 
-    def gather_half(panel_rows):
-        mine = lax.dynamic_index_in_dim(
+    def half(panel_rows):
+        return lax.dynamic_index_in_dim(
             panel_rows.reshape((rows_n // 2, 2) + panel_rows.shape[1:]), core, 1, keepdims=False
         )
-        return lax.all_gather(mine, "col")
-
-    def owned(mine):
-        block = lax.dynamic_index_in_dim(mine, place, 1, keepdims=False)
-        block = lax.dynamic_slice_in_dim(block, col * own, own, 2)
-        return block.transpose(2, 0, 1).reshape(own, k_all)
-
-    def halves(factor):
-        parts = exchange(factor.reshape((cols_n, own) + factor.shape[1:]), "col")
-        parts = parts.reshape((rows_n // 2, 2) + parts.shape[1:])
-        return (
-            lax.dynamic_index_in_dim(parts, core, 1, keepdims=False),
-            lax.dynamic_index_in_dim(parts, 1 - core, 1, keepdims=False),
-        )
-
-    f_one = halves(factor_one)
-    mats, f_one = lax.optimization_barrier((mats, f_one))
+
+    factors = pack(factor_one, factor_two, own)
+    factors = exchange(factors, "col")
+    mats, factors = lax.optimization_barrier((mats, factors))
+    factors = factors.reshape((rows_n // 2, 2) + factors.shape[1:])
+
     one_rows = share(product(head_rows, mats[:, 0]), "row")
-    one_mine = gather_half(one_rows)
-    one_other = lax.ppermute(one_mine, "row", swap)
+    one_whole = lax.all_gather(one_rows, "col")
     remain_head = heads[1] - product(one_rows, mats[:, 1])
     remain_rows = share(remain_head, "row")
     two_rows = share(product(remain_rows, mats[:, 2]), "row")
-    two_mine = gather_half(two_rows)
-    f_two = halves(factor_two)
-    remain = vectors[:, 1:, :] - trailing(f_one[0], one_mine) - trailing(f_one[1], one_other)
-    remain, two_mine = lax.optimization_barrier((remain, two_mine))
+    two_mine = share(half(two_rows), "col")
+
+    by_parity = one_whole.reshape((cols_n, rows_n // 2, 2) + one_whole.shape[2:])
+    done = vectors.transpose(1, 0, 2).reshape(-1, k_all)
+    for parity in (0, 1):
+        done = update(done, factors, by_parity, parity, 0, two_rows)
     two_other = lax.ppermute(two_mine, "row", swap)
-    remaining = remain[:, 1:, :] - trailing(f_two[0], two_mine) - trailing(f_two[1], two_other)
-
-    solved = jnp.concatenate([owned(one_mine)[:, None, :], owned(two_mine)[:, None, :], remaining], axis=1)
-    weighted = solved * lumped_mass[:, :, None]
-    gram = jnp.einsum("jtk,jtl->kl", weighted, solved, precision=HIGHEST, preferred_element_type=jnp.float32)
-
-    blocks = jnp.stack(
-        [gram[i * BLOCK : (i + 1) * BLOCK, j * BLOCK : (j + 1) * BLOCK] for i, j in block_pairs(k_all)]
-    )
+    done = update(done, factors, two_mine[:, :, None], core, 1, two_rows)
+    done = update(done, factors, two_other[:, :, None], 1 - core, 1, two_rows)
+    solved, blocks = finish(done, one_whole, two_mine, lumped_mass, row, col, (rounds, own, k_all))
+    solved = solved.transpose(1, 0, 2)
+
     blocks = blocks.reshape((2, -1, BLOCK))
     there = lax.ppermute(lax.dynamic_index_in_dim(blocks, 1 - core, 0, keepdims=False), "row", swap)
     part = lax.dynamic_index_in_dim(blocks, core, 0, keepdims=False) + there

time: 337 us -> 360 us (1.068)
  Pallas kernels: 26.8 us -> 65.3 us
  matrix products: 36.6 us -> 9.49 us
  blocking collectives: 67.3 us -> 91.4 us
  local copies, waits for them, and re-layouts: 30.4 us -> 10.4 us
  waiting for transfers between devices: 113 us -> 122 us
    all_to_all x4, waiting for transfers between devices: 54.7 us -> 109 us  [exchange(): return lax.all_to_all(blocks, axis, 0, 0)]
    all_gather x2 -> x1, waiting for transfers between devices: 47.3 us -> 0.01 us  [body(): one_whole = lax.all_gather(one_rows, 'col')]
    pallas_call x0 -> x6, Pallas kernels: none -> 38.4 us  [the longest x4 24.7 us: update(): pl.pallas_call(update_kernel, out_shape=jax.ShapeDtypeStruct(start.shape,...]
    dot_general x5 -> x0, matrix products: 27.1 us -> none  [the longest x4 25.2 us: trailing(): jnp.einsum('rjtq,crkq->jtck', factor, panel, precision=HIGHEST, preferred...]
    all_to_all x5, blocking collectives: 67.3 us -> 91.4 us  [exchange(): return lax.all_to_all(blocks, axis, 0, 0)]
    reshape x4 -> x1, local copies, waits for them, and re-layouts: 11.7 us -> 0.11 us  [finish(): mass.T.reshape(-1, 1)]
    dynamic_slice x6 -> x0, local copies, waits for them, and re-layouts: 5.51 us -> none  [the longest x2 2.16 us: owned(): block = lax.dynamic_slice_in_dim(block, col * own, own, 2)]
    dot_general x2 -> x0, local copies, waits for them, and re-layouts: 5.29 us -> none  [trailing(): jnp.einsum('rjtq,crkq->jtck', factor, panel, precision=HIGHEST, preferred...]
  transfers between devices with their start and end apart: 14 -> 12, of which waited for: 11 -> 9; matrix products, arithmetic and copies ran while one was open for 17% -> 3% of each run, Pallas kernels for 0% -> 8%
where the time goes in v4:
time: 360 us; the launch traced here: 359 us
  waiting for transfers between devices  122 us (34%)
  blocking collectives  91.4 us (25%)
  Pallas kernels  65.3 us (18%)
  starting transfers between devices  44.6 us (12%)
  between operations  14.3 us (4%)
  local copies, waits for them, and re-layouts  10.4 us (3%)
  matrix products  9.49 us (3%)
    all_to_all x4, waiting for transfers between devices, exchange(): return lax.all_to_all(blocks, axis, 0, 0)  109 us
    all_to_all x5, blocking collectives, exchange(): return lax.all_to_all(blocks, axis, 0, 0)  91.4 us
    all_to_all x4, starting transfers between devices, exchange(): return lax.all_to_all(blocks, axis, 0, 0)  28.7 us
    pallas_call x1, Pallas kernels, inverse_factor(): pl.pallas_call(functools.partial(inverse_kernel, scale), out_shape=jax.Sh...  26.8 us
    pallas_call x4, Pallas kernels, update(): pl.pallas_call(update_kernel, out_shape=jax.ShapeDtypeStruct(start.shape,...  24.7 us
    pallas_call x1, Pallas kernels, pack(): pl.pallas_call(pack_kernel, out_shape=jax.ShapeDtypeStruct(shape, jnp.flo...  11.3 us
    ppermute x3, starting transfers between devices, body(): lax.ppermute(part, 'row', [(i, i ^ step) for i in range(rows_n)])  8.52 us
  transfers between devices with their start and end apart: 12, of which 9 were waited for; matrix products, arithmetic and copies ran while one was open for 3% of the time, Pallas kernels for 8%

profile of v4, /device:TPU:1, one launch (start us, length us, event | category | flops | bytes accessed | tf_op | source)
XLA Modules:
  0.0 358.9 jit_solution(1087734845767265975)
XLA Ops:
  11.4 7.6 %all-to-all-start.1 = ((f32[16,1,512]{2,1,0:T(1,128)}), f32[16,1,512]{2,1,0:T(1,128)S(1)}, u32[]{:S(2)}, u32[]{:S(2)}) async-start(f32[16,1,512]{2,1,0:T(1,128)} %reshape.59), calls=%async_computation.1 | async-start | bytes 65536 | tf_op jit(solution)/shard_map/all_to_all | solution.py:239
  19.0 11.3 %shard_map.68 = f32[16,2,48,8,128]{4,3,2,1,0:T(8,128)} custom-call(f32[47,128,128]{2,1,0:T(8,128)} %bitcast.76, f32[46,128,128]{2,1,0:T(8,128)} %bitcast.81), custom_call_target="tpu_custom_call" | custom-call | bytes 12320768 | tf_op jit(solution)/shard_map/pallas_call | solution.py:141
  30.3 6.7 %all-to-all-start = ((f32[16,2,48,8,128]{4,3,2,1,0:T(8,128)}), f32[16,2,48,8,128]{4,3,2,1,0:T(8,128)}, u32[]{:S(2)}, u32[]{:S(2)}) async-start(f32[16,2,48,8,128]{4,3,2,1,0:T(8,128)} %shard_map.68), calls=%async_computation | async-start | bytes 12582912 | tf_op jit(solution)/shard_map/all_to_all | solution.py:239
  39.1 91.9 %all-to-all-done = f32[16,2,48,8,128]{4,3,2,1,0:T(8,128)} async-done(((f32[16,2,48,8,128]{4,3,2,1,0:T(8,128)}), f32[16,2,48,8,128]{4,3,2,1,0:T(8,128)}, u32[]{:S(2)}, u32[]{:S(2)}) %all-to-all-start) | async-done | bytes 6291488 | tf_op jit(solution)/shard_map/all_to_all | solution.py:239
  131.8 11.0 %all-to-all-start.2 = ((f32[16,32,128]{2,1,0:T(8,128)}), f32[16,32,128]{2,1,0:T(8,128)S(1)}, u32[]{:S(2)}, u32[]{:S(2)}) async-start(f32[16,32,128]{2,1,0:T(8,128)} %broadcast_in_dim.27), calls=%async_computation.2 | async-start | bytes 524288 | tf_op jit(solution)/shard_map/all_to_all | solution.py:239
  142.8 6.1 %all-gather.5.cloned.1.call-done = f32[48,128,128]{2,1,0:T(8,128)} async-done(((f32[3,128,128]{2,1,0:T(8,128)}), f32[48,128,128]{2,1,0:T(8,128)}) %all-gather.5.cloned.1.call-update) | async-done | bytes 3145744 | tf_op jit(solution)/shard_map/all_gather | solution.py:267
  148.9 5.6 %all-to-all-done.2 = f32[16,32,128]{2,1,0:T(8,128)S(1)} async-done(((f32[16,32,128]{2,1,0:T(8,128)}), f32[16,32,128]{2,1,0:T(8,128)S(1)}, u32[]{:S(2)}, u32[]{:S(2)}) %all-to-all-start.2) | async-done | bytes 262176 | tf_op jit(solution)/shard_map/all_to_all | solution.py:239
  156.9 14.5 %all_to_all.45 = f32[16,32,128]{2,1,0:T(8,128)} all-to-all(f32[16,32,128]{2,1,0:T(8,128)S(1)} %broadcast_in_dim.56), channel_id=1, replica_groups=mesh['row'=16,'col'=16] {'row'}, dimensions={0} | all-to-all | bytes 524288 | tf_op jit(solution)/shard_map/all_to_all | solution.py:239
  171.4 2.5 fusion
  173.9 14.4 %all_to_all.46 = f32[16,32,128]{2,1,0:T(8,128)S(1)} all-to-all(f32[16,32,128]{2,1,0:T(8,128)S(1)} %broadcast_in_dim.57), channel_id=1, replica_groups=mesh['row'=16,'col'=16] {'row'}, dimensions={0} | all-to-all | bytes 524288 | tf_op jit(solution)/shard_map/all_to_all | solution.py:239
  191.4 3.4 all-to-all-start.5
  194.9 11.1 %all-to-all-done.5.after_ref = f32[16,32,128]{2,1,0:T(8,128)S(1)} async-done(((f32[16,32,128]{2,1,0:T(8,128)}), f32[16,32,128]{2,1,0:T(8,128)S(1)}, u32[]{:S(2)}, u32[]{:S(2)}) %all-to-all-start.5) | async-done | bytes 262176 | tf_op jit(solution)/shard_map/all_to_all | solution.py:239
  206.2 40.4 %all_to_all.47.two_ref = f32[16,8,32,128]{3,2,1,0:T(8,128)S(1)} all-to-all(f32[16,8,32,128]{3,2,1,0:T(8,128)S(1)} %broadcast_in_dim.60), channel_id=1, replica_groups=mesh['row'=16,'col'=16] {'col'}, dimensions={0} | all-to-all | bytes 4194304 | tf_op jit(solution)/shard_map/all_to_all | solution.py:239
  247.2 2.6 copy.53
  250.1 6.1 %shard_map.69.start_ref = f32[384,512]{1,0:T(8,128)} custom-call(s32[1]{0:T(128)} %constant.36.clone.1.parity_ref, f32[384,512]{1,0:T(8,128)} %bitcast.77, f32[8,2,2,48,8,128]{5,4,3,2,1,0:T(8,128)} %bitcast.11.factor_ref, f32[16,8,2,32,128]{4,3,2,1,0:T(8,128)} %bitcast.66, f32[16,32,128]{2,1,0:T(8,128)} %copy-done.4), custom_call_target="tpu_custom_call" | custom-call | flops 2415919104 | bytes 3145728 | tf_op jit(solution)/shard_map/pallas_call | solution.py:170
  256.2 6.1 %shard_map.70.start_ref = f32[384,512]{1,0:T(8,128)} custom-call(s32[1]{0:T(128)} %constant.35.clone.1.parity_ref, f32[384,512]{1,0:T(8,128)} %shard_map.69.start_ref, f32[8,2,2,48,8,128]{5,4,3,2,1,0:T(8,128)} %bitcast.11.factor_ref, f32[16,8,2,32,128]{4,3,2,1,0:T(8,128)} %bitcast.67, f32[16,32,128]{2,1,0:T(8,128)} %copy-done.4), custom_call_target="tpu_custom_call" | custom-call | flops 2415919104 | bytes 3145728 | tf_op jit(solution)/shard_map/pallas_call | solution.py:170
  262.3 6.1 %shard_map.71.start_ref = f32[384,512]{1,0:T(8,128)} custom-call(s32[1]{0:T(128)} %bitcast.3.parity_ref.core_ref, f32[384,512]{1,0:T(8,128)} %shard_map.70.start_ref, f32[8,2,2,48,8,128]{5,4,3,2,1,0:T(8,128)} %bitcast.11.factor_ref, f32[16,8,1,32,128]{4,3,2,1,0:T(8,128)} %bitcast.69, f32[16,32,128]{2,1,0:T(8,128)} %copy-done.4), custom_call_target="tpu_custom_call" | custom-call | flops 2415919104 | bytes 3145728 | tf_op jit(solution)/shard_map/pallas_call | solution.py:170
  268.4 6.4 %shard_map.72.update_ref = f32[384,512]{1,0:T(8,128)} custom-call(s32[1]{0:T(128)} %bitcast.2.parity_ref, f32[384,512]{1,0:T(8,128)} %shard_map.71.start_ref, f32[8,2,2,48,8,128]{5,4,3,2,1,0:T(8,128)} %bitcast.11.factor_ref, f32[16,8,1,32,128]{4,3,2,1,0:T(8,128)} %bitcast.27.panel_ref, f32[16,32,128]{2,1,0:T(8,128)} %copy-done.4), custom_call_target="tpu_custom_call" | custom-call | flops 2415919104 | bytes 3145728 | tf_op jit(solution)/shard_map/pallas_call | solution.py:170
  275.9 2.5 shard_map.73
  280.4 11.5 %all_to_all.48 = f32[16,40,128]{2,1,0:T(8,128)S(1)} all-to-all(f32[16,40,128]{2,1,0:T(8,128)S(1)} %bitcast.82), channel_id=1, replica_groups=mesh['row'=16,'col'=16] {'col'}, dimensions={0} | all-to-all | bytes 655360 | tf_op jit(solution)/shard_map/all_to_all | solution.py:239
  298.1 5.5 %collective-permute-start.4 = (f32[40,128]{1,0:T(8,128)S(1)}, f32[40,128]{1,0:T(8,128)S(1)}, u32[]{:S(2)}, u32[]{:S(2)}) collective-permute-start(f32[40,128]{1,0:T(8,128)S(1)} %add.31), channel_id=1, source_target_pairs={{0,128},{16,144},{32,160},{48,176},{64,192},{80,208},{96,224},{112... | collective-permute-start | bytes 61448 | tf_op jit(solution)/shard_map/ppermute | solution.py:302
  304.8 10.7 %all_to_all.49 = f32[16,40,128]{2,1,0:T(8,128)S(1)} all-to-all(f32[16,40,128]{2,1,0:T(8,128)S(1)} %broadcast_in_dim.63), channel_id=1, replica_groups=mesh['row'=16,'col'=16] {'col'}, dimensions={0} | all-to-all | bytes 655360 | tf_op jit(solution)/shard_map/all_to_all | solution.py:239
  315.5 6.1 %collective-permute-start.5 = (f32[5,128,128]{2,1,0:T(8,128)S(1)}, f32[5,128,128]{2,1,0:T(8,128)S(1)}, u32[]{:S(2)}, u32[]{:S(2)}) collective-permute-start(f32[5,128,128]{2,1,0:T(8,128)S(1)} %bitcast.70), channel_id=1, source_target_pairs={{0,16},{16,0},{32,48},{48,32},{64,80},{80,64},{96,112},{112,96},{1... | collective-permute-start | bytes 983048 | tf_op jit(solution)/shard_map/ppermute | solution.py:305
  322.9 26.8 %shard_map.74 = f32[512,512]{1,0:T(8,128)S(1)} custom-call(s32[1]{0:T(128)} %bitcast.3.parity_ref.core_ref, f32[5,128,128]{2,1,0:T(8,128)S(1)} %bitcast.71, f32[5,128,128]{2,1,0:T(8,128)S(1)} %collective-permute-done.5.other_ref), custom_call_target="tpu_custom_call" | custom-call | tf_op jit(solution)/shard_map/pallas_call | solution.py:115
  (64 shorter events, 27.9 us)
Async XLA Ops:
  11.4 18.9 %all-to-all-start.1 = ((f32[16,1,512]{2,1,0:T(1,128)}), f32[16,1,512]{2,1,0:T(1,128)S(1)}, u32[]{:S(2)}, u32[]{:S(2)}) async-start(f32[16,1,512]{2,1,0:T(1,128)} %reshape.59), calls=%async_computation.1 | async-start | bytes 65536 | tf_op jit(solution)/shard_map/all_to_all | solution.py:239
  30.3 100.8 %all-to-all-start = ((f32[16,2,48,8,128]{4,3,2,1,0:T(8,128)}), f32[16,2,48,8,128]{4,3,2,1,0:T(8,128)}, u32[]{:S(2)}, u32[]{:S(2)}) async-start(f32[16,2,48,8,128]{4,3,2,1,0:T(8,128)} %shard_map.68), calls=%async_computation | async-start | bytes 12582912 | tf_op jit(solution)/shard_map/all_to_all | solution.py:239
  37.0 111.9 %all-gather.5.cloned.1.call-start = ((), (), s32[]{:S(2)}) async-start(), calls=%async_computation.9 | async-start | bytes 3342336 | tf_op jit(solution)/shard_map/all_gather | solution.py:267
  131.8 22.7 %all-to-all-start.2 = ((f32[16,32,128]{2,1,0:T(8,128)}), f32[16,32,128]{2,1,0:T(8,128)S(1)}, u32[]{:S(2)}, u32[]{:S(2)}) async-start(f32[16,32,128]{2,1,0:T(8,128)} %broadcast_in_dim.27), calls=%async_computation.2 | async-start | bytes 524288 | tf_op jit(solution)/shard_map/all_to_all | solution.py:239
  142.8 107.3 %all-gather.7.cloned.1.call-start = ((), (), s32[]{:S(2)}) async-start(), calls=%async_computation.10 | async-start | bytes 4456448 | tf_op jit(solution)/shard_map/all_gather | solution.py:280
  191.4 14.5 %all-to-all-start.5 = ((f32[16,32,128]{2,1,0:T(8,128)}), f32[16,32,128]{2,1,0:T(8,128)S(1)}, u32[]{:S(2)}, u32[]{:S(2)}) async-start(f32[16,32,128]{2,1,0:T(8,128)} %broadcast_in_dim.58), calls=%async_computation.5 | async-start | bytes 524288 | tf_op jit(solution)/shard_map/all_to_all | solution.py:239
  206.0 40.6 %copy-start.4 = (f32[16,32,128]{2,1,0:T(8,128)}, f32[16,32,128]{2,1,0:T(8,128)S(1)}, u32[]{:S(2)}) copy-start(f32[16,32,128]{2,1,0:T(8,128)S(1)} %all-to-all-done.5.after_ref) | copy-start | bytes 786436
  206.2 43.6 %copy-start.6 = (f32[8,48]{1,0:T(8,128)S(1)}, f32[8,48]{1,0:T(8,128)}, u32[]{:S(2)}) copy-start(f32[8,48]{1,0:T(8,128)} %param.9) | copy-start | bytes 4612
  246.6 9.6 %copy-start.1 = (f32[16,8,32,128]{3,2,1,0:T(8,128)}, f32[16,8,32,128]{3,2,1,0:T(8,128)S(1)}, u32[]{:S(2)}) copy-start(f32[16,8,32,128]{3,2,1,0:T(8,128)S(1)} %all_to_all.47.two_ref) | copy-start | bytes 6291460
  246.6 21.8 %collective-permute-start = (f32[16,8,32,128]{3,2,1,0:T(8,128)S(1)}, f32[16,8,32,128]{3,2,1,0:T(8,128)}, u32[]{:S(2)}, u32[]{:S(2)}) collective-permute-start(f32[16,8,32,128]{3,2,1,0:T(8,128)S(1)} %all_to_all.47.two_ref), channel_id=1, source_target_pairs={{0,16},{16,0},{32,48},{48,32},{64,80},{80,64},{96,112},{112,96},{1... | collective-permute-start | bytes 6291464 | tf_op jit(solution)/shard_map/ppermute | solution.py:290
  268.4 6.4 %copy-start = (f32[256,32,128]{2,1,0:T(8,128)S(1)}, f32[256,32,128]{2,1,0:T(8,128)}, u32[]{:S(2)}) copy-start(f32[256,32,128]{2,1,0:T(8,128)} %all-gather.7.cloned.1.call-done) | copy-start | bytes 12582916
  268.4 6.4 %copy-start.2 = (f32[16,8,32,128]{3,2,1,0:T(8,128)S(1)}, f32[16,8,32,128]{3,2,1,0:T(8,128)}, u32[]{:S(2)}) copy-start(f32[16,8,32,128]{3,2,1,0:T(8,128)} %copy-done.1) | copy-start | bytes 6291460
  274.8 1.1 copy-start.3
  278.5 1.8 collective-permute-start.1
  291.9 2.7 collective-permute-start.2
  294.6 3.5 collective-permute-start.3
  298.1 6.6 %collective-permute-start.4 = (f32[40,128]{1,0:T(8,128)S(1)}, f32[40,128]{1,0:T(8,128)S(1)}, u32[]{:S(2)}, u32[]{:S(2)}) collective-permute-start(f32[40,128]{1,0:T(8,128)S(1)} %add.31), channel_id=1, source_target_pairs={{0,128},{16,144},{32,160},{48,176},{64,192},{80,208},{96,224},{112... | collective-permute-start | bytes 61448 | tf_op jit(solution)/shard_map/ppermute | solution.py:302
  315.5 7.4 %collective-permute-start.5 = (f32[5,128,128]{2,1,0:T(8,128)S(1)}, f32[5,128,128]{2,1,0:T(8,128)S(1)}, u32[]{:S(2)}, u32[]{:S(2)}) collective-permute-start(f32[5,128,128]{2,1,0:T(8,128)S(1)} %bitcast.70), channel_id=1, source_target_pairs={{0,16},{16,0},{32,48},{48,32},{64,80},{80,64},{96,112},{112,96},{1... | collective-permute-start | bytes 983048 | tf_op jit(solution)/shard_map/ppermute | solution.py:305
  322.1 30.0 %copy-start.5 = (f32[8,48,512]{2,1,0:T(8,128)}, f32[8,48,512]{2,1,0:T(8,128)S(1)}, u32[]{:S(2)}) copy-start(f32[8,48,512]{2,1,0:T(8,128)S(1)} %copy.42) | copy-start | bytes 2359300
Sparse Core Ops, SparseCore 0:
  40.8 108.0 all-gather.4
  171.5 67.8 all-gather.6

commit v5 on v4

--- a/solution.py
+++ b/solution.py
@@ -126,47 +126,25 @@
     )(jnp.full((1,), core, jnp.int32), mine, other)
 
 
-def pack_kernel(one_ref, two_ref, out_ref):
-    for which, ref in enumerate((one_ref, two_ref)):
-        lead = which + 1
-        out_ref[0, which, :lead] = jnp.zeros((lead,) + ref.shape[1:], jnp.float32)
-        out_ref[0, which, lead:] = ref[...]
-
-
-def pack(one, two, own):
-    rows, steps, tile = one.shape
-    blocks = rows // own
-    specs = [pl.BlockSpec((f.shape[1], own, tile), lambda c: (0, c, 0)) for f in (one, two)]
-    shape = (blocks, 2, steps + 1, own, tile)
-    return pl.pallas_call(
-        pack_kernel,
-        out_shape=jax.ShapeDtypeStruct(shape, jnp.float32),
-        grid=(blocks,),
-        in_specs=specs,
-        out_specs=pl.BlockSpec((1,) + shape[1:], lambda c: (c, 0, 0, 0, 0)),
-        compiler_params=pltpu.CompilerParams(vmem_limit_bytes=56 * 1024 * 1024),
-        cost_estimate=pl.CostEstimate(flops=0, bytes_accessed=16 * one.size, transcendentals=0),
-    )(one.transpose(1, 0, 2), two.transpose(1, 0, 2))
-
-
 def pair(ref, first, second, rows):
     return jnp.concatenate([ref[first].reshape(rows, BLOCK), ref[second].reshape(rows, BLOCK)], axis=1)
 
 
-def update_kernel(parity_ref, start_ref, factor_ref, panel_ref, after_ref, out_ref):
+def update_kernel(parity_ref, start_ref, factor_ref, panel_ref, out_ref):
     @pl.when(pl.program_id(0) == 0)
     def _():
         out_ref[...] = start_ref[...]
 
-    rows, cols = out_ref.shape
-    f = pair(factor_ref, (0, 0, 0), (1, 0, 0), rows)
-    p = pair(panel_ref, (slice(None), 0, 0), (slice(None), 1, 0), cols)
-    out_ref[...] -= small_dot(f, p, 1, 1)
-
-
-def update(start, factors, panel, parity, which, after):
-    chips = factors.shape[0]
-    last = panel.shape[2] - 1
+    steps, own = factor_ref.shape[2:4]
+    cols = out_ref.shape[1]
+    lead = out_ref.shape[0] - steps * own
+    f = pair(factor_ref, (0, 0), (1, 0), steps * own)
+    p = pair(panel_ref, (slice(None), 0, 0), (slice(None), 0, 1), cols)
+    out_ref[lead:, :] -= small_dot(f, p, 1, 1)
+
+
+def update(start, factor, panels, which, parity):
+    chips = factor.shape[0]
     return pl.pallas_call(
         update_kernel,
         out_shape=jax.ShapeDtypeStruct(start.shape, jnp.float32),
@@ -175,9 +153,8 @@
             grid=(chips // 2,),
             in_specs=[
                 pl.BlockSpec(start.shape, lambda s, p: (0, 0)),
-                pl.BlockSpec((2, 1, 1) + factors.shape[3:], lambda s, p: (s, p[0], which, 0, 0, 0)),
-                pl.BlockSpec((panel.shape[0], 2, 1) + panel.shape[3:], lambda s, p: (0, s, p[0] * last, 0, 0)),
-                pl.BlockSpec(memory_space=pl.ANY),
+                pl.BlockSpec((2, 1) + factor.shape[2:], lambda s, p: (s, p[0], 0, 0, 0)),
+                pl.BlockSpec((panels.shape[0], 1, 2) + panels.shape[3:], lambda s, p: (0, which, s, 0, 0)),
             ],
             out_specs=pl.BlockSpec(start.shape, lambda s, p: (0, 0)),
         ),
@@ -185,16 +162,16 @@
         cost_estimate=pl.CostEstimate(
             flops=12 * start.size * chips * BLOCK, bytes_accessed=8 * start.size + 8 * start.size, transcendentals=0
         ),
-    )(jnp.full((1,), parity, jnp.int32), start, factors, panel, after)
-
-
-def finish_kernel(at_ref, update_ref, one_ref, two_ref, mass_ref, solved_ref, blocks_ref):
+    )(jnp.full((1,), parity, jnp.int32), start, factor, panels)
+
+
+def finish_kernel(at_ref, update_ref, panels_ref, mass_ref, solved_ref, blocks_ref):
     rounds, own, k_all = solved_ref.shape
     lanes = lax.broadcasted_iota(jnp.int32, (own, BLOCK), 1)
     rows = lax.broadcasted_iota(jnp.int32, (own, BLOCK), 0)
     take = jnp.where(lanes == rows + at_ref[1] * own, 1.0, 0.0)
-    solved_ref[0] = small_dot(take, one_ref[:, 0].reshape(k_all, BLOCK), 1, 1)
-    solved_ref[1] = small_dot(take, two_ref[:, 0].reshape(k_all, BLOCK), 1, 1)
+    for which in range(2):
+        solved_ref[which] = small_dot(take, panels_ref[:, which, 0].reshape(k_all, BLOCK), 1, 1)
     solved_ref[2:] = update_ref[2 * own :, :].reshape(rounds - 2, own, k_all)
     all_rows = solved_ref[...].reshape(own * rounds, k_all)
     weighted = all_rows * mass_ref[...]
@@ -206,10 +183,9 @@
             at += 1
 
 
-def finish(updated, one, two, mass, row, col, shape):
+def finish(updated, panels, mass, place, col, shape):
     rounds, own, k_all = shape
     count = len(block_pairs(k_all))
-    panel = (one.shape[0], 1) + one.shape[2:]
     return pl.pallas_call(
         finish_kernel,
         out_shape=(
@@ -221,8 +197,7 @@
             grid=(1,),
             in_specs=[
                 pl.BlockSpec(updated.shape, lambda s, at: (0, 0)),
-                pl.BlockSpec(panel, lambda s, at: (0, at[0], 0, 0)),
-                pl.BlockSpec(panel, lambda s, at: (0, at[0] // 2, 0, 0)),
+                pl.BlockSpec(panels.shape[:2] + (1,) + panels.shape[3:], lambda s, at: (0, 0, at[0], 0, 0)),
                 pl.BlockSpec((own * rounds, 1), lambda s, at: (0, 0)),
             ],
             out_specs=(
@@ -230,9 +205,9 @@
                 pl.BlockSpec((count, BLOCK, BLOCK), lambda s, at: (0, 0, 0)),
             ),
         ),
-        compiler_params=pltpu.CompilerParams(vmem_limit_bytes=24 * 1024 * 1024),
+        compiler_params=pltpu.CompilerParams(vmem_limit_bytes=56 * 1024 * 1024),
         cost_estimate=pl.CostEstimate(flops=8 * updated.size * k_all, bytes_accessed=12 * updated.size, transcendentals=0),
-    )(jnp.stack([row, col]).astype(jnp.int32), updated, one, two, mass.T.reshape(-1, 1))
+    )(jnp.stack([place, col]).astype(jnp.int32), updated, panels, mass.T.reshape(-1, 1))
 
 
 def exchange(blocks, axis):
@@ -256,41 +231,43 @@
     tile = own * cols_n
     k_part = k_all // cols_n
     swap = [(i, i ^ 1) for i in range(rows_n)]
-
-    mats = jnp.stack([block_inverse[0], factor_one[:, 0, :], block_inverse[1]])
-    heads = vectors[:, :2, :].reshape(own, 2, cols_n, k_part).transpose(2, 1, 0, 3)
-    mats, heads, factor_one = lax.optimization_barrier((mats, heads, factor_one))
-    heads = exchange(heads, "col")
-    heads = heads.transpose(1, 3, 0, 2).reshape(2, k_part, tile)
-    head_rows = share(heads[0], "row")
-
+    turn = [(r * cols_n + c, c * cols_n + r) for r in range(rows_n) for c in range(cols_n)]
+
+    mats = jnp.stack([factor_one[:, 0, :], block_inverse[1]])
     mats = lax.all_gather(mats, "col")
+
+    turned = lax.ppermute(vectors[:, 0, :], ("row", "col"), turn)
+    block = share(turned, "row").reshape(tile, k_all)
+    parts = jnp.einsum("qk,iq->ki", block, block_inverse[0], precision=HIGHEST, preferred_element_type=jnp.float32)
+    one = exchange(parts.reshape(cols_n, k_part, tile), "col").sum(axis=0)
+
+    head = vectors[:, 1, :].reshape(own, cols_n, k_part).transpose(1, 0, 2)
+    head = exchange(head, "col")
+    head = head.transpose(2, 0, 1).reshape(k_part, tile)
 
     def half(panel_rows):
         return lax.dynamic_index_in_dim(
             panel_rows.reshape((rows_n // 2, 2) + panel_rows.shape[1:]), core, 1, keepdims=False
         )
 
-    factors = pack(factor_one, factor_two, own)
-    factors = exchange(factors, "col")
-    mats, factors = lax.optimization_barrier((mats, factors))
-    factors = factors.reshape((rows_n // 2, 2) + factors.shape[1:])
-
-    one_rows = share(product(head_rows, mats[:, 0]), "row")
-    one_whole = lax.all_gather(one_rows, "col")
-    remain_head = heads[1] - product(one_rows, mats[:, 1])
+    def redistribute(factor):
+        parts = factor.reshape((cols_n, own) + factor.shape[1:]).transpose(0, 2, 1, 3)
+        parts = exchange(parts, "col")
+        return parts.reshape((rows_n // 2, 2) + parts.shape[1:])
+
+    one_rows = share(one, "row")
+    remain_head = head - product(one_rows, mats[:, 0])
     remain_rows = share(remain_head, "row")
-    two_rows = share(product(remain_rows, mats[:, 2]), "row")
-    two_mine = share(half(two_rows), "col")
-
-    by_parity = one_whole.reshape((cols_n, rows_n // 2, 2) + one_whole.shape[2:])
+    two_rows = share(product(remain_rows, mats[:, 1]), "row")
+    mine = lax.all_gather(jnp.stack([half(one_rows), half(two_rows)]), "col")
+    other = lax.ppermute(mine, "row", swap)
+    f_one, f_two = redistribute(factor_one), redistribute(factor_two)
+
     done = vectors.transpose(1, 0, 2).reshape(-1, k_all)
-    for parity in (0, 1):
-        done = update(done, factors, by_parity, parity, 0, two_rows)
-    two_other = lax.ppermute(two_mine, "row", swap)
-    done = update(done, factors, two_mine[:, :, None], core, 1, two_rows)
-    done = update(done, factors, two_other[:, :, None], 1 - core, 1, two_rows)
-    solved, blocks = finish(done, one_whole, two_mine, lumped_mass, row, col, (rounds, own, k_all))
+    for which, factor in enumerate((f_one, f_two)):
+        done = update(done, factor, mine, which, core)
+        done = update(done, factor, other, which, 1 - core)
+    solved, blocks = finish(done, mine, lumped_mass, row // 2, col, (rounds, own, k_all))
     solved = solved.transpose(1, 0, 2)
 
     blocks = blocks.reshape((2, -1, BLOCK))

time: 360 us -> 364 us (1.011)
  blocking collectives: 91.4 us -> 66.3 us
  waiting for transfers between devices: 122 us -> 147 us
  Pallas kernels: 65.3 us -> 55.8 us
  local copies, waits for them, and re-layouts: 10.4 us -> 18.2 us
    all_gather x1, waiting for transfers between devices: 0.01 us -> 71.1 us  [body(): mine = lax.all_gather(jnp.stack([half(one_rows), half(two_rows)]), 'col')]
    all_to_all x4 -> x6, waiting for transfers between devices: 109 us -> 68.9 us  [exchange(): return lax.all_to_all(blocks, axis, 0, 0)]
    all_to_all x5 -> x4, blocking collectives: 91.4 us -> 66.3 us  [exchange(): return lax.all_to_all(blocks, axis, 0, 0)]
    pallas_call x1 -> x0, Pallas kernels: 11.3 us -> none  [pack(): pl.pallas_call(pack_kernel, out_shape=jax.ShapeDtypeStruct(shape, jnp.flo...]
    all_gather x1, waiting for transfers between devices: 6.05 us -> 0.01 us  [body(): mats = lax.all_gather(mats, 'col')]
    transpose x0 -> x3, local copies, waits for them, and re-layouts: none -> 5.59 us  [the longest x2 5.57 us: redistribute(): factor.reshape((cols_n, own) + factor.shape[1:]).transpose(0, 2, 1, 3)]
    ppermute x1, starting transfers between devices: 0.61 us -> 4.51 us  [body(): turned = lax.ppermute(vectors[:, 0, :], ('row', 'col'), turn)]
    all_to_all x4 -> x6, starting transfers between devices: 28.7 us -> 26.4 us  [exchange(): return lax.all_to_all(blocks, axis, 0, 0)]
  transfers between devices with their start and end apart: 12 -> 15, of which waited for: 9 -> 11; matrix products, arithmetic and copies ran while one was open for 3% -> 5% of each run, Pallas kernels for 8% -> 3%
where the time goes in v5:
time: 364 us; the launch traced here: 363 us
  waiting for transfers between devices  147 us (40%)
  blocking collectives  66.3 us (18%)
  Pallas kernels  55.8 us (15%)
  starting transfers between devices  48.1 us (13%)
  local copies, waits for them, and re-layouts  18.2 us (5%)
  between operations  14.3 us (4%)
  matrix products  8.96 us (2%)
  other arithmetic  4.61 us (1%)
    all_gather x1, waiting for transfers between devices, body(): mine = lax.all_gather(jnp.stack([half(one_rows), half(two_rows)]), 'col')  71.1 us
    all_to_all x6, waiting for transfers between devices, exchange(): return lax.all_to_all(blocks, axis, 0, 0)  68.9 us
    all_to_all x4, blocking collectives, exchange(): return lax.all_to_all(blocks, axis, 0, 0)  66.3 us
    pallas_call x1, Pallas kernels, inverse_factor(): pl.pallas_call(functools.partial(inverse_kernel, scale), out_shape=jax.Sh...  26.8 us
    all_to_all x6, starting transfers between devices, exchange(): return lax.all_to_all(blocks, axis, 0, 0)  26.4 us
    pallas_call x4, Pallas kernels, update(): pl.pallas_call(update_kernel, out_shape=jax.ShapeDtypeStruct(start.shape,...  24.2 us
    ppermute x3, starting transfers between devices, body(): lax.ppermute(part, 'row', [(i, i ^ step) for i in range(rows_n)])  9.31 us
  transfers between devices with their start and end apart: 15, of which 11 were waited for; matrix products, arithmetic and copies ran while one was open for 5% of the time, Pallas kernels for 3%

profile of v5, /device:TPU:1, one launch (start us, length us, event | category | flops | bytes accessed | tf_op | source)
XLA Modules:
  0.0 362.8 jit_solution(12467387831627515196)
XLA Ops:
  10.8 4.5 %collective-permute-start = (f32[8,512]{1,0:T(8,128)S(1)}, f32[8,512]{1,0:T(8,128)S(1)}, u32[]{:S(2)}, u32[]{:S(2)}) collective-permute-start(f32[8,512]{1,0:T(8,128)S(1)} %bitcast.97), channel_id=1, source_target_pairs={{0,0},{1,16},{2,32},{3,48},{4,64},{5,80},{6,96},{7,112},{8,128},{9... | collective-permute-start | bytes 49160 | tf_op jit(solution)/shard_map/ppermute | solution.py:239
  16.8 28.6 %all_to_all.50 = f32[16,8,512]{2,1,0:T(8,128)S(1)} all-to-all(f32[16,8,512]{2,1,0:T(8,128)S(1)} %broadcast_in_dim.16), channel_id=1, replica_groups=mesh['row'=16,'col'=16] {'row'}, dimensions={0} | all-to-all | bytes 524288 | tf_op jit(solution)/shard_map/all_to_all | solution.py:214
  47.4 4.6 %all-to-all-start.2 = ((f32[16,32,128]{2,1,0:T(8,128)}), f32[16,32,128]{2,1,0:T(8,128)S(1)}, u32[]{:S(2)}, u32[]{:S(2)}) async-start(f32[16,32,128]{2,1,0:T(8,128)} %fusion.3), calls=%async_computation.2 | async-start | bytes 524288 | tf_op jit(solution)/shard_map/all_to_all | solution.py:214
  52.9 11.0 %all-to-all-done.2 = f32[16,32,128]{2,1,0:T(8,128)S(1)} async-done(((f32[16,32,128]{2,1,0:T(8,128)}), f32[16,32,128]{2,1,0:T(8,128)S(1)}, u32[]{:S(2)}, u32[]{:S(2)}) %all-to-all-start.2) | async-done | bytes 262176 | tf_op jit(solution)/shard_map/all_to_all | solution.py:214
  67.4 6.3 %all-to-all-done.4 = f32[16,1,256]{2,1,0:T(1,128)S(1)} async-done(((f32[16,1,256]{2,1,0:T(1,128)}), f32[16,1,256]{2,1,0:T(1,128)S(1)}, u32[]{:S(2)}, u32[]{:S(2)}) %all-to-all-start.4) | async-done | bytes 16416 | tf_op jit(solution)/shard_map/all_to_all | solution.py:214
  74.5 5.2 %all-to-all-start.3 = ((f32[16,32,128]{2,1,0:T(8,128)}), f32[16,32,128]{2,1,0:T(8,128)S(1)}, u32[]{:S(2)}, u32[]{:S(2)}) async-start(f32[16,32,128]{2,1,0:T(8,128)} %broadcast_in_dim.17), calls=%async_computation.3 | async-start | bytes 524288 | tf_op jit(solution)/shard_map/all_to_all | solution.py:214
  80.9 10.6 %all-to-all-done.3 = f32[16,32,128]{2,1,0:T(8,128)S(1)} async-done(((f32[16,32,128]{2,1,0:T(8,128)}), f32[16,32,128]{2,1,0:T(8,128)S(1)}, u32[]{:S(2)}, u32[]{:S(2)}) %all-to-all-start.3) | async-done | bytes 262176 | tf_op jit(solution)/shard_map/all_to_all | solution.py:214
  93.9 14.3 %all_to_all.51 = f32[16,32,128]{2,1,0:T(8,128)S(1)} all-to-all(f32[16,32,128]{2,1,0:T(8,128)S(1)} %broadcast_in_dim.18), channel_id=1, replica_groups=mesh['row'=16,'col'=16] {'row'}, dimensions={0} | all-to-all | bytes 524288 | tf_op jit(solution)/shard_map/all_to_all | solution.py:214
  115.5 10.4 %all-to-all-done.6 = f32[16,32,128]{2,1,0:T(8,128)S(1)} async-done(((f32[16,32,128]{2,1,0:T(8,128)}), f32[16,32,128]{2,1,0:T(8,128)S(1)}, u32[]{:S(2)}, u32[]{:S(2)}) %all-to-all-start.6) | async-done | bytes 262176 | tf_op jit(solution)/shard_map/all_to_all | solution.py:214
  127.5 3.8 %copy_bitcast_fusion = f32[16,47,8,128]{3,2,1,0:T(8,128)} fusion(f32[128,47,128]{2,0,1:T(8,128)} %param.6), kind=kLoop, calls=%fused_computation | loop fusion | bytes 6160384 | tf_op jit(solution)/shard_map/transpose | solution.py:254
  131.3 4.5 %all-to-all-start = ((f32[16,47,8,128]{3,2,1,0:T(8,128)}), f32[16,47,8,128]{3,2,1,0:T(8,128)}, u32[]{:S(2)}, u32[]{:S(2)}) async-start(f32[16,47,8,128]{3,2,1,0:T(8,128)} %copy_bitcast_fusion), calls=%async_computation | async-start | bytes 6160384 | tf_op jit(solution)/shard_map/all_to_all | solution.py:214
  135.8 71.1 %all-gather.7.cloned.1.call-done = f32[32,8,32,128]{3,2,1,0:T(8,128)} async-done(((f32[2,8,32,128]{3,2,1,0:T(8,128)}), f32[32,8,32,128]{3,2,1,0:T(8,128)}) %all-gather.7.cloned.1.call-update) | async-done | bytes 4194320 | tf_op jit(solution)/shard_map/all_gather | solution.py:262
  209.3 5.2 %all-to-all-start.7 = ((f32[16,46,8,128]{3,2,1,0:T(8,128)}), f32[16,46,8,128]{3,2,1,0:T(8,128)}, u32[]{:S(2)}, u32[]{:S(2)}) async-start(f32[16,46,8,128]{3,2,1,0:T(8,128)} %copy_bitcast_fusion.1), calls=%async_computation.7 | async-start | bytes 6029312 | tf_op jit(solution)/shard_map/all_to_all | solution.py:214
  218.5 6.1 %shard_map.68.start_ref = f32[384,512]{1,0:T(8,128)} custom-call(s32[1]{0:T(128)} %bitcast.3.parity_ref.core_ref, f32[384,512]{1,0:T(8,128)} %bitcast.91, f32[8,2,47,8,128]{4,3,2,1,0:T(8,128)} %bitcast.8.factor_ref, f32[16,2,8,32,128]{4,3,2,1,0:T(8,128)} %bitcast.80), custom_call_target="tpu_custom_call" | custom-call | flops 2415919104 | bytes 3145728 | tf_op jit(solution)/shard_map/pallas_call | solution.py:148
  224.6 6.1 %shard_map.69.start_ref = f32[384,512]{1,0:T(8,128)} custom-call(s32[1]{0:T(128)} %bitcast.2.parity_ref, f32[384,512]{1,0:T(8,128)} %shard_map.68.start_ref, f32[8,2,47,8,128]{4,3,2,1,0:T(8,128)} %bitcast.8.factor_ref, f32[16,2,8,32,128]{4,3,2,1,0:T(8,128)} %collective-permute-done.1.panel_ref), custom_call_target="tpu_custom_call" | custom-call | flops 2415919104 | bytes 3145728 | tf_op jit(solution)/shard_map/pallas_call | solution.py:148
  230.7 30.6 %all-to-all-done.7 = f32[16,46,8,128]{3,2,1,0:T(8,128)} async-done(((f32[16,46,8,128]{3,2,1,0:T(8,128)}), f32[16,46,8,128]{3,2,1,0:T(8,128)}, u32[]{:S(2)}, u32[]{:S(2)}) %all-to-all-start.7) | async-done | bytes 3014688 | tf_op jit(solution)/shard_map/all_to_all | solution.py:214
  261.2 6.0 %shard_map.70.start_ref = f32[384,512]{1,0:T(8,128)} custom-call(s32[1]{0:T(128)} %bitcast.3.parity_ref.core_ref, f32[384,512]{1,0:T(8,128)} %shard_map.69.start_ref, f32[8,2,46,8,128]{4,3,2,1,0:T(8,128)} %bitcast.31.factor_ref, f32[16,2,8,32,128]{4,3,2,1,0:T(8,128)} %bitcast.81), custom_call_target="tpu_custom_call" | custom-call | flops 2415919104 | bytes 3145728 | tf_op jit(solution)/shard_map/pallas_call | solution.py:148
  267.2 6.0 %shard_map.71.update_ref = f32[384,512]{1,0:T(8,128)} custom-call(s32[1]{0:T(128)} %bitcast.2.parity_ref, f32[384,512]{1,0:T(8,128)} %shard_map.70.start_ref, f32[8,2,46,8,128]{4,3,2,1,0:T(8,128)} %bitcast.31.factor_ref, f32[16,2,8,32,128]{4,3,2,1,0:T(8,128)} %collective-permute-done.1.panel_ref), custom_call_target="tpu_custom_call" | custom-call | flops 2415919104 | bytes 3145728 | tf_op jit(solution)/shard_map/pallas_call | solution.py:148
  273.3 4.8 %shard_map.72 = (f32[48,8,512]{2,1,0:T(8,128)}, f32[10,128,128]{2,1,0:T(8,128)}) custom-call(s32[2]{0:T(128)} %pad_add_fusion.at_ref, f32[384,512]{1,0:T(8,128)} %shard_map.71.update_ref, f32[16,2,8,32,128]{4,3,2,1,0:T(8,128)} %bitcast.82, f32[384,1]{1,0:T(8,128)} %reshape.71.mass_ref), custom_call_target="tpu_custom_call" | custom-call | flops 805306368 | bytes 2359296 | tf_op jit(solution)/shard_map/pallas_call | solution.py:189
  282.7 12.7 %all_to_all.52 = f32[16,40,128]{2,1,0:T(8,128)S(1)} all-to-all(f32[16,40,128]{2,1,0:T(8,128)S(1)} %bitcast.86), channel_id=1, replica_groups=mesh['row'=16,'col'=16] {'col'}, dimensions={0} | all-to-all | bytes 655360 | tf_op jit(solution)/shard_map/all_to_all | solution.py:214
  301.6 5.7 %collective-permute-start.5 = (f32[40,128]{1,0:T(8,128)S(1)}, f32[40,128]{1,0:T(8,128)S(1)}, u32[]{:S(2)}, u32[]{:S(2)}) collective-permute-start(f32[40,128]{1,0:T(8,128)S(1)} %add.33), channel_id=1, source_target_pairs={{0,128},{16,144},{32,160},{48,176},{64,192},{80,208},{96,224},{112... | collective-permute-start | bytes 61448 | tf_op jit(solution)/shard_map/ppermute | solution.py:279
  308.6 10.7 %all_to_all.53 = f32[16,40,128]{2,1,0:T(8,128)S(1)} all-to-all(f32[16,40,128]{2,1,0:T(8,128)S(1)} %broadcast_in_dim.20), channel_id=1, replica_groups=mesh['row'=16,'col'=16] {'col'}, dimensions={0} | all-to-all | bytes 655360 | tf_op jit(solution)/shard_map/all_to_all | solution.py:214
  319.3 5.8 %collective-permute-start.6 = (f32[5,128,128]{2,1,0:T(8,128)S(1)}, f32[5,128,128]{2,1,0:T(8,128)S(1)}, u32[]{:S(2)}, u32[]{:S(2)}) collective-permute-start(f32[5,128,128]{2,1,0:T(8,128)S(1)} %bitcast.77), channel_id=1, source_target_pairs={{0,16},{16,0},{32,48},{48,32},{64,80},{80,64},{96,112},{112,96},{1... | collective-permute-start | bytes 983048 | tf_op jit(solution)/shard_map/ppermute | solution.py:282
  326.7 26.8 %shard_map.73 = f32[512,512]{1,0:T(8,128)S(1)} custom-call(s32[1]{0:T(128)} %bitcast.3.parity_ref.core_ref, f32[5,128,128]{2,1,0:T(8,128)S(1)} %bitcast.78, f32[5,128,128]{2,1,0:T(8,128)S(1)} %collective-permute-done.6.other_ref), custom_call_target="tpu_custom_call" | custom-call | tf_op jit(solution)/shard_map/pallas_call | solution.py:115
  (63 shorter events, 47.2 us)
Async XLA Ops:
  7.2 200.4 %copy-start = (f32[128,46,128]{2,0,1:T(8,128)S(1)}, f32[128,46,128]{2,0,1:T(8,128)}, u32[]{:S(2)}) copy-start(f32[128,46,128]{2,0,1:T(8,128)} %param.7) | copy-start | bytes 9043972
  7.2 84.4 %all-gather.5.cloned.1.call-start = ((), (), s32[]{:S(2)}) async-start(), calls=%async_computation.10 | async-start | bytes 2228224 | tf_op jit(solution)/shard_map/all_gather | solution.py:237
  10.8 5.9 %collective-permute-start = (f32[8,512]{1,0:T(8,128)S(1)}, f32[8,512]{1,0:T(8,128)S(1)}, u32[]{:S(2)}, u32[]{:S(2)}) collective-permute-start(f32[8,512]{1,0:T(8,128)S(1)} %bitcast.97), channel_id=1, source_target_pairs={{0,0},{1,16},{2,32},{3,48},{4,64},{5,80},{6,96},{7,112},{8,128},{9... | collective-permute-start | bytes 49160 | tf_op jit(solution)/shard_map/ppermute | solution.py:239
  47.4 16.5 %all-to-all-start.2 = ((f32[16,32,128]{2,1,0:T(8,128)}), f32[16,32,128]{2,1,0:T(8,128)S(1)}, u32[]{:S(2)}, u32[]{:S(2)}) async-start(f32[16,32,128]{2,1,0:T(8,128)} %fusion.3), calls=%async_computation.2 | async-start | bytes 524288 | tf_op jit(solution)/shard_map/all_to_all | solution.py:214
  63.9 9.8 %all-to-all-start.4 = ((f32[16,1,256]{2,1,0:T(1,128)}), f32[16,1,256]{2,1,0:T(1,128)S(1)}, u32[]{:S(2)}, u32[]{:S(2)}) async-start(f32[16,1,256]{2,1,0:T(1,128)} %reshape.73), calls=%async_computation.4 | async-start | bytes 32768 | tf_op jit(solution)/shard_map/all_to_all | solution.py:214
  74.5 17.0 %all-to-all-start.3 = ((f32[16,32,128]{2,1,0:T(8,128)}), f32[16,32,128]{2,1,0:T(8,128)S(1)}, u32[]{:S(2)}, u32[]{:S(2)}) async-start(f32[16,32,128]{2,1,0:T(8,128)} %broadcast_in_dim.17), calls=%async_computation.3 | async-start | bytes 524288 | tf_op jit(solution)/shard_map/all_to_all | solution.py:214
  111.3 14.6 %all-to-all-start.6 = ((f32[16,32,128]{2,1,0:T(8,128)}), f32[16,32,128]{2,1,0:T(8,128)S(1)}, u32[]{:S(2)}, u32[]{:S(2)}) async-start(f32[16,32,128]{2,1,0:T(8,128)} %broadcast_in_dim.19), calls=%async_computation.6 | async-start | bytes 524288 | tf_op jit(solution)/shard_map/all_to_all | solution.py:214
  114.7 92.1 %all-gather.7.cloned.1.call-start = ((), (), s32[]{:S(2)}) async-start(), calls=%async_computation.11 | async-start | bytes 4456448 | tf_op jit(solution)/shard_map/all_gather | solution.py:262
  131.3 78.0 %all-to-all-start = ((f32[16,47,8,128]{3,2,1,0:T(8,128)}), f32[16,47,8,128]{3,2,1,0:T(8,128)}, u32[]{:S(2)}, u32[]{:S(2)}) async-start(f32[16,47,8,128]{3,2,1,0:T(8,128)} %copy_bitcast_fusion), calls=%async_computation | async-start | bytes 6160384 | tf_op jit(solution)/shard_map/all_to_all | solution.py:214
  206.9 17.7 %collective-permute-start.1 = (f32[16,2,8,32,128]{4,3,2,1,0:T(8,128)}, f32[16,2,8,32,128]{4,3,2,1,0:T(8,128)}, u32[]{:S(2)}, u32[]{:S(2)}) collective-permute-start(f32[16,2,8,32,128]{4,3,2,1,0:T(8,128)} %bitcast.79), channel_id=1, source_target_pairs={{0,16},{16,0},{32,48},{48,32},{64,80},{80,64},{96,112},{112,96},{1... | collective-permute-start | bytes 12582920 | tf_op jit(solution)/shard_map/ppermute | solution.py:263
  209.3 7.7 %copy-start.2 = (f32[8,48]{1,0:T(8,128)S(1)}, f32[8,48]{1,0:T(8,128)}, u32[]{:S(2)}) copy-start(f32[8,48]{1,0:T(8,128)} %param.9) | copy-start | bytes 4612
  209.3 51.9 %all-to-all-start.7 = ((f32[16,46,8,128]{3,2,1,0:T(8,128)}), f32[16,46,8,128]{3,2,1,0:T(8,128)}, u32[]{:S(2)}, u32[]{:S(2)}) async-start(f32[16,46,8,128]{3,2,1,0:T(8,128)} %copy_bitcast_fusion.1), calls=%async_computation.7 | async-start | bytes 6029312 | tf_op jit(solution)/shard_map/all_to_all | solution.py:214
  279.0 2.6 collective-permute-start.2
  295.4 2.7 collective-permute-start.3
  298.1 3.5 collective-permute-start.4
  301.6 7.0 %collective-permute-start.5 = (f32[40,128]{1,0:T(8,128)S(1)}, f32[40,128]{1,0:T(8,128)S(1)}, u32[]{:S(2)}, u32[]{:S(2)}) collective-permute-start(f32[40,128]{1,0:T(8,128)S(1)} %add.33), channel_id=1, source_target_pairs={{0,128},{16,144},{32,160},{48,176},{64,192},{80,208},{96,224},{112... | collective-permute-start | bytes 61448 | tf_op jit(solution)/shard_map/ppermute | solution.py:279
  319.3 7.4 %collective-permute-start.6 = (f32[5,128,128]{2,1,0:T(8,128)S(1)}, f32[5,128,128]{2,1,0:T(8,128)S(1)}, u32[]{:S(2)}, u32[]{:S(2)}) collective-permute-start(f32[5,128,128]{2,1,0:T(8,128)S(1)} %bitcast.77), channel_id=1, source_target_pairs={{0,16},{16,0},{32,48},{48,32},{64,80},{80,64},{96,112},{112,96},{1... | collective-permute-start | bytes 983048 | tf_op jit(solution)/shard_map/ppermute | solution.py:282
  326.7 29.2 %copy-start.1 = (f32[8,48,512]{2,1,0:T(8,128)}, f32[8,48,512]{2,1,0:T(8,128)S(1)}, u32[]{:S(2)}) copy-start(f32[8,48,512]{2,1,0:T(8,128)S(1)} %copy.39) | copy-start | bytes 2359300
Sparse Core Ops, SparseCore 0:
  11.0 55.6 all-gather.4
  127.6 79.1 all-gather.6

commit v6 on v5

--- a/solution.py
+++ b/solution.py
@@ -126,25 +126,25 @@
     )(jnp.full((1,), core, jnp.int32), mine, other)
 
 
-def pair(ref, first, second, rows):
-    return jnp.concatenate([ref[first].reshape(rows, BLOCK), ref[second].reshape(rows, BLOCK)], axis=1)
-
-
-def update_kernel(parity_ref, start_ref, factor_ref, panel_ref, out_ref):
+def update_kernel(core_ref, start_ref, factor_ref, mine_ref, other_ref, out_ref):
     @pl.when(pl.program_id(0) == 0)
     def _():
         out_ref[...] = start_ref[...]
 
-    steps, own = factor_ref.shape[2:4]
+    chips, _, steps, own, _ = factor_ref.shape
     cols = out_ref.shape[1]
     lead = out_ref.shape[0] - steps * own
-    f = pair(factor_ref, (0, 0), (1, 0), steps * own)
-    p = pair(panel_ref, (slice(None), 0, 0), (slice(None), 0, 1), cols)
-    out_ref[lead:, :] -= small_dot(f, p, 1, 1)
-
-
-def update(start, factor, panels, which, parity):
+    f, p = [], []
+    for ref, parity in ((mine_ref, core_ref[0]), (other_ref, 1 - core_ref[0])):
+        for z in range(chips):
+            f.append(factor_ref[z, parity].reshape(steps * own, BLOCK))
+            p.append(ref[:, 0, z].reshape(cols, BLOCK))
+    out_ref[lead:, :] -= small_dot(jnp.concatenate(f, axis=1), jnp.concatenate(p, axis=1), 1, 1)
+
+
+def update(start, factor, mine, other, which, core):
     chips = factor.shape[0]
+    panel = pl.BlockSpec((mine.shape[0], 1, 2) + mine.shape[3:], lambda s, p: (0, which, s, 0, 0))
     return pl.pallas_call(
         update_kernel,
         out_shape=jax.ShapeDtypeStruct(start.shape, jnp.float32),
@@ -153,16 +153,17 @@
             grid=(chips // 2,),
             in_specs=[
                 pl.BlockSpec(start.shape, lambda s, p: (0, 0)),
-                pl.BlockSpec((2, 1) + factor.shape[2:], lambda s, p: (s, p[0], 0, 0, 0)),
-                pl.BlockSpec((panels.shape[0], 1, 2) + panels.shape[3:], lambda s, p: (0, which, s, 0, 0)),
+                pl.BlockSpec((2,) + factor.shape[1:], lambda s, p: (s, 0, 0, 0, 0)),
+                panel,
+                panel,
             ],
             out_specs=pl.BlockSpec(start.shape, lambda s, p: (0, 0)),
         ),
         compiler_params=pltpu.CompilerParams(vmem_limit_bytes=56 * 1024 * 1024),
         cost_estimate=pl.CostEstimate(
-            flops=12 * start.size * chips * BLOCK, bytes_accessed=8 * start.size + 8 * start.size, transcendentals=0
-        ),
-    )(jnp.full((1,), parity, jnp.int32), start, factor, panels)
+            flops=24 * start.size * chips * BLOCK, bytes_accessed=24 * start.size, transcendentals=0
+        ),
+    )(jnp.full((1,), core, jnp.int32), start, factor, mine, other)
 
 
 def finish_kernel(at_ref, update_ref, panels_ref, mass_ref, solved_ref, blocks_ref):
@@ -219,8 +220,65 @@
     return exchange(jnp.broadcast_to(block[None], (size,) + block.shape), axis)
 
 
-def product(rows, tiles):
-    return jnp.einsum("rkq,riq->ki", rows, tiles, precision=HIGHEST, preferred_element_type=jnp.float32)
+def gather_row(block):
+    size = lax.axis_size("row")
+    row = lax.axis_index("row")
+    step, axis = size // 2, 0
+    while step:
+        got = lax.ppermute(block, "row", [(i, i ^ step) for i in range(size)])
+        upper = (row & step) != 0
+        block = jnp.stack([jnp.where(upper, got, block), jnp.where(upper, block, got)], axis=axis)
+        step, axis = step // 2, axis + 1
+    return block.reshape((size,) + block.shape[axis:])
+
+
+def product_kernel(rows_ref, tiles_ref, after_ref, out_ref):
+    count = rows_ref.shape[0]
+    rows = jnp.concatenate([rows_ref[r] for r in range(count)], axis=1)
+    tiles = jnp.concatenate([tiles_ref[r, 0] for r in range(count)], axis=1)
+    out_ref[...] = small_dot(rows, tiles, 1, 1)
+
+
+def product(rows, tiles, which, after):
+    shape = (rows.shape[1], tiles.shape[2])
+    return pl.pallas_call(
+        product_kernel,
+        out_shape=jax.ShapeDtypeStruct(shape, jnp.float32),
+        grid=(1,),
+        in_specs=[
+            pl.BlockSpec(rows.shape, lambda s: (0, 0, 0)),
+            pl.BlockSpec((tiles.shape[0], 1) + tiles.shape[2:], lambda s: (0, which, 0, 0)),
+            pl.BlockSpec(memory_space=pl.ANY),
+        ],
+        out_specs=pl.BlockSpec(shape, lambda s: (0, 0)),
+        compiler_params=pltpu.CompilerParams(vmem_limit_bytes=56 * 1024 * 1024),
+        cost_estimate=pl.CostEstimate(
+            flops=12 * rows.size * tiles.shape[2], bytes_accessed=4 * (rows.size + tiles.size // 2), transcendentals=0
+        ),
+    )(rows, tiles, after)
+
+
+def halves_kernel(core_ref, one_ref, two_ref, after_ref, out_ref):
+    out_ref[0] = one_ref[:, 0]
+    out_ref[1] = two_ref[:, 0]
+
+
+def halves(one, two, core, after):
+    pairs = (one.shape[0] // 2, 2) + one.shape[1:]
+    half = pl.BlockSpec((pairs[0], 1) + pairs[2:], lambda s, p: (0, p[0], 0, 0))
+    shape = (2, pairs[0]) + pairs[2:]
+    return pl.pallas_call(
+        halves_kernel,
+        out_shape=jax.ShapeDtypeStruct(shape, jnp.float32),
+        grid_spec=pltpu.PrefetchScalarGridSpec(
+            num_scalar_prefetch=1,
+            grid=(1,),
+            in_specs=[half, half, pl.BlockSpec(memory_space=pl.ANY)],
+            out_specs=pl.BlockSpec(shape, lambda s, p: (0, 0, 0, 0)),
+        ),
+        compiler_params=pltpu.CompilerParams(vmem_limit_bytes=56 * 1024 * 1024),
+        cost_estimate=pl.CostEstimate(flops=0, bytes_accessed=8 * one.size, transcendentals=0),
+    )(jnp.full((1,), core, jnp.int32), one.reshape(pairs), two.reshape(pairs), after)
 
 
 def body(vectors, factor_one, factor_two, block_inverse, lumped_mass):
@@ -237,36 +295,33 @@
     mats = lax.all_gather(mats, "col")
 
     turned = lax.ppermute(vectors[:, 0, :], ("row", "col"), turn)
-    block = share(turned, "row").reshape(tile, k_all)
+    block = gather_row(turned).reshape(tile, k_all)
     parts = jnp.einsum("qk,iq->ki", block, block_inverse[0], precision=HIGHEST, preferred_element_type=jnp.float32)
-    one = exchange(parts.reshape(cols_n, k_part, tile), "col").sum(axis=0)
-
-    head = vectors[:, 1, :].reshape(own, cols_n, k_part).transpose(1, 0, 2)
-    head = exchange(head, "col")
+    head = vectors[:, 1, :].reshape(own, cols_n, k_part).transpose(1, 0, 2).reshape(cols_n, -1, BLOCK)
+    head_rows = head.shape[1]
+    head = jnp.pad(head, ((0, 0), (0, own - head_rows), (0, 0)))
+    both = exchange(jnp.concatenate([parts.reshape(cols_n, k_part, tile), head], axis=1), "col")
+    one = both[:, :k_part].sum(axis=0)
+    head = both[:, k_part : k_part + head_rows].reshape(cols_n, own, k_part)
     head = head.transpose(2, 0, 1).reshape(k_part, tile)
-
-    def half(panel_rows):
-        return lax.dynamic_index_in_dim(
-            panel_rows.reshape((rows_n // 2, 2) + panel_rows.shape[1:]), core, 1, keepdims=False
-        )
 
     def redistribute(factor):
         parts = factor.reshape((cols_n, own) + factor.shape[1:]).transpose(0, 2, 1, 3)
         parts = exchange(parts, "col")
         return parts.reshape((rows_n // 2, 2) + parts.shape[1:])
 
-    one_rows = share(one, "row")
-    remain_head = head - product(one_rows, mats[:, 0])
-    remain_rows = share(remain_head, "row")
-    two_rows = share(product(remain_rows, mats[:, 1]), "row")
-    mine = lax.all_gather(jnp.stack([half(one_rows), half(two_rows)]), "col")
+    one_rows = gather_row(one)
+    f_one = redistribute(factor_one)
+    f_two = redistribute(factor_two)
+    remain_head = head - product(one_rows, mats, 0, one_rows)
+    remain_rows = gather_row(remain_head)
+    two_rows = gather_row(product(remain_rows, mats, 1, f_one))
+    mine = lax.all_gather(halves(one_rows, two_rows, core, f_two), "col")
     other = lax.ppermute(mine, "row", swap)
-    f_one, f_two = redistribute(factor_one), redistribute(factor_two)
 
     done = vectors.transpose(1, 0, 2).reshape(-1, k_all)
     for which, factor in enumerate((f_one, f_two)):
-        done = update(done, factor, mine, which, core)
-        done = update(done, factor, other, which, 1 - core)
+        done = update(done, factor, mine, other, which, core)
     solved, blocks = finish(done, mine, lumped_mass, row // 2, col, (rounds, own, k_all))
     solved = solved.transpose(1, 0, 2)
 

time: 364 us -> 345 us (0.948)
  blocking collectives: 66.3 us -> 24.3 us
  starting transfers between devices: 48.1 us -> 88.3 us
  waiting for transfers between devices: 147 us -> 133 us
  matrix products: 8.96 us -> 3.56 us
    all_to_all x6 -> x3, waiting for transfers between devices: 68.9 us -> 13.2 us  [exchange(): return lax.all_to_all(blocks, axis, 0, 0)]
    ppermute x0 -> x16, starting transfers between devices: none -> 48.9 us  [gather_row(): got = lax.ppermute(block, 'row', [(i, i ^ step) for i in range(size)])]
    all_to_all x4 -> x2, blocking collectives: 66.3 us -> 24.3 us  [exchange(): return lax.all_to_all(blocks, axis, 0, 0)]
    ppermute x0 -> x16, waiting for transfers between devices: none -> 32.3 us  [gather_row(): got = lax.ppermute(block, 'row', [(i, i ^ step) for i in range(size)])]
    all_gather x1, waiting for transfers between devices: 0.01 us -> 21.7 us  [body(): mats = lax.all_gather(mats, 'col')]
    all_gather x1, waiting for transfers between devices: 71.1 us -> 55.5 us  [body(): mine = lax.all_gather(halves(one_rows, two_rows, core, f_two), 'col')]
    all_to_all x6 -> x3, starting transfers between devices: 26.4 us -> 18.6 us  [exchange(): return lax.all_to_all(blocks, axis, 0, 0)]
    pallas_call x0 -> x3, Pallas kernels: none -> 7.73 us  [the longest x2 6.03 us: product(): pl.pallas_call(product_kernel, out_shape=jax.ShapeDtypeStruct(shape, jnp....]
  transfers between devices with their start and end apart: 15 -> 28, of which waited for: 11 -> 24; matrix products, arithmetic and copies ran while one was open for 5% -> 6% of each run, Pallas kernels for 3% -> 2%
where the time goes in v6:
time: 345 us; the launch traced here: 344 us
  waiting for transfers between devices  133 us (39%)
  starting transfers between devices  88.3 us (26%)
  Pallas kernels  55.9 us (16%)
  blocking collectives  24.3 us (7%)
  local copies, waits for them, and re-layouts  17.1 us (5%)
  between operations  14.4 us (4%)
  other arithmetic  7.96 us (2%)
  matrix products  3.56 us (1%)
    all_gather x1, waiting for transfers between devices, body(): mine = lax.all_gather(halves(one_rows, two_rows, core, f_two), 'col')  55.5 us
    ppermute x16, starting transfers between devices, gather_row(): got = lax.ppermute(block, 'row', [(i, i ^ step) for i in range(size)])  48.9 us
    ppermute x16, waiting for transfers between devices, gather_row(): got = lax.ppermute(block, 'row', [(i, i ^ step) for i in range(size)])  32.3 us
    pallas_call x1, Pallas kernels, inverse_factor(): pl.pallas_call(functools.partial(inverse_kernel, scale), out_shape=jax.Sh...  26.8 us
    all_to_all x2, blocking collectives, exchange(): return lax.all_to_all(blocks, axis, 0, 0)  24.3 us
    all_gather x1, waiting for transfers between devices, body(): mats = lax.all_gather(mats, 'col')  21.7 us
    all_to_all x3, starting transfers between devices, exchange(): return lax.all_to_all(blocks, axis, 0, 0)  18.6 us
    pallas_call x2, Pallas kernels, update(): pl.pallas_call(update_kernel, out_shape=jax.ShapeDtypeStruct(start.shape,...  16.6 us
  transfers between devices with their start and end apart: 28, of which 24 were waited for; matrix products, arithmetic and copies ran while one was open for 6% of the time, Pallas kernels for 2%

profile of v6, /device:TPU:1, one launch (start us, length us, event | category | flops | bytes accessed | tf_op | source)
XLA Modules:
  0.0 344.2 jit_solution(11215520952288666870)
XLA Ops:
  8.4 4.5 %collective-permute-start = (f32[8,512]{1,0:T(8,128)S(1)}, f32[8,512]{1,0:T(8,128)S(1)}, u32[]{:S(2)}, u32[]{:S(2)}) collective-permute-start(f32[8,512]{1,0:T(8,128)S(1)} %bitcast.143), channel_id=1, source_target_pairs={{0,0},{1,16},{2,32},{3,48},{4,64},{5,80},{6,96},{7,112},{8,128},{9... | collective-permute-start | bytes 49160 | tf_op jit(solution)/shard_map/ppermute | solution.py:297
  14.3 14.2 %collective-permute-start.1 = (f32[8,512]{1,0:T(8,128)S(1)}, f32[8,512]{1,0:T(8,128)S(1)}, u32[]{:S(2)}, u32[]{:S(2)}) collective-permute-start(f32[8,512]{1,0:T(8,128)S(1)} %collective-permute-done), channel_id=1, source_target_pairs={{0,128},{16,144},{32,160},{48,176},{64,192},{80,208},{96,224},{112... | collective-permute-start | bytes 49160 | tf_op jit(solution)/shard_map/ppermute | solution.py:228
  37.3 3.8 %collective-permute-start.4 = (f32[2,2,2,8,512]{4,3,0,1,2:T(8,128)S(1)}, f32[2,2,2,8,512]{4,3,0,1,2:T(8,128)S(1)}, u32[]{:S(2)}, u32[]{:S(2)}) collective-permute-start(f32[2,2,2,8,512]{4,3,0,1,2:T(8,128)S(1)} %pad_maximum_fusion.5), channel_id=1, source_target_pairs={{0,16},{16,0},{32,48},{48,32},{64,80},{80,64},{96,112},{112,96},{1... | collective-permute-start | bytes 393224 | tf_op jit(solution)/shard_map/ppermute | solution.py:228
  44.3 6.7 %all-to-all-start.1 = ((f32[16,40,128]{2,1,0:T(8,128)}), f32[16,40,128]{2,1,0:T(8,128)S(1)}, u32[]{:S(2)}, u32[]{:S(2)}) async-start(f32[16,40,128]{2,1,0:T(8,128)} %select_maximum_fusion), calls=%async_computation.1 | async-start | bytes 655360 | tf_op jit(solution)/shard_map/all_to_all | solution.py:215
  51.0 3.7 %copy_bitcast_fusion = f32[16,47,8,128]{3,2,1,0:T(8,128)} fusion(f32[128,47,128]{2,0,1:T(8,128)} %param.6), kind=kLoop, calls=%fused_computation | loop fusion | bytes 6160384 | tf_op jit(solution)/shard_map/transpose | solution.py:309
  54.7 5.4 %all-to-all-done.1 = f32[16,40,128]{2,1,0:T(8,128)S(1)} async-done(((f32[16,40,128]{2,1,0:T(8,128)}), f32[16,40,128]{2,1,0:T(8,128)S(1)}, u32[]{:S(2)}, u32[]{:S(2)}) %all-to-all-start.1) | async-done | bytes 327712 | tf_op jit(solution)/shard_map/all_to_all | solution.py:215
  60.1 4.5 %all-to-all-start = ((f32[16,47,8,128]{3,2,1,0:T(8,128)}), f32[16,47,8,128]{3,2,1,0:T(8,128)}, u32[]{:S(2)}, u32[]{:S(2)}) async-start(f32[16,47,8,128]{3,2,1,0:T(8,128)} %copy_bitcast_fusion), calls=%async_computation | async-start | bytes 6160384 | tf_op jit(solution)/shard_map/all_to_all | solution.py:215
  64.7 4.3 %collective-permute-start.5 = (f32[32,128]{1,0:T(8,128)S(1)}, f32[32,128]{1,0:T(8,128)S(1)}, u32[]{:S(2)}, u32[]{:S(2)}) collective-permute-start(f32[32,128]{1,0:T(8,128)S(1)} %slice_reduce_fusion), channel_id=1, source_target_pairs={{0,128},{16,144},{32,160},{48,176},{64,192},{80,208},{96,224},{112... | collective-permute-start | bytes 49160 | tf_op jit(solution)/shard_map/ppermute | solution.py:228
  80.1 4.3 %collective-permute-start.8 = (f32[2,2,2,32,128]{4,3,0,1,2:T(8,128)}, f32[2,2,2,32,128]{4,3,0,1,2:T(8,128)}, u32[]{:S(2)}, u32[]{:S(2)}) collective-permute-start(f32[2,2,2,32,128]{4,3,0,1,2:T(8,128)} %pad_maximum_fusion.6), channel_id=1, source_target_pairs={{0,16},{16,0},{32,48},{48,32},{64,80},{80,64},{96,112},{112,96},{1... | collective-permute-start | bytes 393224 | tf_op jit(solution)/shard_map/ppermute | solution.py:228
  87.4 21.7 %all-gather.5.cloned.1.call-done = f32[32,128,128]{2,1,0:T(8,128)} async-done(((f32[2,128,128]{2,1,0:T(8,128)}), f32[32,128,128]{2,1,0:T(8,128)}) %all-gather.5.cloned.1.call-update) | async-done | bytes 2097168 | tf_op jit(solution)/shard_map/all_gather | solution.py:295
  112.9 4.2 %collective-permute-start.9 = (f32[32,128]{1,0:T(8,128)S(1)}, f32[32,128]{1,0:T(8,128)S(1)}, u32[]{:S(2)}, u32[]{:S(2)}) collective-permute-start(f32[32,128]{1,0:T(8,128)S(1)} %sub.11), channel_id=1, source_target_pairs={{0,128},{16,144},{32,160},{48,176},{64,192},{80,208},{96,224},{112... | collective-permute-start | bytes 49160 | tf_op jit(solution)/shard_map/ppermute | solution.py:228
  124.0 7.4 %all-to-all-start.2 = ((f32[16,46,8,128]{3,2,1,0:T(8,128)}), f32[16,46,8,128]{3,2,1,0:T(8,128)}, u32[]{:S(2)}, u32[]{:S(2)}) async-start(f32[16,46,8,128]{3,2,1,0:T(8,128)} %copy_bitcast_fusion.1), calls=%async_computation.2 | async-start | bytes 6029312 | tf_op jit(solution)/shard_map/all_to_all | solution.py:215
  143.0 3.6 %collective-permute-start.13 = (f32[32,128]{1,0:T(8,128)}, f32[32,128]{1,0:T(8,128)S(1)}, u32[]{:S(2)}, u32[]{:S(2)}) collective-permute-start(f32[32,128]{1,0:T(8,128)} %shard_map.69), channel_id=1, source_target_pairs={{0,128},{16,144},{32,160},{48,176},{64,192},{80,208},{96,224},{112... | collective-permute-start | bytes 49160 | tf_op jit(solution)/shard_map/ppermute | solution.py:228
  150.5 4.4 %collective-permute-done.14 = f32[2,32,128]{2,1,0:T(8,128)S(1)} collective-permute-done((f32[2,32,128]{2,1,0:T(8,128)S(1)}, f32[2,32,128]{2,1,0:T(8,128)S(1)}, u32[]{:S(2)}, u32[]{:S(2)}) %collective-permute-start.14) | collective-permute-done | bytes 32800 | tf_op jit(solution)/shard_map/ppermute | solution.py:228
  164.4 7.8 %all-to-all-done.2 = f32[16,46,8,128]{3,2,1,0:T(8,128)} async-done(((f32[16,46,8,128]{3,2,1,0:T(8,128)}), f32[16,46,8,128]{3,2,1,0:T(8,128)}, u32[]{:S(2)}, u32[]{:S(2)}) %all-to-all-start.2) | async-done | bytes 3014688 | tf_op jit(solution)/shard_map/all_to_all | solution.py:215
  173.9 55.5 %all-gather.7.cloned.1.call-done = f32[32,8,32,128]{3,2,1,0:T(8,128)} async-done(((f32[2,8,32,128]{3,2,1,0:T(8,128)}), f32[32,8,32,128]{3,2,1,0:T(8,128)}) %all-gather.7.cloned.1.call-update) | async-done | bytes 4194320 | tf_op jit(solution)/shard_map/all_gather | solution.py:319
  237.2 8.4 %shard_map.71.start_ref = f32[384,512]{1,0:T(8,128)} custom-call(s32[1]{0:T(128)} %bitcast.2.core_ref, f32[384,512]{1,0:T(8,128)} %bitcast.134, f32[8,2,47,8,128]{4,3,2,1,0:T(8,128)} %bitcast.7.after_ref.factor_ref, f32[16,2,8,32,128]{4,3,2,1,0:T(8,128)} %bitcast.121, f32[16,2,8,32,128]{4,3,2,1,0:T(8,128)} %collective-permute-done.17.other_ref), custom_call_target="tpu_custom_call" | custom-call | flops 4831838208 | bytes 4718592 | tf_op jit(solution)/shard_map/pallas_call | solution.py:148
  245.6 8.2 %shard_map.72.update_ref = f32[384,512]{1,0:T(8,128)} custom-call(s32[1]{0:T(128)} %bitcast.2.core_ref, f32[384,512]{1,0:T(8,128)} %shard_map.71.start_ref, f32[8,2,46,8,128]{4,3,2,1,0:T(8,128)} %bitcast.57.after_ref.factor_ref, f32[16,2,8,32,128]{4,3,2,1,0:T(8,128)} %bitcast.122, f32[16,2,8,32,128]{4,3,2,1,0:T(8,128)} %collective-permute-done.17.other_ref), custom_call_target="tpu_custom_call" | custom-call | flops 4831838208 | bytes 4718592 | tf_op jit(solution)/shard_map/pallas_call | solution.py:148
  253.8 4.8 %shard_map.73 = (f32[48,8,512]{2,1,0:T(8,128)}, f32[10,128,128]{2,1,0:T(8,128)}) custom-call(s32[2]{0:T(128)} %pad_add_fusion.at_ref, f32[384,512]{1,0:T(8,128)} %shard_map.72.update_ref, f32[16,2,8,32,128]{4,3,2,1,0:T(8,128)} %bitcast.123, f32[384,1]{1,0:T(8,128)} %reshape.75.mass_ref), custom_call_target="tpu_custom_call" | custom-call | flops 805306368 | bytes 2359296 | tf_op jit(solution)/shard_map/pallas_call | solution.py:190
  263.2 13.6 %all_to_all.25 = f32[16,40,128]{2,1,0:T(8,128)S(1)} all-to-all(f32[16,40,128]{2,1,0:T(8,128)S(1)} %bitcast.126), channel_id=1, replica_groups=mesh['row'=16,'col'=16] {'col'}, dimensions={0} | all-to-all | bytes 655360 | tf_op jit(solution)/shard_map/all_to_all | solution.py:215
  283.1 5.7 %collective-permute-start.21 = (f32[40,128]{1,0:T(8,128)S(1)}, f32[40,128]{1,0:T(8,128)S(1)}, u32[]{:S(2)}, u32[]{:S(2)}) collective-permute-start(f32[40,128]{1,0:T(8,128)S(1)} %add.32), channel_id=1, source_target_pairs={{0,128},{16,144},{32,160},{48,176},{64,192},{80,208},{96,224},{112... | collective-permute-start | bytes 61448 | tf_op jit(solution)/shard_map/ppermute | solution.py:334
  290.1 10.7 %all_to_all.26 = f32[16,40,128]{2,1,0:T(8,128)S(1)} all-to-all(f32[16,40,128]{2,1,0:T(8,128)S(1)} %broadcast_in_dim.5), channel_id=1, replica_groups=mesh['row'=16,'col'=16] {'col'}, dimensions={0} | all-to-all | bytes 655360 | tf_op jit(solution)/shard_map/all_to_all | solution.py:215
  300.8 5.8 %collective-permute-start.22 = (f32[5,128,128]{2,1,0:T(8,128)S(1)}, f32[5,128,128]{2,1,0:T(8,128)S(1)}, u32[]{:S(2)}, u32[]{:S(2)}) collective-permute-start(f32[5,128,128]{2,1,0:T(8,128)S(1)} %bitcast.116), channel_id=1, source_target_pairs={{0,16},{16,0},{32,48},{48,32},{64,80},{80,64},{96,112},{112,96},{1... | collective-permute-start | bytes 983048 | tf_op jit(solution)/shard_map/ppermute | solution.py:337
  308.2 26.8 %shard_map.74 = f32[512,512]{1,0:T(8,128)S(1)} custom-call(s32[1]{0:T(128)} %bitcast.2.core_ref, f32[5,128,128]{2,1,0:T(8,128)S(1)} %bitcast.117, f32[5,128,128]{2,1,0:T(8,128)S(1)} %collective-permute-done.22.other_ref), custom_call_target="tpu_custom_call" | custom-call | tf_op jit(solution)/shard_map/pallas_call | solution.py:115
  (119 shorter events, 89.6 us)
Async XLA Ops:
  7.2 102.0 %all-gather.5.cloned.1.call-start = ((), (), s32[]{:S(2)}) async-start(), calls=%async_computation.5 | async-start | bytes 2228224 | tf_op jit(solution)/shard_map/all_gather | solution.py:295
  8.4 5.9 %collective-permute-start = (f32[8,512]{1,0:T(8,128)S(1)}, f32[8,512]{1,0:T(8,128)S(1)}, u32[]{:S(2)}, u32[]{:S(2)}) collective-permute-start(f32[8,512]{1,0:T(8,128)S(1)} %bitcast.143), channel_id=1, source_target_pairs={{0,0},{1,16},{2,32},{3,48},{4,64},{5,80},{6,96},{7,112},{8,128},{9... | collective-permute-start | bytes 49160 | tf_op jit(solution)/shard_map/ppermute | solution.py:297
  14.3 15.9 %collective-permute-start.1 = (f32[8,512]{1,0:T(8,128)S(1)}, f32[8,512]{1,0:T(8,128)S(1)}, u32[]{:S(2)}, u32[]{:S(2)}) collective-permute-start(f32[8,512]{1,0:T(8,128)S(1)} %collective-permute-done), channel_id=1, source_target_pairs={{0,128},{16,144},{32,160},{48,176},{64,192},{80,208},{96,224},{112... | collective-permute-start | bytes 49160 | tf_op jit(solution)/shard_map/ppermute | solution.py:228
  30.2 3.8 %collective-permute-start.2 = (f32[2,8,512]{2,1,0:T(8,128)S(1)}, f32[2,8,512]{2,1,0:T(8,128)S(1)}, u32[]{:S(2)}, u32[]{:S(2)}) collective-permute-start(f32[2,8,512]{2,1,0:T(8,128)S(1)} %pad_maximum_fusion.14), channel_id=1, source_target_pairs={{0,64},{16,80},{32,96},{48,112},{64,0},{80,16},{96,32},{112,48},{1... | collective-permute-start | bytes 98312 | tf_op jit(solution)/shard_map/ppermute | solution.py:228
  37.3 4.8 %collective-permute-start.4 = (f32[2,2,2,8,512]{4,3,0,1,2:T(8,128)S(1)}, f32[2,2,2,8,512]{4,3,0,1,2:T(8,128)S(1)}, u32[]{:S(2)}, u32[]{:S(2)}) collective-permute-start(f32[2,2,2,8,512]{4,3,0,1,2:T(8,128)S(1)} %pad_maximum_fusion.5), channel_id=1, source_target_pairs={{0,16},{16,0},{32,48},{48,32},{64,80},{80,64},{96,112},{112,96},{1... | collective-permute-start | bytes 393224 | tf_op jit(solution)/shard_map/ppermute | solution.py:228
  44.3 15.9 %all-to-all-start.1 = ((f32[16,40,128]{2,1,0:T(8,128)}), f32[16,40,128]{2,1,0:T(8,128)S(1)}, u32[]{:S(2)}, u32[]{:S(2)}) async-start(f32[16,40,128]{2,1,0:T(8,128)} %select_maximum_fusion), calls=%async_computation.1 | async-start | bytes 655360 | tf_op jit(solution)/shard_map/all_to_all | solution.py:215
  60.1 63.9 %all-to-all-start = ((f32[16,47,8,128]{3,2,1,0:T(8,128)}), f32[16,47,8,128]{3,2,1,0:T(8,128)}, u32[]{:S(2)}, u32[]{:S(2)}) async-start(f32[16,47,8,128]{3,2,1,0:T(8,128)} %copy_bitcast_fusion), calls=%async_computation | async-start | bytes 6160384 | tf_op jit(solution)/shard_map/all_to_all | solution.py:215
  64.7 6.6 %collective-permute-start.5 = (f32[32,128]{1,0:T(8,128)S(1)}, f32[32,128]{1,0:T(8,128)S(1)}, u32[]{:S(2)}, u32[]{:S(2)}) collective-permute-start(f32[32,128]{1,0:T(8,128)S(1)} %slice_reduce_fusion), channel_id=1, source_target_pairs={{0,128},{16,144},{32,160},{48,176},{64,192},{80,208},{96,224},{112... | collective-permute-start | bytes 49160 | tf_op jit(solution)/shard_map/ppermute | solution.py:228
  71.3 4.5 %collective-permute-start.6 = (f32[2,32,128]{2,1,0:T(8,128)S(1)}, f32[2,32,128]{2,1,0:T(8,128)S(1)}, u32[]{:S(2)}, u32[]{:S(2)}) collective-permute-start(f32[2,32,128]{2,1,0:T(8,128)S(1)} %pad_maximum_fusion.15), channel_id=1, source_target_pairs={{0,64},{16,80},{32,96},{48,112},{64,0},{80,16},{96,32},{112,48},{1... | collective-permute-start | bytes 98312 | tf_op jit(solution)/shard_map/ppermute | solution.py:228
  75.7 3.7 %collective-permute-start.7 = (f32[2,2,32,128]{3,2,0,1:T(8,128)S(1)}, f32[2,2,32,128]{3,2,0,1:T(8,128)S(1)}, u32[]{:S(2)}, u32[]{:S(2)}) collective-permute-start(f32[2,2,32,128]{3,2,0,1:T(8,128)S(1)} %pad_maximum_fusion.11), channel_id=1, source_target_pairs={{0,32},{16,48},{32,0},{48,16},{64,96},{80,112},{96,64},{112,80},{1... | collective-permute-start | bytes 196616 | tf_op jit(solution)/shard_map/ppermute | solution.py:228
  80.1 5.6 %collective-permute-start.8 = (f32[2,2,2,32,128]{4,3,0,1,2:T(8,128)}, f32[2,2,2,32,128]{4,3,0,1,2:T(8,128)}, u32[]{:S(2)}, u32[]{:S(2)}) collective-permute-start(f32[2,2,2,32,128]{4,3,0,1,2:T(8,128)} %pad_maximum_fusion.6), channel_id=1, source_target_pairs={{0,16},{16,0},{32,48},{48,32},{64,80},{80,64},{96,112},{112,96},{1... | collective-permute-start | bytes 393224 | tf_op jit(solution)/shard_map/ppermute | solution.py:228
  112.9 6.5 %collective-permute-start.9 = (f32[32,128]{1,0:T(8,128)S(1)}, f32[32,128]{1,0:T(8,128)S(1)}, u32[]{:S(2)}, u32[]{:S(2)}) collective-permute-start(f32[32,128]{1,0:T(8,128)S(1)} %sub.11), channel_id=1, source_target_pairs={{0,128},{16,144},{32,160},{48,176},{64,192},{80,208},{96,224},{112... | collective-permute-start | bytes 49160 | tf_op jit(solution)/shard_map/ppermute | solution.py:228
  119.4 12.1 %collective-permute-start.10 = (f32[2,32,128]{2,1,0:T(8,128)S(1)}, f32[2,32,128]{2,1,0:T(8,128)S(1)}, u32[]{:S(2)}, u32[]{:S(2)}) collective-permute-start(f32[2,32,128]{2,1,0:T(8,128)S(1)} %pad_maximum_fusion.16), channel_id=1, source_target_pairs={{0,64},{16,80},{32,96},{48,112},{64,0},{80,16},{96,32},{112,48},{1... | collective-permute-start | bytes 98312 | tf_op jit(solution)/shard_map/ppermute | solution.py:228
  124.0 48.2 %all-to-all-start.2 = ((f32[16,46,8,128]{3,2,1,0:T(8,128)}), f32[16,46,8,128]{3,2,1,0:T(8,128)}, u32[]{:S(2)}, u32[]{:S(2)}) async-start(f32[16,46,8,128]{3,2,1,0:T(8,128)} %copy_bitcast_fusion.1), calls=%async_computation.2 | async-start | bytes 6029312 | tf_op jit(solution)/shard_map/all_to_all | solution.py:215
  131.5 98.0 %all-gather.7.cloned.1.call-start = ((), (), s32[]{:S(2)}) async-start(), calls=%async_computation.6 | async-start | bytes 4456448 | tf_op jit(solution)/shard_map/all_gather | solution.py:319
  134.8 4.4 %collective-permute-start.12 = (f32[2,2,2,32,128]{4,3,0,1,2:T(8,128)S(1)}, f32[2,2,2,32,128]{4,3,0,1,2:T(8,128)S(1)}, u32[]{:S(2)}, u32[]{:S(2)}) collective-permute-start(f32[2,2,2,32,128]{4,3,0,1,2:T(8,128)S(1)} %pad_maximum_fusion.8), channel_id=1, source_target_pairs={{0,16},{16,0},{32,48},{48,32},{64,80},{80,64},{96,112},{112,96},{1... | collective-permute-start | bytes 393224 | tf_op jit(solution)/shard_map/ppermute | solution.py:228
  143.0 6.8 %collective-permute-start.13 = (f32[32,128]{1,0:T(8,128)}, f32[32,128]{1,0:T(8,128)S(1)}, u32[]{:S(2)}, u32[]{:S(2)}) collective-permute-start(f32[32,128]{1,0:T(8,128)} %shard_map.69), channel_id=1, source_target_pairs={{0,128},{16,144},{32,160},{48,176},{64,192},{80,208},{96,224},{112... | collective-permute-start | bytes 49160 | tf_op jit(solution)/shard_map/ppermute | solution.py:228
  150.5 4.4 %collective-permute-start.14 = (f32[2,32,128]{2,1,0:T(8,128)S(1)}, f32[2,32,128]{2,1,0:T(8,128)S(1)}, u32[]{:S(2)}, u32[]{:S(2)}) collective-permute-start(f32[2,32,128]{2,1,0:T(8,128)S(1)} %pad_maximum_fusion.17), channel_id=1, source_target_pairs={{0,64},{16,80},{32,96},{48,112},{64,0},{80,16},{96,32},{112,48},{1... | collective-permute-start | bytes 98312 | tf_op jit(solution)/shard_map/ppermute | solution.py:228
  155.0 3.8 %collective-permute-start.15 = (f32[2,2,32,128]{3,2,0,1:T(8,128)S(1)}, f32[2,2,32,128]{3,2,0,1:T(8,128)S(1)}, u32[]{:S(2)}, u32[]{:S(2)}) collective-permute-start(f32[2,2,32,128]{3,2,0,1:T(8,128)S(1)} %pad_maximum_fusion.13), channel_id=1, source_target_pairs={{0,32},{16,48},{32,0},{48,16},{64,96},{80,112},{96,64},{112,80},{1... | collective-permute-start | bytes 196616 | tf_op jit(solution)/shard_map/ppermute | solution.py:228
  159.4 4.1 %collective-permute-start.16 = (f32[2,2,2,32,128]{4,3,0,1,2:T(8,128)}, f32[2,2,2,32,128]{4,3,0,1,2:T(8,128)S(1)}, u32[]{:S(2)}, u32[]{:S(2)}) collective-permute-start(f32[2,2,2,32,128]{4,3,0,1,2:T(8,128)} %pad_maximum_fusion.9), channel_id=1, source_target_pairs={{0,16},{16,0},{32,48},{48,32},{64,80},{80,64},{96,112},{112,96},{1... | collective-permute-start | bytes 393224 | tf_op jit(solution)/shard_map/ppermute | solution.py:228
  229.4 7.8 %collective-permute-start.17 = (f32[16,2,8,32,128]{4,3,2,1,0:T(8,128)}, f32[16,2,8,32,128]{4,3,2,1,0:T(8,128)}, u32[]{:S(2)}, u32[]{:S(2)}) collective-permute-start(f32[16,2,8,32,128]{4,3,2,1,0:T(8,128)} %bitcast.120), channel_id=1, source_target_pairs={{0,16},{16,0},{32,48},{48,32},{64,80},{80,64},{96,112},{112,96},{1... | collective-permute-start | bytes 12582920 | tf_op jit(solution)/shard_map/ppermute | solution.py:320
  279.6 3.5 %collective-permute-start.20 = (f32[40,128]{1,0:T(8,128)S(1)}, f32[40,128]{1,0:T(8,128)S(1)}, u32[]{:S(2)}, u32[]{:S(2)}) collective-permute-start(f32[40,128]{1,0:T(8,128)S(1)} %add.31), channel_id=1, source_target_pairs={{0,64},{16,80},{32,96},{48,112},{64,0},{80,16},{96,32},{112,48},{1... | collective-permute-start | bytes 61448 | tf_op jit(solution)/shard_map/ppermute | solution.py:334
  283.1 7.0 %collective-permute-start.21 = (f32[40,128]{1,0:T(8,128)S(1)}, f32[40,128]{1,0:T(8,128)S(1)}, u32[]{:S(2)}, u32[]{:S(2)}) collective-permute-start(f32[40,128]{1,0:T(8,128)S(1)} %add.32), channel_id=1, source_target_pairs={{0,128},{16,144},{32,160},{48,176},{64,192},{80,208},{96,224},{112... | collective-permute-start | bytes 61448 | tf_op jit(solution)/shard_map/ppermute | solution.py:334
  300.8 7.4 %collective-permute-start.22 = (f32[5,128,128]{2,1,0:T(8,128)S(1)}, f32[5,128,128]{2,1,0:T(8,128)S(1)}, u32[]{:S(2)}, u32[]{:S(2)}) collective-permute-start(f32[5,128,128]{2,1,0:T(8,128)S(1)} %bitcast.116), channel_id=1, source_target_pairs={{0,16},{16,0},{32,48},{48,32},{64,80},{80,64},{96,112},{112,96},{1... | collective-permute-start | bytes 983048 | tf_op jit(solution)/shard_map/ppermute | solution.py:337
  (7 other events, 223.4 us)
Sparse Core Ops, SparseCore 0:
  31.1 77.9 all-gather.4
  174.1 55.3 all-gather.6

commit v7 on v6

--- a/solution.py
+++ b/solution.py
@@ -138,13 +138,13 @@
     for ref, parity in ((mine_ref, core_ref[0]), (other_ref, 1 - core_ref[0])):
         for z in range(chips):
             f.append(factor_ref[z, parity].reshape(steps * own, BLOCK))
-            p.append(ref[:, 0, z].reshape(cols, BLOCK))
+            p.append(ref[:, z].reshape(cols, BLOCK))
     out_ref[lead:, :] -= small_dot(jnp.concatenate(f, axis=1), jnp.concatenate(p, axis=1), 1, 1)
 
 
-def update(start, factor, mine, other, which, core):
+def update(start, factor, mine, other, core):
     chips = factor.shape[0]
-    panel = pl.BlockSpec((mine.shape[0], 1, 2) + mine.shape[3:], lambda s, p: (0, which, s, 0, 0))
+    panel = pl.BlockSpec((mine.shape[0], 2) + mine.shape[2:], lambda s, p: (0, s, 0, 0))
     return pl.pallas_call(
         update_kernel,
         out_shape=jax.ShapeDtypeStruct(start.shape, jnp.float32),
@@ -166,13 +166,13 @@
     )(jnp.full((1,), core, jnp.int32), start, factor, mine, other)
 
 
-def finish_kernel(at_ref, update_ref, panels_ref, mass_ref, solved_ref, blocks_ref):
+def finish_kernel(at_ref, update_ref, one_ref, two_ref, mass_ref, solved_ref, blocks_ref):
     rounds, own, k_all = solved_ref.shape
     lanes = lax.broadcasted_iota(jnp.int32, (own, BLOCK), 1)
     rows = lax.broadcasted_iota(jnp.int32, (own, BLOCK), 0)
     take = jnp.where(lanes == rows + at_ref[1] * own, 1.0, 0.0)
-    for which in range(2):
-        solved_ref[which] = small_dot(take, panels_ref[:, which, 0].reshape(k_all, BLOCK), 1, 1)
+    for which, ref in enumerate((one_ref, two_ref)):
+        solved_ref[which] = small_dot(take, ref[:, 0].reshape(k_all, BLOCK), 1, 1)
     solved_ref[2:] = update_ref[2 * own :, :].reshape(rounds - 2, own, k_all)
     all_rows = solved_ref[...].reshape(own * rounds, k_all)
     weighted = all_rows * mass_ref[...]
@@ -184,8 +184,9 @@
             at += 1
 
 
-def finish(updated, panels, mass, place, col, shape):
+def finish(updated, one, two, mass, place, col, shape):
     rounds, own, k_all = shape
+    panel = pl.BlockSpec((one.shape[0], 1) + one.shape[2:], lambda s, at: (0, at[0], 0, 0))
     count = len(block_pairs(k_all))
     return pl.pallas_call(
         finish_kernel,
@@ -198,7 +199,8 @@
             grid=(1,),
             in_specs=[
                 pl.BlockSpec(updated.shape, lambda s, at: (0, 0)),
-                pl.BlockSpec(panels.shape[:2] + (1,) + panels.shape[3:], lambda s, at: (0, 0, at[0], 0, 0)),
+                panel,
+                panel,
                 pl.BlockSpec((own * rounds, 1), lambda s, at: (0, 0)),
             ],
             out_specs=(
@@ -208,7 +210,7 @@
         ),
         compiler_params=pltpu.CompilerParams(vmem_limit_bytes=56 * 1024 * 1024),
         cost_estimate=pl.CostEstimate(flops=8 * updated.size * k_all, bytes_accessed=12 * updated.size, transcendentals=0),
-    )(jnp.stack([place, col]).astype(jnp.int32), updated, panels, mass.T.reshape(-1, 1))
+    )(jnp.stack([place, col]).astype(jnp.int32), updated, one, two, mass.T.reshape(-1, 1))
 
 
 def exchange(blocks, axis):
@@ -258,27 +260,40 @@
     )(rows, tiles, after)
 
 
-def halves_kernel(core_ref, one_ref, two_ref, after_ref, out_ref):
-    out_ref[0] = one_ref[:, 0]
-    out_ref[1] = two_ref[:, 0]
-
-
-def halves(one, two, core, after):
-    pairs = (one.shape[0] // 2, 2) + one.shape[1:]
-    half = pl.BlockSpec((pairs[0], 1) + pairs[2:], lambda s, p: (0, p[0], 0, 0))
-    shape = (2, pairs[0]) + pairs[2:]
-    return pl.pallas_call(
-        halves_kernel,
+def hold_kernel(block_ref, after_ref, out_ref):
+    out_ref[...] = block_ref[...]
+
+
+def hold(block, after):
+    return pl.pallas_call(
+        hold_kernel,
+        out_shape=jax.ShapeDtypeStruct(block.shape, block.dtype),
+        in_specs=[pl.BlockSpec(memory_space=pltpu.VMEM), pl.BlockSpec(memory_space=pl.ANY)],
+        out_specs=pl.BlockSpec(memory_space=pltpu.VMEM),
+        cost_estimate=pl.CostEstimate(flops=0, bytes_accessed=8 * block.size, transcendentals=0),
+    )(block, after)
+
+
+def half_kernel(core_ref, panel_ref, first_ref, second_ref, out_ref):
+    out_ref[...] = panel_ref[:, 0]
+
+
+def half(panel, core, first, second):
+    pairs = (panel.shape[0] // 2, 2) + panel.shape[1:]
+    shape = (pairs[0],) + pairs[2:]
+    after = pl.BlockSpec(memory_space=pl.ANY)
+    return pl.pallas_call(
+        half_kernel,
         out_shape=jax.ShapeDtypeStruct(shape, jnp.float32),
         grid_spec=pltpu.PrefetchScalarGridSpec(
             num_scalar_prefetch=1,
             grid=(1,),
-            in_specs=[half, half, pl.BlockSpec(memory_space=pl.ANY)],
-            out_specs=pl.BlockSpec(shape, lambda s, p: (0, 0, 0, 0)),
+            in_specs=[pl.BlockSpec((pairs[0], 1) + pairs[2:], lambda s, p: (0, p[0], 0, 0)), after, after],
+            out_specs=pl.BlockSpec(shape, lambda s, p: (0, 0, 0)),
         ),
         compiler_params=pltpu.CompilerParams(vmem_limit_bytes=56 * 1024 * 1024),
-        cost_estimate=pl.CostEstimate(flops=0, bytes_accessed=8 * one.size, transcendentals=0),
-    )(jnp.full((1,), core, jnp.int32), one.reshape(pairs), two.reshape(pairs), after)
+        cost_estimate=pl.CostEstimate(flops=0, bytes_accessed=4 * panel.size, transcendentals=0),
+    )(jnp.full((1,), core, jnp.int32), panel.reshape(pairs), first, second)
 
 
 def body(vectors, factor_one, factor_two, block_inverse, lumped_mass):
@@ -291,10 +306,10 @@
     swap = [(i, i ^ 1) for i in range(rows_n)]
     turn = [(r * cols_n + c, c * cols_n + r) for r in range(rows_n) for c in range(cols_n)]
 
-    mats = jnp.stack([factor_one[:, 0, :], block_inverse[1]])
-    mats = lax.all_gather(mats, "col")
-
-    turned = lax.ppermute(vectors[:, 0, :], ("row", "col"), turn)
+    stack = jnp.stack([factor_one[:, 0, :], block_inverse[1]])
+    mats = lax.all_gather(stack, "col")
+
+    turned = lax.ppermute(hold(vectors[:, 0, :], stack), ("row", "col"), turn)
     block = gather_row(turned).reshape(tile, k_all)
     parts = jnp.einsum("qk,iq->ki", block, block_inverse[0], precision=HIGHEST, preferred_element_type=jnp.float32)
     head = vectors[:, 1, :].reshape(own, cols_n, k_part).transpose(1, 0, 2).reshape(cols_n, -1, BLOCK)
@@ -316,13 +331,15 @@
     remain_head = head - product(one_rows, mats, 0, one_rows)
     remain_rows = gather_row(remain_head)
     two_rows = gather_row(product(remain_rows, mats, 1, f_one))
-    mine = lax.all_gather(halves(one_rows, two_rows, core, f_two), "col")
-    other = lax.ppermute(mine, "row", swap)
+    one_mine = lax.all_gather(half(one_rows, core, one_rows, one_rows), "col")
+    two_mine = share(half(two_rows, core, f_two, one_mine), "col")
+    mine = (one_mine, two_mine)
+    other = [lax.ppermute(panel, "row", swap) for panel in mine]
 
     done = vectors.transpose(1, 0, 2).reshape(-1, k_all)
     for which, factor in enumerate((f_one, f_two)):
-        done = update(done, factor, mine, other, which, core)
-    solved, blocks = finish(done, mine, lumped_mass, row // 2, col, (rounds, own, k_all))
+        done = update(done, factor, mine[which], other[which], core)
+    solved, blocks = finish(done, one_mine, two_mine, lumped_mass, row // 2, col, (rounds, own, k_all))
     solved = solved.transpose(1, 0, 2)
 
     blocks = blocks.reshape((2, -1, BLOCK))

time: 345 us -> 334 us (0.968)
  waiting for transfers between devices: 133 us -> 107 us
  starting transfers between devices: 88.3 us -> 98.9 us
    all_gather x2, waiting for transfers between devices: 77.2 us -> 32.9 us  [the longest x1 19 us: body(): one_mine = lax.all_gather(half(one_rows, core, one_rows, one_rows), 'col')]
    all_to_all x3 -> x4, waiting for transfers between devices: 13.2 us -> 34.3 us  [exchange(): return lax.all_to_all(blocks, axis, 0, 0)]
    ppermute x1 -> x3, starting transfers between devices: 4.51 us -> 10.2 us  [the longest x2 5.72 us: body(): other = [lax.ppermute(panel, 'row', swap) for panel in mine]]
    ppermute x16, starting transfers between devices: 48.9 us -> 53 us  [gather_row(): got = lax.ppermute(block, 'row', [(i, i ^ step) for i in range(size)])]
    all_to_all x3 -> x4, starting transfers between devices: 18.6 us -> 20.9 us  [exchange(): return lax.all_to_all(blocks, axis, 0, 0)]
  transfers between devices with their start and end apart: 28 -> 30, of which waited for: 24 -> 25; matrix products, arithmetic and copies ran while one was open for 6% -> 6% of each run, Pallas kernels for 2% -> 5%
where the time goes in v7:
time: 334 us; the launch traced here: 333 us
  waiting for transfers between devices  107 us (32%)
  starting transfers between devices  98.9 us (30%)
  Pallas kernels  58.8 us (18%)
  blocking collectives  22.4 us (7%)
  local copies, waits for them, and re-layouts  20.3 us (6%)
  between operations  14.4 us (4%)
  other arithmetic  7.9 us (2%)
  matrix products  3.56 us (1%)
    ppermute x16, starting transfers between devices, gather_row(): got = lax.ppermute(block, 'row', [(i, i ^ step) for i in range(size)])  53 us
    all_to_all x4, waiting for transfers between devices, exchange(): return lax.all_to_all(blocks, axis, 0, 0)  34.3 us
    ppermute x16, waiting for transfers between devices, gather_row(): got = lax.ppermute(block, 'row', [(i, i ^ step) for i in range(size)])  32.1 us
    pallas_call x1, Pallas kernels, inverse_factor(): pl.pallas_call(functools.partial(inverse_kernel, scale), out_shape=jax.Sh...  26.8 us
    all_to_all x2, blocking collectives, exchange(): return lax.all_to_all(blocks, axis, 0, 0)  22.4 us
    all_to_all x4, starting transfers between devices, exchange(): return lax.all_to_all(blocks, axis, 0, 0)  20.9 us
    all_gather x1, waiting for transfers between devices, body(): one_mine = lax.all_gather(half(one_rows, core, one_rows, one_rows), 'col')  19 us
    pallas_call x2, Pallas kernels, update(): pl.pallas_call(update_kernel, out_shape=jax.ShapeDtypeStruct(start.shape,...  16.6 us
  transfers between devices with their start and end apart: 30, of which 25 were waited for; matrix products, arithmetic and copies ran while one was open for 6% of the time, Pallas kernels for 5%

profile of v7, /device:TPU:1, one launch (start us, length us, event | category | flops | bytes accessed | tf_op | source)
XLA Modules:
  0.0 333.1 jit_solution(8452553945785566893)
XLA Ops:
  12.7 4.5 %collective-permute-start = (f32[8,512]{1,0:T(8,128)}, f32[8,512]{1,0:T(8,128)S(1)}, u32[]{:S(2)}, u32[]{:S(2)}) collective-permute-start(f32[8,512]{1,0:T(8,128)} %shard_map.68), channel_id=1, source_target_pairs={{0,0},{1,16},{2,32},{3,48},{4,64},{5,80},{6,96},{7,112},{8,128},{9... | collective-permute-start | bytes 49160 | tf_op jit(solution)/shard_map/ppermute | solution.py:312
  18.8 14.2 %collective-permute-start.1 = (f32[8,512]{1,0:T(8,128)S(1)}, f32[8,512]{1,0:T(8,128)S(1)}, u32[]{:S(2)}, u32[]{:S(2)}) collective-permute-start(f32[8,512]{1,0:T(8,128)S(1)} %collective-permute-done), channel_id=1, source_target_pairs={{0,128},{16,144},{32,160},{48,176},{64,192},{80,208},{96,224},{112... | collective-permute-start | bytes 49160 | tf_op jit(solution)/shard_map/ppermute | solution.py:230
  41.1 4.1 %collective-permute-start.4 = (f32[2,2,2,8,512]{4,3,0,1,2:T(8,128)S(1)}, f32[2,2,2,8,512]{4,3,0,1,2:T(8,128)S(1)}, u32[]{:S(2)}, u32[]{:S(2)}) collective-permute-start(f32[2,2,2,8,512]{4,3,0,1,2:T(8,128)S(1)} %pad_maximum_fusion.6), channel_id=1, source_target_pairs={{0,16},{16,0},{32,48},{48,32},{64,80},{80,64},{96,112},{112,96},{1... | collective-permute-start | bytes 393224 | tf_op jit(solution)/shard_map/ppermute | solution.py:230
  48.4 7.0 %all-to-all-start.1 = ((f32[16,40,128]{2,1,0:T(8,128)}), f32[16,40,128]{2,1,0:T(8,128)S(1)}, u32[]{:S(2)}, u32[]{:S(2)}) async-start(f32[16,40,128]{2,1,0:T(8,128)} %select_maximum_fusion), calls=%async_computation.1 | async-start | bytes 655360 | tf_op jit(solution)/shard_map/all_to_all | solution.py:217
  59.2 5.1 %all-to-all-done.1 = f32[16,40,128]{2,1,0:T(8,128)S(1)} async-done(((f32[16,40,128]{2,1,0:T(8,128)}), f32[16,40,128]{2,1,0:T(8,128)S(1)}, u32[]{:S(2)}, u32[]{:S(2)}) %all-to-all-start.1) | async-done | bytes 327712 | tf_op jit(solution)/shard_map/all_to_all | solution.py:217
  64.2 4.5 %all-to-all-start = ((f32[16,47,8,128]{3,2,1,0:T(8,128)}), f32[16,47,8,128]{3,2,1,0:T(8,128)}, u32[]{:S(2)}, u32[]{:S(2)}) async-start(f32[16,47,8,128]{3,2,1,0:T(8,128)} %copy_bitcast_fusion), calls=%async_computation | async-start | bytes 6160384 | tf_op jit(solution)/shard_map/all_to_all | solution.py:217
  68.8 3.9 %collective-permute-start.5 = (f32[32,128]{1,0:T(8,128)S(1)}, f32[32,128]{1,0:T(8,128)S(1)}, u32[]{:S(2)}, u32[]{:S(2)}) collective-permute-start(f32[32,128]{1,0:T(8,128)S(1)} %slice_reduce_fusion), channel_id=1, source_target_pairs={{0,128},{16,144},{32,160},{48,176},{64,192},{80,208},{96,224},{112... | collective-permute-start | bytes 49160 | tf_op jit(solution)/shard_map/ppermute | solution.py:230
  84.4 3.8 %collective-permute-start.8 = (f32[2,2,2,32,128]{4,3,0,1,2:T(8,128)}, f32[2,2,2,32,128]{4,3,0,1,2:T(8,128)}, u32[]{:S(2)}, u32[]{:S(2)}) collective-permute-start(f32[2,2,2,32,128]{4,3,0,1,2:T(8,128)} %pad_maximum_fusion.7), channel_id=1, source_target_pairs={{0,16},{16,0},{32,48},{48,32},{64,80},{80,64},{96,112},{112,96},{1... | collective-permute-start | bytes 393224 | tf_op jit(solution)/shard_map/ppermute | solution.py:230
  93.7 13.9 %all-gather.7.cloned.1.call-done = f32[32,128,128]{2,1,0:T(8,128)} async-done(((f32[2,128,128]{2,1,0:T(8,128)}), f32[32,128,128]{2,1,0:T(8,128)}) %all-gather.7.cloned.1.call-update) | async-done | bytes 2097168 | tf_op jit(solution)/shard_map/all_gather | solution.py:310
  111.3 4.8 %collective-permute-start.10 = (f32[32,128]{1,0:T(8,128)S(1)}, f32[32,128]{1,0:T(8,128)S(1)}, u32[]{:S(2)}, u32[]{:S(2)}) collective-permute-start(f32[32,128]{1,0:T(8,128)S(1)} %sub.11), channel_id=1, source_target_pairs={{0,128},{16,144},{32,160},{48,176},{64,192},{80,208},{96,224},{112... | collective-permute-start | bytes 49160 | tf_op jit(solution)/shard_map/ppermute | solution.py:230
  123.0 4.5 %all-to-all-start.2 = ((f32[16,46,8,128]{3,2,1,0:T(8,128)}), f32[16,46,8,128]{3,2,1,0:T(8,128)}, u32[]{:S(2)}, u32[]{:S(2)}) async-start(f32[16,46,8,128]{3,2,1,0:T(8,128)} %copy_bitcast_fusion.1), calls=%async_computation.2 | async-start | bytes 6029312 | tf_op jit(solution)/shard_map/all_to_all | solution.py:217
  148.8 3.9 %collective-permute-done.15 = f32[2,32,128]{2,1,0:T(8,128)S(1)} collective-permute-done((f32[2,32,128]{2,1,0:T(8,128)S(1)}, f32[2,32,128]{2,1,0:T(8,128)S(1)}, u32[]{:S(2)}, u32[]{:S(2)}) %collective-permute-start.15) | collective-permute-done | bytes 32800 | tf_op jit(solution)/shard_map/ppermute | solution.py:230
  164.5 19.0 %all-gather.5.cloned.1.call-done = f32[128,32,128]{2,1,0:T(8,128)} async-done(((f32[8,32,128]{2,1,0:T(8,128)}), f32[128,32,128]{2,1,0:T(8,128)}) %all-gather.5.cloned.1.call-update) | async-done | bytes 2097168 | tf_op jit(solution)/shard_map/all_gather | solution.py:334
  187.6 4.8 %all-to-all-start.3 = ((f32[16,8,32,128]{3,2,1,0:T(8,128)}), f32[16,8,32,128]{3,2,1,0:T(8,128)}, u32[]{:S(2)}, u32[]{:S(2)}) async-start(f32[16,8,32,128]{3,2,1,0:T(8,128)} %broadcast_in_dim.7), calls=%async_computation.3 | async-start | bytes 4194304 | tf_op jit(solution)/shard_map/all_to_all | solution.py:217
  194.3 26.0 %all-to-all-done.3.mine_ref.two_ref = f32[16,8,32,128]{3,2,1,0:T(8,128)} async-done(((f32[16,8,32,128]{3,2,1,0:T(8,128)}), f32[16,8,32,128]{3,2,1,0:T(8,128)}, u32[]{:S(2)}, u32[]{:S(2)}) %all-to-all-start.3) | async-done | bytes 2097184 | tf_op jit(solution)/shard_map/all_to_all | solution.py:217
  220.3 3.8 %collective-permute-start.18 = (f32[16,8,32,128]{3,2,1,0:T(8,128)}, f32[16,8,32,128]{3,2,1,0:T(8,128)}, u32[]{:S(2)}, u32[]{:S(2)}) collective-permute-start(f32[16,8,32,128]{3,2,1,0:T(8,128)} %all-to-all-done.3.mine_ref.two_ref), channel_id=1, source_target_pairs={{0,16},{16,0},{32,48},{48,32},{64,80},{80,64},{96,112},{112,96},{1... | collective-permute-start | bytes 6291464 | tf_op jit(solution)/shard_map/ppermute | solution.py:337
  228.2 8.4 %shard_map.70.start_ref = f32[384,512]{1,0:T(8,128)} custom-call(s32[1]{0:T(128)} %bitcast.2.core_ref, f32[384,512]{1,0:T(8,128)} %bitcast.140, f32[8,2,47,8,128]{4,3,2,1,0:T(8,128)} %bitcast.7.factor_ref.after_ref, f32[16,8,32,128]{3,2,1,0:T(8,128)} %bitcast.126, f32[16,8,32,128]{3,2,1,0:T(8,128)} %collective-permute-done.9.other_ref), custom_call_target="tpu_custom_call" | custom-call | flops 4831838208 | bytes 4718592 | tf_op jit(solution)/shard_map/pallas_call | solution.py:148
  236.6 8.2 %shard_map.74.update_ref = f32[384,512]{1,0:T(8,128)} custom-call(s32[1]{0:T(128)} %bitcast.2.core_ref, f32[384,512]{1,0:T(8,128)} %shard_map.70.start_ref, f32[8,2,46,8,128]{4,3,2,1,0:T(8,128)} %bitcast.40.first_ref.factor_ref, f32[16,8,32,128]{3,2,1,0:T(8,128)} %all-to-all-done.3.mine_ref.two_ref, f32[16,8,32,128]{3,2,1,0:T(8,128)} %collective-permute-done.18.other_ref), custom_call_target="tpu_custom_call" | custom-call | flops 4831838208 | bytes 4718592 | tf_op jit(solution)/shard_map/pallas_call | solution.py:148
  244.8 4.8 %shard_map.75 = (f32[48,8,512]{2,1,0:T(8,128)}, f32[10,128,128]{2,1,0:T(8,128)}) custom-call(s32[2]{0:T(128)} %pad_add_fusion.at_ref, f32[384,512]{1,0:T(8,128)} %shard_map.74.update_ref, f32[16,8,32,128]{3,2,1,0:T(8,128)} %bitcast.127, f32[16,8,32,128]{3,2,1,0:T(8,128)} %all-to-all-done.3.mine_ref.two_ref, f32[384,1]{1,0:T(8,128)} %reshape.76.mass_ref), custom_call_target="tpu_custom_call" | custom-call | flops 805306368 | bytes 2359296 | tf_op jit(solution)/shard_map/pallas_call | solution.py:191
  254.2 11.6 %all_to_all.30 = f32[16,40,128]{2,1,0:T(8,128)S(1)} all-to-all(f32[16,40,128]{2,1,0:T(8,128)S(1)} %bitcast.132), channel_id=1, replica_groups=mesh['row'=16,'col'=16] {'col'}, dimensions={0} | all-to-all | bytes 655360 | tf_op jit(solution)/shard_map/all_to_all | solution.py:217
  272.4 5.4 %collective-permute-start.22 = (f32[40,128]{1,0:T(8,128)S(1)}, f32[40,128]{1,0:T(8,128)S(1)}, u32[]{:S(2)}, u32[]{:S(2)}) collective-permute-start(f32[40,128]{1,0:T(8,128)S(1)} %add.32), channel_id=1, source_target_pairs={{0,128},{16,144},{32,160},{48,176},{64,192},{80,208},{96,224},{112... | collective-permute-start | bytes 61448 | tf_op jit(solution)/shard_map/ppermute | solution.py:351
  279.0 10.9 %all_to_all.31 = f32[16,40,128]{2,1,0:T(8,128)S(1)} all-to-all(f32[16,40,128]{2,1,0:T(8,128)S(1)} %broadcast_in_dim.8), channel_id=1, replica_groups=mesh['row'=16,'col'=16] {'col'}, dimensions={0} | all-to-all | bytes 655360 | tf_op jit(solution)/shard_map/all_to_all | solution.py:217
  289.9 5.5 %collective-permute-start.23 = (f32[5,128,128]{2,1,0:T(8,128)S(1)}, f32[5,128,128]{2,1,0:T(8,128)S(1)}, u32[]{:S(2)}, u32[]{:S(2)}) collective-permute-start(f32[5,128,128]{2,1,0:T(8,128)S(1)} %bitcast.120), channel_id=1, source_target_pairs={{0,16},{16,0},{32,48},{48,32},{64,80},{80,64},{96,112},{112,96},{1... | collective-permute-start | bytes 983048 | tf_op jit(solution)/shard_map/ppermute | solution.py:354
  297.0 26.8 %shard_map.76 = f32[512,512]{1,0:T(8,128)S(1)} custom-call(s32[1]{0:T(128)} %bitcast.2.core_ref, f32[5,128,128]{2,1,0:T(8,128)S(1)} %bitcast.121, f32[5,128,128]{2,1,0:T(8,128)S(1)} %collective-permute-done.23.other_ref), custom_call_target="tpu_custom_call" | custom-call | tf_op jit(solution)/shard_map/pallas_call | solution.py:115
  (127 shorter events, 109.2 us)
Async XLA Ops:
  7.2 100.4 %all-gather.7.cloned.1.call-start = ((), (), s32[]{:S(2)}) async-start(), calls=%async_computation.7 | async-start | bytes 2228224 | tf_op jit(solution)/shard_map/all_gather | solution.py:310
  12.7 6.1 %collective-permute-start = (f32[8,512]{1,0:T(8,128)}, f32[8,512]{1,0:T(8,128)S(1)}, u32[]{:S(2)}, u32[]{:S(2)}) collective-permute-start(f32[8,512]{1,0:T(8,128)} %shard_map.68), channel_id=1, source_target_pairs={{0,0},{1,16},{2,32},{3,48},{4,64},{5,80},{6,96},{7,112},{8,128},{9... | collective-permute-start | bytes 49160 | tf_op jit(solution)/shard_map/ppermute | solution.py:312
  18.8 15.3 %collective-permute-start.1 = (f32[8,512]{1,0:T(8,128)S(1)}, f32[8,512]{1,0:T(8,128)S(1)}, u32[]{:S(2)}, u32[]{:S(2)}) collective-permute-start(f32[8,512]{1,0:T(8,128)S(1)} %collective-permute-done), channel_id=1, source_target_pairs={{0,128},{16,144},{32,160},{48,176},{64,192},{80,208},{96,224},{112... | collective-permute-start | bytes 49160 | tf_op jit(solution)/shard_map/ppermute | solution.py:230
  41.1 5.1 %collective-permute-start.4 = (f32[2,2,2,8,512]{4,3,0,1,2:T(8,128)S(1)}, f32[2,2,2,8,512]{4,3,0,1,2:T(8,128)S(1)}, u32[]{:S(2)}, u32[]{:S(2)}) collective-permute-start(f32[2,2,2,8,512]{4,3,0,1,2:T(8,128)S(1)} %pad_maximum_fusion.6), channel_id=1, source_target_pairs={{0,16},{16,0},{32,48},{48,32},{64,80},{80,64},{96,112},{112,96},{1... | collective-permute-start | bytes 393224 | tf_op jit(solution)/shard_map/ppermute | solution.py:230
  48.4 15.9 %all-to-all-start.1 = ((f32[16,40,128]{2,1,0:T(8,128)}), f32[16,40,128]{2,1,0:T(8,128)S(1)}, u32[]{:S(2)}, u32[]{:S(2)}) async-start(f32[16,40,128]{2,1,0:T(8,128)} %select_maximum_fusion), calls=%async_computation.1 | async-start | bytes 655360 | tf_op jit(solution)/shard_map/all_to_all | solution.py:217
  64.2 58.8 %all-to-all-start = ((f32[16,47,8,128]{3,2,1,0:T(8,128)}), f32[16,47,8,128]{3,2,1,0:T(8,128)}, u32[]{:S(2)}, u32[]{:S(2)}) async-start(f32[16,47,8,128]{3,2,1,0:T(8,128)} %copy_bitcast_fusion), calls=%async_computation | async-start | bytes 6160384 | tf_op jit(solution)/shard_map/all_to_all | solution.py:217
  68.7 114.8 %all-gather.5.cloned.1.call-start = ((), (), s32[]{:S(2)}) async-start(), calls=%async_computation.6 | async-start | bytes 2228224 | tf_op jit(solution)/shard_map/all_gather | solution.py:334
  68.8 6.6 %collective-permute-start.5 = (f32[32,128]{1,0:T(8,128)S(1)}, f32[32,128]{1,0:T(8,128)S(1)}, u32[]{:S(2)}, u32[]{:S(2)}) collective-permute-start(f32[32,128]{1,0:T(8,128)S(1)} %slice_reduce_fusion), channel_id=1, source_target_pairs={{0,128},{16,144},{32,160},{48,176},{64,192},{80,208},{96,224},{112... | collective-permute-start | bytes 49160 | tf_op jit(solution)/shard_map/ppermute | solution.py:230
  75.4 4.6 %collective-permute-start.6 = (f32[2,32,128]{2,1,0:T(8,128)S(1)}, f32[2,32,128]{2,1,0:T(8,128)S(1)}, u32[]{:S(2)}, u32[]{:S(2)}) collective-permute-start(f32[2,32,128]{2,1,0:T(8,128)S(1)} %pad_maximum_fusion.15), channel_id=1, source_target_pairs={{0,64},{16,80},{32,96},{48,112},{64,0},{80,16},{96,32},{112,48},{1... | collective-permute-start | bytes 98312 | tf_op jit(solution)/shard_map/ppermute | solution.py:230
  84.4 5.1 %collective-permute-start.8 = (f32[2,2,2,32,128]{4,3,0,1,2:T(8,128)}, f32[2,2,2,32,128]{4,3,0,1,2:T(8,128)}, u32[]{:S(2)}, u32[]{:S(2)}) collective-permute-start(f32[2,2,2,32,128]{4,3,0,1,2:T(8,128)} %pad_maximum_fusion.7), channel_id=1, source_target_pairs={{0,16},{16,0},{32,48},{48,32},{64,80},{80,64},{96,112},{112,96},{1... | collective-permute-start | bytes 393224 | tf_op jit(solution)/shard_map/ppermute | solution.py:230
  111.3 6.5 %collective-permute-start.10 = (f32[32,128]{1,0:T(8,128)S(1)}, f32[32,128]{1,0:T(8,128)S(1)}, u32[]{:S(2)}, u32[]{:S(2)}) collective-permute-start(f32[32,128]{1,0:T(8,128)S(1)} %sub.11), channel_id=1, source_target_pairs={{0,128},{16,144},{32,160},{48,176},{64,192},{80,208},{96,224},{112... | collective-permute-start | bytes 49160 | tf_op jit(solution)/shard_map/ppermute | solution.py:230
  117.8 9.7 %collective-permute-start.11 = (f32[2,32,128]{2,1,0:T(8,128)S(1)}, f32[2,32,128]{2,1,0:T(8,128)S(1)}, u32[]{:S(2)}, u32[]{:S(2)}) collective-permute-start(f32[2,32,128]{2,1,0:T(8,128)S(1)} %pad_maximum_fusion.16), channel_id=1, source_target_pairs={{0,64},{16,80},{32,96},{48,112},{64,0},{80,16},{96,32},{112,48},{1... | collective-permute-start | bytes 98312 | tf_op jit(solution)/shard_map/ppermute | solution.py:230
  123.0 41.5 %all-to-all-start.2 = ((f32[16,46,8,128]{3,2,1,0:T(8,128)}), f32[16,46,8,128]{3,2,1,0:T(8,128)}, u32[]{:S(2)}, u32[]{:S(2)}) async-start(f32[16,46,8,128]{3,2,1,0:T(8,128)} %copy_bitcast_fusion.1), calls=%async_computation.2 | async-start | bytes 6029312 | tf_op jit(solution)/shard_map/all_to_all | solution.py:217
  127.6 5.5 %collective-permute-start.12 = (f32[2,2,32,128]{3,2,0,1:T(8,128)S(1)}, f32[2,2,32,128]{3,2,0,1:T(8,128)S(1)}, u32[]{:S(2)}, u32[]{:S(2)}) collective-permute-start(f32[2,2,32,128]{3,2,0,1:T(8,128)S(1)} %pad_maximum_fusion.12), channel_id=1, source_target_pairs={{0,32},{16,48},{32,0},{48,16},{64,96},{80,112},{96,64},{112,80},{1... | collective-permute-start | bytes 196616 | tf_op jit(solution)/shard_map/ppermute | solution.py:230
  133.1 4.2 %collective-permute-start.13 = (f32[2,2,2,32,128]{4,3,0,1,2:T(8,128)S(1)}, f32[2,2,2,32,128]{4,3,0,1,2:T(8,128)S(1)}, u32[]{:S(2)}, u32[]{:S(2)}) collective-permute-start(f32[2,2,2,32,128]{4,3,0,1,2:T(8,128)S(1)} %pad_maximum_fusion.8), channel_id=1, source_target_pairs={{0,16},{16,0},{32,48},{48,32},{64,80},{80,64},{96,112},{112,96},{1... | collective-permute-start | bytes 393224 | tf_op jit(solution)/shard_map/ppermute | solution.py:230
  141.1 6.8 %collective-permute-start.14 = (f32[32,128]{1,0:T(8,128)}, f32[32,128]{1,0:T(8,128)S(1)}, u32[]{:S(2)}, u32[]{:S(2)}) collective-permute-start(f32[32,128]{1,0:T(8,128)} %shard_map.72), channel_id=1, source_target_pairs={{0,128},{16,144},{32,160},{48,176},{64,192},{80,208},{96,224},{112... | collective-permute-start | bytes 49160 | tf_op jit(solution)/shard_map/ppermute | solution.py:230
  148.6 4.1 %collective-permute-start.15 = (f32[2,32,128]{2,1,0:T(8,128)S(1)}, f32[2,32,128]{2,1,0:T(8,128)S(1)}, u32[]{:S(2)}, u32[]{:S(2)}) collective-permute-start(f32[2,32,128]{2,1,0:T(8,128)S(1)} %pad_maximum_fusion.17), channel_id=1, source_target_pairs={{0,64},{16,80},{32,96},{48,112},{64,0},{80,16},{96,32},{112,48},{1... | collective-permute-start | bytes 98312 | tf_op jit(solution)/shard_map/ppermute | solution.py:230
  152.7 3.8 %collective-permute-start.16 = (f32[2,2,32,128]{3,2,0,1:T(8,128)S(1)}, f32[2,2,32,128]{3,2,0,1:T(8,128)S(1)}, u32[]{:S(2)}, u32[]{:S(2)}) collective-permute-start(f32[2,2,32,128]{3,2,0,1:T(8,128)S(1)} %pad_maximum_fusion.13), channel_id=1, source_target_pairs={{0,32},{16,48},{32,0},{48,16},{64,96},{80,112},{96,64},{112,80},{1... | collective-permute-start | bytes 196616 | tf_op jit(solution)/shard_map/ppermute | solution.py:230
  156.5 4.0 %collective-permute-start.17 = (f32[2,2,2,32,128]{4,3,0,1,2:T(8,128)S(1)}, f32[2,2,2,32,128]{4,3,0,1,2:T(8,128)S(1)}, u32[]{:S(2)}, u32[]{:S(2)}) collective-permute-start(f32[2,2,2,32,128]{4,3,0,1,2:T(8,128)S(1)} %pad_maximum_fusion.9), channel_id=1, source_target_pairs={{0,16},{16,0},{32,48},{48,32},{64,80},{80,64},{96,112},{112,96},{1... | collective-permute-start | bytes 393224 | tf_op jit(solution)/shard_map/ppermute | solution.py:230
  187.6 32.7 %all-to-all-start.3 = ((f32[16,8,32,128]{3,2,1,0:T(8,128)}), f32[16,8,32,128]{3,2,1,0:T(8,128)}, u32[]{:S(2)}, u32[]{:S(2)}) async-start(f32[16,8,32,128]{3,2,1,0:T(8,128)} %broadcast_in_dim.7), calls=%async_computation.3 | async-start | bytes 4194304 | tf_op jit(solution)/shard_map/all_to_all | solution.py:217
  192.5 35.7 %collective-permute-start.9 = (f32[16,8,32,128]{3,2,1,0:T(8,128)}, f32[16,8,32,128]{3,2,1,0:T(8,128)}, u32[]{:S(2)}, u32[]{:S(2)}) collective-permute-start(f32[16,8,32,128]{3,2,1,0:T(8,128)} %bitcast.125), channel_id=1, source_target_pairs={{0,16},{16,0},{32,48},{48,32},{64,80},{80,64},{96,112},{112,96},{1... | collective-permute-start | bytes 6291464 | tf_op jit(solution)/shard_map/ppermute | solution.py:337
  220.3 16.2 %collective-permute-start.18 = (f32[16,8,32,128]{3,2,1,0:T(8,128)}, f32[16,8,32,128]{3,2,1,0:T(8,128)}, u32[]{:S(2)}, u32[]{:S(2)}) collective-permute-start(f32[16,8,32,128]{3,2,1,0:T(8,128)} %all-to-all-done.3.mine_ref.two_ref), channel_id=1, source_target_pairs={{0,16},{16,0},{32,48},{48,32},{64,80},{80,64},{96,112},{112,96},{1... | collective-permute-start | bytes 6291464 | tf_op jit(solution)/shard_map/ppermute | solution.py:337
  272.4 6.6 %collective-permute-start.22 = (f32[40,128]{1,0:T(8,128)S(1)}, f32[40,128]{1,0:T(8,128)S(1)}, u32[]{:S(2)}, u32[]{:S(2)}) collective-permute-start(f32[40,128]{1,0:T(8,128)S(1)} %add.32), channel_id=1, source_target_pairs={{0,128},{16,144},{32,160},{48,176},{64,192},{80,208},{96,224},{112... | collective-permute-start | bytes 61448 | tf_op jit(solution)/shard_map/ppermute | solution.py:351
  289.9 7.1 %collective-permute-start.23 = (f32[5,128,128]{2,1,0:T(8,128)S(1)}, f32[5,128,128]{2,1,0:T(8,128)S(1)}, u32[]{:S(2)}, u32[]{:S(2)}) collective-permute-start(f32[5,128,128]{2,1,0:T(8,128)S(1)} %bitcast.120), channel_id=1, source_target_pairs={{0,16},{16,0},{32,48},{48,32},{64,80},{80,64},{96,112},{112,96},{1... | collective-permute-start | bytes 983048 | tf_op jit(solution)/shard_map/ppermute | solution.py:354
  (9 other events, 201.2 us)
Sparse Core Ops, SparseCore 0:
  33.1 74.4 all-gather.6
  110.0 73.4 all-gather.4

commit v8 on v7

--- a/solution.py
+++ b/solution.py
@@ -74,7 +74,7 @@
     return [(i, j) for i in range(n // BLOCK) for j in range(i, n // BLOCK)]
 
 
-def inverse_kernel(scale, core_ref, mine_ref, other_ref, out_ref, a_ref, s_ref, t_ref):
+def inverse_kernel(scale, core_ref, mine_ref, other_ref, out_ref, a_ref, s_ref, t_ref, u_ref):
     n = out_ref.shape[0]
     pairs = block_pairs(n)
     half = len(pairs) // 2
@@ -97,10 +97,11 @@
         u = small_dot(inv, jnp.where(below, a_ref[rows, :], 0.0), 1, 0)
         x = small_dot(inv, out_ref[rows, :], 1, 0)
         out_ref[rows, :] = x
+        u_ref[...] = u
 
         def rest(i, _):
             later = pl.ds(pl.multiple_of(i * BLOCK, BLOCK), BLOCK)
-            ui = small_dot(inv, a_ref[rows, later], 1, 0)
+            ui = u_ref[:, later]
             a_ref[later, :] = a_ref[later, :] - small_dot(ui, u, 0, 0)
             out_ref[later, :] = out_ref[later, :] - small_dot(ui, x, 0, 0)
             return 0
@@ -121,6 +122,7 @@
             pltpu.VMEM((n, n), jnp.float32),
             pltpu.VMEM((BLOCK, BLOCK), jnp.float32),
             pltpu.VMEM((BLOCK, BLOCK), jnp.float32),
+            pltpu.VMEM((BLOCK, n), jnp.float32),
         ],
         compiler_params=pltpu.CompilerParams(vmem_limit_bytes=16 * 1024 * 1024),
     )(jnp.full((1,), core, jnp.int32), mine, other)
@@ -274,26 +276,40 @@
     )(block, after)
 
 
-def half_kernel(core_ref, panel_ref, first_ref, second_ref, out_ref):
+def keep_kernel(block_ref, after_ref, out_ref):
+    pass
+
+
+def keep(block, after):
+    return pl.pallas_call(
+        keep_kernel,
+        out_shape=jax.ShapeDtypeStruct(block.shape, block.dtype),
+        in_specs=[pl.BlockSpec(memory_space=pl.ANY)] * 2,
+        out_specs=pl.BlockSpec(memory_space=pl.ANY),
+        input_output_aliases={0: 0},
+        compiler_params=pltpu.CompilerParams(vmem_limit_bytes=56 * 1024 * 1024),
+    )(block, after)
+
+
+def half_kernel(core_ref, panel_ref, after_ref, out_ref):
     out_ref[...] = panel_ref[:, 0]
 
 
-def half(panel, core, first, second):
+def half(panel, core, after):
     pairs = (panel.shape[0] // 2, 2) + panel.shape[1:]
     shape = (pairs[0],) + pairs[2:]
-    after = pl.BlockSpec(memory_space=pl.ANY)
     return pl.pallas_call(
         half_kernel,
         out_shape=jax.ShapeDtypeStruct(shape, jnp.float32),
         grid_spec=pltpu.PrefetchScalarGridSpec(
             num_scalar_prefetch=1,
             grid=(1,),
-            in_specs=[pl.BlockSpec((pairs[0], 1) + pairs[2:], lambda s, p: (0, p[0], 0, 0)), after, after],
+            in_specs=[pl.BlockSpec((pairs[0], 1) + pairs[2:], lambda s, p: (0, p[0], 0, 0)), pl.BlockSpec(memory_space=pl.ANY)],
             out_specs=pl.BlockSpec(shape, lambda s, p: (0, 0, 0)),
         ),
         compiler_params=pltpu.CompilerParams(vmem_limit_bytes=56 * 1024 * 1024),
         cost_estimate=pl.CostEstimate(flops=0, bytes_accessed=4 * panel.size, transcendentals=0),
-    )(jnp.full((1,), core, jnp.int32), panel.reshape(pairs), first, second)
+    )(jnp.full((1,), core, jnp.int32), panel.reshape(pairs), after)
 
 
 def body(vectors, factor_one, factor_two, block_inverse, lumped_mass):
@@ -325,20 +341,20 @@
         parts = exchange(parts, "col")
         return parts.reshape((rows_n // 2, 2) + parts.shape[1:])
 
-    one_rows = gather_row(one)
+    one_rows = gather_row(hold(one, mats))
     f_one = redistribute(factor_one)
     f_two = redistribute(factor_two)
     remain_head = head - product(one_rows, mats, 0, one_rows)
     remain_rows = gather_row(remain_head)
     two_rows = gather_row(product(remain_rows, mats, 1, f_one))
-    one_mine = lax.all_gather(half(one_rows, core, one_rows, one_rows), "col")
-    two_mine = share(half(two_rows, core, f_two, one_mine), "col")
-    mine = (one_mine, two_mine)
-    other = [lax.ppermute(panel, "row", swap) for panel in mine]
-
+    one_mine = lax.all_gather(half(one_rows, core, one_rows), "col")
+    two_half = half(two_rows, core, f_two)
+    one_mine = keep(one_mine, two_half)
+    two_mine = share(two_half, "col")
     done = vectors.transpose(1, 0, 2).reshape(-1, k_all)
-    for which, factor in enumerate((f_one, f_two)):
-        done = update(done, factor, mine[which], other[which], core)
+    done = update(done, f_one, one_mine, lax.ppermute(one_mine, "row", swap), core)
+    two_mine = keep(two_mine, done)
+    done = update(done, f_two, two_mine, lax.ppermute(two_mine, "row", swap), core)
     solved, blocks = finish(done, one_mine, two_mine, lumped_mass, row // 2, col, (rounds, own, k_all))
     solved = solved.transpose(1, 0, 2)
 

time: 334 us -> 313 us (0.937)
  waiting for transfers between devices: 107 us -> 90.6 us
  starting transfers between devices: 98.9 us -> 93.5 us
    all_gather x1, waiting for transfers between devices: 13.9 us -> 0.01 us  [body(): mats = lax.all_gather(stack, 'col')]
    all_gather x1, waiting for transfers between devices: 19 us -> 6.61 us  [body(): one_mine = lax.all_gather(half(one_rows, core, one_rows), 'col')]
    all_to_all x4, waiting for transfers between devices: 34.3 us -> 39.2 us  [exchange(): return lax.all_to_all(blocks, axis, 0, 0)]
    ppermute x2, starting transfers between devices: 5.72 us -> 1.97 us  [the longest x1 1.17 us: body(): lax.ppermute(two_mine, 'row', swap)]
  transfers between devices with their start and end apart: 30 -> 30, of which waited for: 25 -> 25; matrix products, arithmetic and copies ran while one was open for 6% -> 8% of each run, Pallas kernels for 5% -> 6%
where the time goes in v8:
time: 313 us; the launch traced here: 312 us
  starting transfers between devices  93.5 us (30%)
  waiting for transfers between devices  90.6 us (29%)
  Pallas kernels  58.6 us (19%)
  blocking collectives  22.7 us (7%)
  local copies, waits for them, and re-layouts  19.4 us (6%)
  between operations  14.4 us (5%)
  other arithmetic  9.12 us (3%)
  matrix products  3.56 us (1%)
    ppermute x16, starting transfers between devices, gather_row(): got = lax.ppermute(block, 'row', [(i, i ^ step) for i in range(size)])  50 us
    all_to_all x4, waiting for transfers between devices, exchange(): return lax.all_to_all(blocks, axis, 0, 0)  39.2 us
    ppermute x16, waiting for transfers between devices, gather_row(): got = lax.ppermute(block, 'row', [(i, i ^ step) for i in range(size)])  32.9 us
    pallas_call x1, Pallas kernels, inverse_factor(): pl.pallas_call(functools.partial(inverse_kernel, scale), out_shape=jax.Sh...  25.4 us
    all_to_all x4, starting transfers between devices, exchange(): return lax.all_to_all(blocks, axis, 0, 0)  23.5 us
    all_to_all x2, blocking collectives, exchange(): return lax.all_to_all(blocks, axis, 0, 0)  22.7 us
    pallas_call x2, Pallas kernels, update(): pl.pallas_call(update_kernel, out_shape=jax.ShapeDtypeStruct(start.shape,...  16.6 us
    ppermute x3, starting transfers between devices, body(): lax.ppermute(part, 'row', [(i, i ^ step) for i in range(rows_n)])  7.23 us
  transfers between devices with their start and end apart: 30, of which 25 were waited for; matrix products, arithmetic and copies ran while one was open for 8% of the time, Pallas kernels for 6%

profile of v8, /device:TPU:1, one launch (start us, length us, event | category | flops | bytes accessed | tf_op | source)
XLA Modules:
  0.0 311.9 jit_solution(6746859836811236962)
XLA Ops:
  12.7 4.5 %collective-permute-start = (f32[8,512]{1,0:T(8,128)}, f32[8,512]{1,0:T(8,128)S(1)}, u32[]{:S(2)}, u32[]{:S(2)}) collective-permute-start(f32[8,512]{1,0:T(8,128)} %shard_map.68), channel_id=1, source_target_pairs={{0,0},{1,16},{2,32},{3,48},{4,64},{5,80},{6,96},{7,112},{8,128},{9... | collective-permute-start | bytes 49160 | tf_op jit(solution)/shard_map/ppermute | solution.py:328
  18.8 14.2 %collective-permute-start.1 = (f32[8,512]{1,0:T(8,128)S(1)}, f32[8,512]{1,0:T(8,128)S(1)}, u32[]{:S(2)}, u32[]{:S(2)}) collective-permute-start(f32[8,512]{1,0:T(8,128)S(1)} %collective-permute-done), channel_id=1, source_target_pairs={{0,128},{16,144},{32,160},{48,176},{64,192},{80,208},{96,224},{112... | collective-permute-start | bytes 49160 | tf_op jit(solution)/shard_map/ppermute | solution.py:232
  41.2 4.1 %collective-permute-start.4 = (f32[2,2,2,8,512]{4,3,0,1,2:T(8,128)S(1)}, f32[2,2,2,8,512]{4,3,0,1,2:T(8,128)S(1)}, u32[]{:S(2)}, u32[]{:S(2)}) collective-permute-start(f32[2,2,2,8,512]{4,3,0,1,2:T(8,128)S(1)} %pad_maximum_fusion.6), channel_id=1, source_target_pairs={{0,16},{16,0},{32,48},{48,32},{64,80},{80,64},{96,112},{112,96},{1... | collective-permute-start | bytes 393224 | tf_op jit(solution)/shard_map/ppermute | solution.py:232
  48.4 7.0 %all-to-all-start.1 = ((f32[16,40,128]{2,1,0:T(8,128)}), f32[16,40,128]{2,1,0:T(8,128)S(1)}, u32[]{:S(2)}, u32[]{:S(2)}) async-start(f32[16,40,128]{2,1,0:T(8,128)} %select_maximum_fusion), calls=%async_computation.1 | async-start | bytes 655360 | tf_op jit(solution)/shard_map/all_to_all | solution.py:219
  55.5 3.8 %copy_bitcast_fusion = f32[16,47,8,128]{3,2,1,0:T(8,128)} fusion(f32[128,47,128]{2,0,1:T(8,128)} %param.6), kind=kLoop, calls=%fused_computation | loop fusion | bytes 6160384 | tf_op jit(solution)/shard_map/transpose | solution.py:340
  59.3 7.0 %all-to-all-done.1 = f32[16,40,128]{2,1,0:T(8,128)S(1)} async-done(((f32[16,40,128]{2,1,0:T(8,128)}), f32[16,40,128]{2,1,0:T(8,128)S(1)}, u32[]{:S(2)}, u32[]{:S(2)}) %all-to-all-start.1) | async-done | bytes 327712 | tf_op jit(solution)/shard_map/all_to_all | solution.py:219
  66.3 4.5 %all-to-all-start = ((f32[16,47,8,128]{3,2,1,0:T(8,128)}), f32[16,47,8,128]{3,2,1,0:T(8,128)}, u32[]{:S(2)}, u32[]{:S(2)}) async-start(f32[16,47,8,128]{3,2,1,0:T(8,128)} %copy_bitcast_fusion), calls=%async_computation | async-start | bytes 6160384 | tf_op jit(solution)/shard_map/all_to_all | solution.py:219
  72.8 4.4 %collective-permute-start.5 = (f32[32,128]{1,0:T(8,128)}, f32[32,128]{1,0:T(8,128)S(1)}, u32[]{:S(2)}, u32[]{:S(2)}) collective-permute-start(f32[32,128]{1,0:T(8,128)} %shard_map.69), channel_id=1, source_target_pairs={{0,128},{16,144},{32,160},{48,176},{64,192},{80,208},{96,224},{112... | collective-permute-start | bytes 49160 | tf_op jit(solution)/shard_map/ppermute | solution.py:232
  88.6 5.0 %collective-permute-start.8 = (f32[2,2,2,32,128]{4,3,0,1,2:T(8,128)}, f32[2,2,2,32,128]{4,3,0,1,2:T(8,128)}, u32[]{:S(2)}, u32[]{:S(2)}) collective-permute-start(f32[2,2,2,32,128]{4,3,0,1,2:T(8,128)} %pad_maximum_fusion.7), channel_id=1, source_target_pairs={{0,16},{16,0},{32,48},{48,32},{64,80},{80,64},{96,112},{112,96},{1... | collective-permute-start | bytes 393224 | tf_op jit(solution)/shard_map/ppermute | solution.py:232
  102.9 4.1 %collective-permute-start.9 = (f32[32,128]{1,0:T(8,128)S(1)}, f32[32,128]{1,0:T(8,128)S(1)}, u32[]{:S(2)}, u32[]{:S(2)}) collective-permute-start(f32[32,128]{1,0:T(8,128)S(1)} %sub.11), channel_id=1, source_target_pairs={{0,128},{16,144},{32,160},{48,176},{64,192},{80,208},{96,224},{112... | collective-permute-start | bytes 49160 | tf_op jit(solution)/shard_map/ppermute | solution.py:232
  113.6 6.9 %all-to-all-start.2 = ((f32[16,46,8,128]{3,2,1,0:T(8,128)}), f32[16,46,8,128]{3,2,1,0:T(8,128)}, u32[]{:S(2)}, u32[]{:S(2)}) async-start(f32[16,46,8,128]{3,2,1,0:T(8,128)} %copy_bitcast_fusion.1), calls=%async_computation.2 | async-start | bytes 6029312 | tf_op jit(solution)/shard_map/all_to_all | solution.py:219
  131.8 4.2 %collective-permute-start.13 = (f32[32,128]{1,0:T(8,128)}, f32[32,128]{1,0:T(8,128)S(1)}, u32[]{:S(2)}, u32[]{:S(2)}) collective-permute-start(f32[32,128]{1,0:T(8,128)} %shard_map.72), channel_id=1, source_target_pairs={{0,128},{16,144},{32,160},{48,176},{64,192},{80,208},{96,224},{112... | collective-permute-start | bytes 49160 | tf_op jit(solution)/shard_map/ppermute | solution.py:232
  152.2 9.8 %all-to-all-done.2 = f32[16,46,8,128]{3,2,1,0:T(8,128)} async-done(((f32[16,46,8,128]{3,2,1,0:T(8,128)}), f32[16,46,8,128]{3,2,1,0:T(8,128)}, u32[]{:S(2)}, u32[]{:S(2)}) %all-to-all-start.2) | async-done | bytes 3014688 | tf_op jit(solution)/shard_map/all_to_all | solution.py:219
  163.6 6.6 %all-gather.7.cloned.1.call-done = f32[128,32,128]{2,1,0:T(8,128)} async-done(((f32[8,32,128]{2,1,0:T(8,128)}), f32[128,32,128]{2,1,0:T(8,128)}) %all-gather.7.cloned.1.call-update) | async-done | bytes 2097168 | tf_op jit(solution)/shard_map/all_gather | solution.py:350
  172.5 5.1 %all-to-all-start.3 = ((f32[16,8,32,128]{3,2,1,0:T(8,128)}), f32[16,8,32,128]{3,2,1,0:T(8,128)}, u32[]{:S(2)}, u32[]{:S(2)}) async-start(f32[16,8,32,128]{3,2,1,0:T(8,128)} %broadcast_in_dim.7), calls=%async_computation.3 | async-start | bytes 4194304 | tf_op jit(solution)/shard_map/all_to_all | solution.py:219
  180.2 8.4 %shard_map.75.after_ref.start_ref = f32[384,512]{1,0:T(8,128)} custom-call(s32[1]{0:T(128)} %bitcast.2.core_ref, f32[384,512]{1,0:T(8,128)} %bitcast.137, f32[8,2,47,8,128]{4,3,2,1,0:T(8,128)} %bitcast.7.after_ref.factor_ref, f32[16,8,32,128]{3,2,1,0:T(8,128)} %shard_map.74.mine_ref.one_ref, f32[16,8,32,128]{3,2,1,0:T(8,128)} %collective-permute-done.17.other_ref), custom_call_target="tpu_custom_call" | custom-call | flops 4831838208 | bytes 4718592 | tf_op jit(solution)/shard_map/pallas_call | solution.py:150
  188.5 22.4 %all-to-all-done.3.block_ref = f32[16,8,32,128]{3,2,1,0:T(8,128)} async-done(((f32[16,8,32,128]{3,2,1,0:T(8,128)}), f32[16,8,32,128]{3,2,1,0:T(8,128)}, u32[]{:S(2)}, u32[]{:S(2)}) %all-to-all-start.3) | async-done | bytes 2097184 | tf_op jit(solution)/shard_map/all_to_all | solution.py:219
  216.3 8.2 %shard_map.77.update_ref = f32[384,512]{1,0:T(8,128)} custom-call(s32[1]{0:T(128)} %bitcast.2.core_ref, f32[384,512]{1,0:T(8,128)} %shard_map.75.after_ref.start_ref, f32[8,2,46,8,128]{4,3,2,1,0:T(8,128)} %bitcast.60.after_ref.factor_ref, f32[16,8,32,128]{3,2,1,0:T(8,128)} %shard_map.76.mine_ref.two_ref, f32[16,8,32,128]{3,2,1,0:T(8,128)} %collective-permute-done.18.other_ref), custom_call_target="tpu_custom_call" | custom-call | flops 4831838208 | bytes 4718592 | tf_op jit(solution)/shard_map/pallas_call | solution.py:150
  224.5 4.8 %shard_map.78 = (f32[48,8,512]{2,1,0:T(8,128)}, f32[10,128,128]{2,1,0:T(8,128)}) custom-call(s32[2]{0:T(128)} %pad_add_fusion.at_ref, f32[384,512]{1,0:T(8,128)} %shard_map.77.update_ref, f32[16,8,32,128]{3,2,1,0:T(8,128)} %shard_map.74.mine_ref.one_ref, f32[16,8,32,128]{3,2,1,0:T(8,128)} %shard_map.76.mine_ref.two_ref, f32[384,1]{1,0:T(8,128)} %reshape.76.mass_ref), custom_call_target="tpu_custom_call" | custom-call | flops 805306368 | bytes 2359296 | tf_op jit(solution)/shard_map/pallas_call | solution.py:193
  233.9 12.0 %all_to_all.30 = f32[16,40,128]{2,1,0:T(8,128)S(1)} all-to-all(f32[16,40,128]{2,1,0:T(8,128)S(1)} %bitcast.129), channel_id=1, replica_groups=mesh['row'=16,'col'=16] {'col'}, dimensions={0} | all-to-all | bytes 655360 | tf_op jit(solution)/shard_map/all_to_all | solution.py:219
  252.4 5.7 %collective-permute-start.22 = (f32[40,128]{1,0:T(8,128)S(1)}, f32[40,128]{1,0:T(8,128)S(1)}, u32[]{:S(2)}, u32[]{:S(2)}) collective-permute-start(f32[40,128]{1,0:T(8,128)S(1)} %add.32), channel_id=1, source_target_pairs={{0,128},{16,144},{32,160},{48,176},{64,192},{80,208},{96,224},{112... | collective-permute-start | bytes 61448 | tf_op jit(solution)/shard_map/ppermute | solution.py:367
  259.3 10.7 %all_to_all.31 = f32[16,40,128]{2,1,0:T(8,128)S(1)} all-to-all(f32[16,40,128]{2,1,0:T(8,128)S(1)} %broadcast_in_dim.8), channel_id=1, replica_groups=mesh['row'=16,'col'=16] {'col'}, dimensions={0} | all-to-all | bytes 655360 | tf_op jit(solution)/shard_map/all_to_all | solution.py:219
  270.0 5.7 %collective-permute-start.23 = (f32[5,128,128]{2,1,0:T(8,128)S(1)}, f32[5,128,128]{2,1,0:T(8,128)S(1)}, u32[]{:S(2)}, u32[]{:S(2)}) collective-permute-start(f32[5,128,128]{2,1,0:T(8,128)S(1)} %bitcast.120), channel_id=1, source_target_pairs={{0,16},{16,0},{32,48},{48,32},{64,80},{80,64},{96,112},{112,96},{1... | collective-permute-start | bytes 983048 | tf_op jit(solution)/shard_map/ppermute | solution.py:370
  277.3 25.4 %shard_map.79 = f32[512,512]{1,0:T(8,128)S(1)} custom-call(s32[1]{0:T(128)} %bitcast.2.core_ref, f32[5,128,128]{2,1,0:T(8,128)S(1)} %bitcast.121, f32[5,128,128]{2,1,0:T(8,128)S(1)} %collective-permute-done.23.other_ref), custom_call_target="tpu_custom_call" | custom-call | tf_op jit(solution)/shard_map/pallas_call | solution.py:116
  (132 shorter events, 102.9 us)
Async XLA Ops:
  7.2 64.3 %all-gather.5.cloned.1.call-start = ((), (), s32[]{:S(2)}) async-start(), calls=%async_computation.6 | async-start | bytes 2228224 | tf_op jit(solution)/shard_map/all_gather | solution.py:326
  12.7 6.1 %collective-permute-start = (f32[8,512]{1,0:T(8,128)}, f32[8,512]{1,0:T(8,128)S(1)}, u32[]{:S(2)}, u32[]{:S(2)}) collective-permute-start(f32[8,512]{1,0:T(8,128)} %shard_map.68), channel_id=1, source_target_pairs={{0,0},{1,16},{2,32},{3,48},{4,64},{5,80},{6,96},{7,112},{8,128},{9... | collective-permute-start | bytes 49160 | tf_op jit(solution)/shard_map/ppermute | solution.py:328
  18.8 15.3 %collective-permute-start.1 = (f32[8,512]{1,0:T(8,128)S(1)}, f32[8,512]{1,0:T(8,128)S(1)}, u32[]{:S(2)}, u32[]{:S(2)}) collective-permute-start(f32[8,512]{1,0:T(8,128)S(1)} %collective-permute-done), channel_id=1, source_target_pairs={{0,128},{16,144},{32,160},{48,176},{64,192},{80,208},{96,224},{112... | collective-permute-start | bytes 49160 | tf_op jit(solution)/shard_map/ppermute | solution.py:232
  34.2 3.8 %collective-permute-start.2 = (f32[2,8,512]{2,1,0:T(8,128)S(1)}, f32[2,8,512]{2,1,0:T(8,128)S(1)}, u32[]{:S(2)}, u32[]{:S(2)}) collective-permute-start(f32[2,8,512]{2,1,0:T(8,128)S(1)} %pad_maximum_fusion.14), channel_id=1, source_target_pairs={{0,64},{16,80},{32,96},{48,112},{64,0},{80,16},{96,32},{112,48},{1... | collective-permute-start | bytes 98312 | tf_op jit(solution)/shard_map/ppermute | solution.py:232
  41.2 5.1 %collective-permute-start.4 = (f32[2,2,2,8,512]{4,3,0,1,2:T(8,128)S(1)}, f32[2,2,2,8,512]{4,3,0,1,2:T(8,128)S(1)}, u32[]{:S(2)}, u32[]{:S(2)}) collective-permute-start(f32[2,2,2,8,512]{4,3,0,1,2:T(8,128)S(1)} %pad_maximum_fusion.6), channel_id=1, source_target_pairs={{0,16},{16,0},{32,48},{48,32},{64,80},{80,64},{96,112},{112,96},{1... | collective-permute-start | bytes 393224 | tf_op jit(solution)/shard_map/ppermute | solution.py:232
  48.4 17.8 %all-to-all-start.1 = ((f32[16,40,128]{2,1,0:T(8,128)}), f32[16,40,128]{2,1,0:T(8,128)S(1)}, u32[]{:S(2)}, u32[]{:S(2)}) async-start(f32[16,40,128]{2,1,0:T(8,128)} %select_maximum_fusion), calls=%async_computation.1 | async-start | bytes 655360 | tf_op jit(solution)/shard_map/all_to_all | solution.py:219
  66.3 47.3 %all-to-all-start = ((f32[16,47,8,128]{3,2,1,0:T(8,128)}), f32[16,47,8,128]{3,2,1,0:T(8,128)}, u32[]{:S(2)}, u32[]{:S(2)}) async-start(f32[16,47,8,128]{3,2,1,0:T(8,128)} %copy_bitcast_fusion), calls=%async_computation | async-start | bytes 6160384 | tf_op jit(solution)/shard_map/all_to_all | solution.py:219
  70.8 99.4 %all-gather.7.cloned.1.call-start = ((), (), s32[]{:S(2)}) async-start(), calls=%async_computation.7 | async-start | bytes 2228224 | tf_op jit(solution)/shard_map/all_gather | solution.py:350
  72.8 6.7 %collective-permute-start.5 = (f32[32,128]{1,0:T(8,128)}, f32[32,128]{1,0:T(8,128)S(1)}, u32[]{:S(2)}, u32[]{:S(2)}) collective-permute-start(f32[32,128]{1,0:T(8,128)} %shard_map.69), channel_id=1, source_target_pairs={{0,128},{16,144},{32,160},{48,176},{64,192},{80,208},{96,224},{112... | collective-permute-start | bytes 49160 | tf_op jit(solution)/shard_map/ppermute | solution.py:232
  80.2 4.1 %collective-permute-start.6 = (f32[2,32,128]{2,1,0:T(8,128)S(1)}, f32[2,32,128]{2,1,0:T(8,128)S(1)}, u32[]{:S(2)}, u32[]{:S(2)}) collective-permute-start(f32[2,32,128]{2,1,0:T(8,128)S(1)} %pad_maximum_fusion.15), channel_id=1, source_target_pairs={{0,64},{16,80},{32,96},{48,112},{64,0},{80,16},{96,32},{112,48},{1... | collective-permute-start | bytes 98312 | tf_op jit(solution)/shard_map/ppermute | solution.py:232
  88.6 6.4 %collective-permute-start.8 = (f32[2,2,2,32,128]{4,3,0,1,2:T(8,128)}, f32[2,2,2,32,128]{4,3,0,1,2:T(8,128)}, u32[]{:S(2)}, u32[]{:S(2)}) collective-permute-start(f32[2,2,2,32,128]{4,3,0,1,2:T(8,128)} %pad_maximum_fusion.7), channel_id=1, source_target_pairs={{0,16},{16,0},{32,48},{48,32},{64,80},{80,64},{96,112},{112,96},{1... | collective-permute-start | bytes 393224 | tf_op jit(solution)/shard_map/ppermute | solution.py:232
  102.9 6.6 %collective-permute-start.9 = (f32[32,128]{1,0:T(8,128)S(1)}, f32[32,128]{1,0:T(8,128)S(1)}, u32[]{:S(2)}, u32[]{:S(2)}) collective-permute-start(f32[32,128]{1,0:T(8,128)S(1)} %sub.11), channel_id=1, source_target_pairs={{0,128},{16,144},{32,160},{48,176},{64,192},{80,208},{96,224},{112... | collective-permute-start | bytes 49160 | tf_op jit(solution)/shard_map/ppermute | solution.py:232
  109.5 10.9 %collective-permute-start.10 = (f32[2,32,128]{2,1,0:T(8,128)S(1)}, f32[2,32,128]{2,1,0:T(8,128)S(1)}, u32[]{:S(2)}, u32[]{:S(2)}) collective-permute-start(f32[2,32,128]{2,1,0:T(8,128)S(1)} %pad_maximum_fusion.16), channel_id=1, source_target_pairs={{0,64},{16,80},{32,96},{48,112},{64,0},{80,16},{96,32},{112,48},{1... | collective-permute-start | bytes 98312 | tf_op jit(solution)/shard_map/ppermute | solution.py:232
  113.6 48.4 %all-to-all-start.2 = ((f32[16,46,8,128]{3,2,1,0:T(8,128)}), f32[16,46,8,128]{3,2,1,0:T(8,128)}, u32[]{:S(2)}, u32[]{:S(2)}) async-start(f32[16,46,8,128]{3,2,1,0:T(8,128)} %copy_bitcast_fusion.1), calls=%async_computation.2 | async-start | bytes 6029312 | tf_op jit(solution)/shard_map/all_to_all | solution.py:219
  124.1 3.9 %collective-permute-start.12 = (f32[2,2,2,32,128]{4,3,0,1,2:T(8,128)S(1)}, f32[2,2,2,32,128]{4,3,0,1,2:T(8,128)S(1)}, u32[]{:S(2)}, u32[]{:S(2)}) collective-permute-start(f32[2,2,2,32,128]{4,3,0,1,2:T(8,128)S(1)} %pad_maximum_fusion.8), channel_id=1, source_target_pairs={{0,16},{16,0},{32,48},{48,32},{64,80},{80,64},{96,112},{112,96},{1... | collective-permute-start | bytes 393224 | tf_op jit(solution)/shard_map/ppermute | solution.py:232
  131.8 6.8 %collective-permute-start.13 = (f32[32,128]{1,0:T(8,128)}, f32[32,128]{1,0:T(8,128)S(1)}, u32[]{:S(2)}, u32[]{:S(2)}) collective-permute-start(f32[32,128]{1,0:T(8,128)} %shard_map.72), channel_id=1, source_target_pairs={{0,128},{16,144},{32,160},{48,176},{64,192},{80,208},{96,224},{112... | collective-permute-start | bytes 49160 | tf_op jit(solution)/shard_map/ppermute | solution.py:232
  139.4 4.1 %collective-permute-start.14 = (f32[2,32,128]{2,1,0:T(8,128)S(1)}, f32[2,32,128]{2,1,0:T(8,128)S(1)}, u32[]{:S(2)}, u32[]{:S(2)}) collective-permute-start(f32[2,32,128]{2,1,0:T(8,128)S(1)} %pad_maximum_fusion.17), channel_id=1, source_target_pairs={{0,64},{16,80},{32,96},{48,112},{64,0},{80,16},{96,32},{112,48},{1... | collective-permute-start | bytes 98312 | tf_op jit(solution)/shard_map/ppermute | solution.py:232
  147.1 4.3 %collective-permute-start.16 = (f32[2,2,2,32,128]{4,3,0,1,2:T(8,128)S(1)}, f32[2,2,2,32,128]{4,3,0,1,2:T(8,128)S(1)}, u32[]{:S(2)}, u32[]{:S(2)}) collective-permute-start(f32[2,2,2,32,128]{4,3,0,1,2:T(8,128)S(1)} %pad_maximum_fusion.9), channel_id=1, source_target_pairs={{0,16},{16,0},{32,48},{48,32},{64,80},{80,64},{96,112},{112,96},{1... | collective-permute-start | bytes 393224 | tf_op jit(solution)/shard_map/ppermute | solution.py:232
  170.2 10.0 %collective-permute-start.17 = (f32[16,8,32,128]{3,2,1,0:T(8,128)}, f32[16,8,32,128]{3,2,1,0:T(8,128)}, u32[]{:S(2)}, u32[]{:S(2)}) collective-permute-start(f32[16,8,32,128]{3,2,1,0:T(8,128)} %shard_map.74.mine_ref.one_ref), channel_id=1, source_target_pairs={{0,16},{16,0},{32,48},{48,32},{64,80},{80,64},{96,112},{112,96},{1... | collective-permute-start | bytes 6291464 | tf_op jit(solution)/shard_map/ppermute | solution.py:355
  172.5 38.4 %all-to-all-start.3 = ((f32[16,8,32,128]{3,2,1,0:T(8,128)}), f32[16,8,32,128]{3,2,1,0:T(8,128)}, u32[]{:S(2)}, u32[]{:S(2)}) async-start(f32[16,8,32,128]{3,2,1,0:T(8,128)} %broadcast_in_dim.7), calls=%async_computation.3 | async-start | bytes 4194304 | tf_op jit(solution)/shard_map/all_to_all | solution.py:219
  211.0 5.3 %collective-permute-start.18 = (f32[16,8,32,128]{3,2,1,0:T(8,128)}, f32[16,8,32,128]{3,2,1,0:T(8,128)}, u32[]{:S(2)}, u32[]{:S(2)}) collective-permute-start(f32[16,8,32,128]{3,2,1,0:T(8,128)} %shard_map.76.mine_ref.two_ref), channel_id=1, source_target_pairs={{0,16},{16,0},{32,48},{48,32},{64,80},{80,64},{96,112},{112,96},{1... | collective-permute-start | bytes 6291464 | tf_op jit(solution)/shard_map/ppermute | solution.py:357
  248.6 3.8 %collective-permute-start.21 = (f32[40,128]{1,0:T(8,128)S(1)}, f32[40,128]{1,0:T(8,128)S(1)}, u32[]{:S(2)}, u32[]{:S(2)}) collective-permute-start(f32[40,128]{1,0:T(8,128)S(1)} %add.31), channel_id=1, source_target_pairs={{0,64},{16,80},{32,96},{48,112},{64,0},{80,16},{96,32},{112,48},{1... | collective-permute-start | bytes 61448 | tf_op jit(solution)/shard_map/ppermute | solution.py:367
  252.4 6.9 %collective-permute-start.22 = (f32[40,128]{1,0:T(8,128)S(1)}, f32[40,128]{1,0:T(8,128)S(1)}, u32[]{:S(2)}, u32[]{:S(2)}) collective-permute-start(f32[40,128]{1,0:T(8,128)S(1)} %add.32), channel_id=1, source_target_pairs={{0,128},{16,144},{32,160},{48,176},{64,192},{80,208},{96,224},{112... | collective-permute-start | bytes 61448 | tf_op jit(solution)/shard_map/ppermute | solution.py:367
  270.0 7.3 %collective-permute-start.23 = (f32[5,128,128]{2,1,0:T(8,128)S(1)}, f32[5,128,128]{2,1,0:T(8,128)S(1)}, u32[]{:S(2)}, u32[]{:S(2)}) collective-permute-start(f32[5,128,128]{2,1,0:T(8,128)S(1)} %bitcast.120), channel_id=1, source_target_pairs={{0,16},{16,0},{32,48},{48,32},{64,80},{80,64},{96,112},{112,96},{1... | collective-permute-start | bytes 983048 | tf_op jit(solution)/shard_map/ppermute | solution.py:370
  (10 other events, 182.0 us)
Sparse Core Ops, SparseCore 0:
  11.0 56.3 all-gather.4
  99.1 71.0 all-gather.6

commit v9 on v8

--- a/solution.py
+++ b/solution.py
@@ -168,7 +168,7 @@
     )(jnp.full((1,), core, jnp.int32), start, factor, mine, other)
 
 
-def finish_kernel(at_ref, update_ref, one_ref, two_ref, mass_ref, solved_ref, blocks_ref):
+def finish_kernel(at_ref, update_ref, one_ref, two_ref, mass_ref, solved_ref, mine_ref, there_ref):
     rounds, own, k_all = solved_ref.shape
     lanes = lax.broadcasted_iota(jnp.int32, (own, BLOCK), 1)
     rows = lax.broadcasted_iota(jnp.int32, (own, BLOCK), 0)
@@ -182,18 +182,29 @@
     for i in range(k_all // BLOCK):
         got = small_dot(weighted[:, i * BLOCK : (i + 1) * BLOCK], all_rows[:, i * BLOCK :], 0, 0)
         for j in range(k_all // BLOCK - i):
-            blocks_ref[at] = got[:, j * BLOCK : (j + 1) * BLOCK]
+            side, place = at // mine_ref.shape[0], at % mine_ref.shape[0]
+            part = got[:, j * BLOCK : (j + 1) * BLOCK]
+
+            @pl.when(at_ref[2] == side)
+            def _():
+                mine_ref[place] = part
+
+            @pl.when(at_ref[2] != side)
+            def _():
+                there_ref[place] = part
+
             at += 1
 
 
-def finish(updated, one, two, mass, place, col, shape):
+def finish(updated, one, two, mass, place, col, core, shape):
     rounds, own, k_all = shape
     panel = pl.BlockSpec((one.shape[0], 1) + one.shape[2:], lambda s, at: (0, at[0], 0, 0))
-    count = len(block_pairs(k_all))
+    count = len(block_pairs(k_all)) // 2
     return pl.pallas_call(
         finish_kernel,
         out_shape=(
             jax.ShapeDtypeStruct(shape, jnp.float32),
+            jax.ShapeDtypeStruct((count, BLOCK, BLOCK), jnp.float32),
             jax.ShapeDtypeStruct((count, BLOCK, BLOCK), jnp.float32),
         ),
         grid_spec=pltpu.PrefetchScalarGridSpec(
@@ -208,11 +219,12 @@
             out_specs=(
                 pl.BlockSpec(shape, lambda s, at: (0, 0, 0)),
                 pl.BlockSpec((count, BLOCK, BLOCK), lambda s, at: (0, 0, 0)),
+                pl.BlockSpec((count, BLOCK, BLOCK), lambda s, at: (0, 0, 0)),
             ),
         ),
         compiler_params=pltpu.CompilerParams(vmem_limit_bytes=56 * 1024 * 1024),
         cost_estimate=pl.CostEstimate(flops=8 * updated.size * k_all, bytes_accessed=12 * updated.size, transcendentals=0),
-    )(jnp.stack([place, col]).astype(jnp.int32), updated, one, two, mass.T.reshape(-1, 1))
+    )(jnp.stack([place, col, core]).astype(jnp.int32), updated, one, two, mass.T.reshape(-1, 1))
 
 
 def exchange(blocks, axis):
@@ -355,12 +367,10 @@
     done = update(done, f_one, one_mine, lax.ppermute(one_mine, "row", swap), core)
     two_mine = keep(two_mine, done)
     done = update(done, f_two, two_mine, lax.ppermute(two_mine, "row", swap), core)
-    solved, blocks = finish(done, one_mine, two_mine, lumped_mass, row // 2, col, (rounds, own, k_all))
+    solved, kept, given = finish(done, one_mine, two_mine, lumped_mass, row // 2, col, core, (rounds, own, k_all))
     solved = solved.transpose(1, 0, 2)
 
-    blocks = blocks.reshape((2, -1, BLOCK))
-    there = lax.ppermute(lax.dynamic_index_in_dim(blocks, 1 - core, 0, keepdims=False), "row", swap)
-    part = lax.dynamic_index_in_dim(blocks, core, 0, keepdims=False) + there
+    part = kept + lax.ppermute(given, "row", swap)
     part = exchange(part.reshape(cols_n, -1, BLOCK), "col").sum(axis=0)
     step = 2
     while step < rows_n:

time: 313 us -> 313 us (level)
  no operation moved by 1% of the time
where the time goes in v9:
time: 313 us; the launch traced here: 311 us
  starting transfers between devices  93.5 us (30%)
  waiting for transfers between devices  90.6 us (29%)
  Pallas kernels  59.8 us (19%)
  blocking collectives  22.7 us (7%)
  local copies, waits for them, and re-layouts  17.7 us (6%)
  between operations  14.4 us (5%)
  other arithmetic  9.14 us (3%)
  matrix products  3.56 us (1%)
    ppermute x16, starting transfers between devices, gather_row(): got = lax.ppermute(block, 'row', [(i, i ^ step) for i in range(size)])  50 us
    all_to_all x4, waiting for transfers between devices, exchange(): return lax.all_to_all(blocks, axis, 0, 0)  39.2 us
    ppermute x16, waiting for transfers between devices, gather_row(): got = lax.ppermute(block, 'row', [(i, i ^ step) for i in range(size)])  32.9 us
    pallas_call x1, Pallas kernels, inverse_factor(): pl.pallas_call(functools.partial(inverse_kernel, scale), out_shape=jax.Sh...  25.4 us
    all_to_all x4, starting transfers between devices, exchange(): return lax.all_to_all(blocks, axis, 0, 0)  23.5 us
    all_to_all x2, blocking collectives, exchange(): return lax.all_to_all(blocks, axis, 0, 0)  22.7 us
    pallas_call x2, Pallas kernels, update(): pl.pallas_call(update_kernel, out_shape=jax.ShapeDtypeStruct(start.shape,...  16.6 us
    ppermute x3, starting transfers between devices, body(): lax.ppermute(part, 'row', [(i, i ^ step) for i in range(rows_n)])  7.23 us
  transfers between devices with their start and end apart: 30, of which 25 were waited for; matrix products, arithmetic and copies ran while one was open for 8% of the time, Pallas kernels for 6%

profile of v9, /device:TPU:1, one launch (start us, length us, event | category | flops | bytes accessed | tf_op | source)
XLA Modules:
  0.0 311.4 jit_solution(17735790254684000125)
XLA Ops:
  12.7 4.5 %collective-permute-start = (f32[8,512]{1,0:T(8,128)}, f32[8,512]{1,0:T(8,128)S(1)}, u32[]{:S(2)}, u32[]{:S(2)}) collective-permute-start(f32[8,512]{1,0:T(8,128)} %shard_map.68), channel_id=1, source_target_pairs={{0,0},{1,16},{2,32},{3,48},{4,64},{5,80},{6,96},{7,112},{8,128},{9... | collective-permute-start | bytes 49160 | tf_op jit(solution)/shard_map/ppermute | solution.py:340
  18.8 14.2 %collective-permute-start.1 = (f32[8,512]{1,0:T(8,128)S(1)}, f32[8,512]{1,0:T(8,128)S(1)}, u32[]{:S(2)}, u32[]{:S(2)}) collective-permute-start(f32[8,512]{1,0:T(8,128)S(1)} %collective-permute-done), channel_id=1, source_target_pairs={{0,128},{16,144},{32,160},{48,176},{64,192},{80,208},{96,224},{112... | collective-permute-start | bytes 49160 | tf_op jit(solution)/shard_map/ppermute | solution.py:244
  41.2 4.1 %collective-permute-start.4 = (f32[2,2,2,8,512]{4,3,0,1,2:T(8,128)S(1)}, f32[2,2,2,8,512]{4,3,0,1,2:T(8,128)S(1)}, u32[]{:S(2)}, u32[]{:S(2)}) collective-permute-start(f32[2,2,2,8,512]{4,3,0,1,2:T(8,128)S(1)} %pad_maximum_fusion.6), channel_id=1, source_target_pairs={{0,16},{16,0},{32,48},{48,32},{64,80},{80,64},{96,112},{112,96},{1... | collective-permute-start | bytes 393224 | tf_op jit(solution)/shard_map/ppermute | solution.py:244
  48.4 7.0 %all-to-all-start.1 = ((f32[16,40,128]{2,1,0:T(8,128)}), f32[16,40,128]{2,1,0:T(8,128)S(1)}, u32[]{:S(2)}, u32[]{:S(2)}) async-start(f32[16,40,128]{2,1,0:T(8,128)} %select_maximum_fusion), calls=%async_computation.1 | async-start | bytes 655360 | tf_op jit(solution)/shard_map/all_to_all | solution.py:231
  55.5 3.8 %copy_bitcast_fusion = f32[16,47,8,128]{3,2,1,0:T(8,128)} fusion(f32[128,47,128]{2,0,1:T(8,128)} %param.6), kind=kLoop, calls=%fused_computation | loop fusion | bytes 6160384 | tf_op jit(solution)/shard_map/transpose | solution.py:352
  59.3 7.0 %all-to-all-done.1 = f32[16,40,128]{2,1,0:T(8,128)S(1)} async-done(((f32[16,40,128]{2,1,0:T(8,128)}), f32[16,40,128]{2,1,0:T(8,128)S(1)}, u32[]{:S(2)}, u32[]{:S(2)}) %all-to-all-start.1) | async-done | bytes 327712 | tf_op jit(solution)/shard_map/all_to_all | solution.py:231
  66.3 4.5 %all-to-all-start = ((f32[16,47,8,128]{3,2,1,0:T(8,128)}), f32[16,47,8,128]{3,2,1,0:T(8,128)}, u32[]{:S(2)}, u32[]{:S(2)}) async-start(f32[16,47,8,128]{3,2,1,0:T(8,128)} %copy_bitcast_fusion), calls=%async_computation | async-start | bytes 6160384 | tf_op jit(solution)/shard_map/all_to_all | solution.py:231
  72.8 4.4 %collective-permute-start.5 = (f32[32,128]{1,0:T(8,128)}, f32[32,128]{1,0:T(8,128)S(1)}, u32[]{:S(2)}, u32[]{:S(2)}) collective-permute-start(f32[32,128]{1,0:T(8,128)} %shard_map.69), channel_id=1, source_target_pairs={{0,128},{16,144},{32,160},{48,176},{64,192},{80,208},{96,224},{112... | collective-permute-start | bytes 49160 | tf_op jit(solution)/shard_map/ppermute | solution.py:244
  88.6 5.0 %collective-permute-start.8 = (f32[2,2,2,32,128]{4,3,0,1,2:T(8,128)}, f32[2,2,2,32,128]{4,3,0,1,2:T(8,128)}, u32[]{:S(2)}, u32[]{:S(2)}) collective-permute-start(f32[2,2,2,32,128]{4,3,0,1,2:T(8,128)} %pad_maximum_fusion.7), channel_id=1, source_target_pairs={{0,16},{16,0},{32,48},{48,32},{64,80},{80,64},{96,112},{112,96},{1... | collective-permute-start | bytes 393224 | tf_op jit(solution)/shard_map/ppermute | solution.py:244
  102.9 4.1 %collective-permute-start.9 = (f32[32,128]{1,0:T(8,128)S(1)}, f32[32,128]{1,0:T(8,128)S(1)}, u32[]{:S(2)}, u32[]{:S(2)}) collective-permute-start(f32[32,128]{1,0:T(8,128)S(1)} %sub.8), channel_id=1, source_target_pairs={{0,128},{16,144},{32,160},{48,176},{64,192},{80,208},{96,224},{112... | collective-permute-start | bytes 49160 | tf_op jit(solution)/shard_map/ppermute | solution.py:244
  113.6 6.9 %all-to-all-start.2 = ((f32[16,46,8,128]{3,2,1,0:T(8,128)}), f32[16,46,8,128]{3,2,1,0:T(8,128)}, u32[]{:S(2)}, u32[]{:S(2)}) async-start(f32[16,46,8,128]{3,2,1,0:T(8,128)} %copy_bitcast_fusion.1), calls=%async_computation.2 | async-start | bytes 6029312 | tf_op jit(solution)/shard_map/all_to_all | solution.py:231
  131.8 4.2 %collective-permute-start.13 = (f32[32,128]{1,0:T(8,128)}, f32[32,128]{1,0:T(8,128)S(1)}, u32[]{:S(2)}, u32[]{:S(2)}) collective-permute-start(f32[32,128]{1,0:T(8,128)} %shard_map.72), channel_id=1, source_target_pairs={{0,128},{16,144},{32,160},{48,176},{64,192},{80,208},{96,224},{112... | collective-permute-start | bytes 49160 | tf_op jit(solution)/shard_map/ppermute | solution.py:244
  152.2 9.8 %all-to-all-done.2 = f32[16,46,8,128]{3,2,1,0:T(8,128)} async-done(((f32[16,46,8,128]{3,2,1,0:T(8,128)}), f32[16,46,8,128]{3,2,1,0:T(8,128)}, u32[]{:S(2)}, u32[]{:S(2)}) %all-to-all-start.2) | async-done | bytes 3014688 | tf_op jit(solution)/shard_map/all_to_all | solution.py:231
  163.6 6.6 %all-gather.7.cloned.1.call-done = f32[128,32,128]{2,1,0:T(8,128)} async-done(((f32[8,32,128]{2,1,0:T(8,128)}), f32[128,32,128]{2,1,0:T(8,128)}) %all-gather.7.cloned.1.call-update) | async-done | bytes 2097168 | tf_op jit(solution)/shard_map/all_gather | solution.py:362
  172.5 5.1 %all-to-all-start.3 = ((f32[16,8,32,128]{3,2,1,0:T(8,128)}), f32[16,8,32,128]{3,2,1,0:T(8,128)}, u32[]{:S(2)}, u32[]{:S(2)}) async-start(f32[16,8,32,128]{3,2,1,0:T(8,128)} %broadcast_in_dim.4), calls=%async_computation.3 | async-start | bytes 4194304 | tf_op jit(solution)/shard_map/all_to_all | solution.py:231
  180.2 8.4 %shard_map.75.after_ref.start_ref = f32[384,512]{1,0:T(8,128)} custom-call(s32[1]{0:T(128)} %bitcast.2.core_ref, f32[384,512]{1,0:T(8,128)} %bitcast.132, f32[8,2,47,8,128]{4,3,2,1,0:T(8,128)} %bitcast.7.after_ref.factor_ref, f32[16,8,32,128]{3,2,1,0:T(8,128)} %shard_map.74.mine_ref.one_ref, f32[16,8,32,128]{3,2,1,0:T(8,128)} %collective-permute-done.17.other_ref), custom_call_target="tpu_custom_call" | custom-call | flops 4831838208 | bytes 4718592 | tf_op jit(solution)/shard_map/pallas_call | solution.py:150
  188.5 22.4 %all-to-all-done.3.block_ref = f32[16,8,32,128]{3,2,1,0:T(8,128)} async-done(((f32[16,8,32,128]{3,2,1,0:T(8,128)}), f32[16,8,32,128]{3,2,1,0:T(8,128)}, u32[]{:S(2)}, u32[]{:S(2)}) %all-to-all-start.3) | async-done | bytes 2097184 | tf_op jit(solution)/shard_map/all_to_all | solution.py:231
  216.3 8.2 %shard_map.77.update_ref = f32[384,512]{1,0:T(8,128)} custom-call(s32[1]{0:T(128)} %bitcast.2.core_ref, f32[384,512]{1,0:T(8,128)} %shard_map.75.after_ref.start_ref, f32[8,2,46,8,128]{4,3,2,1,0:T(8,128)} %bitcast.60.after_ref.factor_ref, f32[16,8,32,128]{3,2,1,0:T(8,128)} %shard_map.76.mine_ref.two_ref, f32[16,8,32,128]{3,2,1,0:T(8,128)} %collective-permute-done.18.other_ref), custom_call_target="tpu_custom_call" | custom-call | flops 4831838208 | bytes 4718592 | tf_op jit(solution)/shard_map/pallas_call | solution.py:150
  224.5 6.0 %shard_map.78 = (f32[48,8,512]{2,1,0:T(8,128)}, f32[5,128,128]{2,1,0:T(8,128)}, f32[5,128,128]{2,1,0:T(8,128)}) custom-call(s32[3]{0:T(128)} %pad_add_fusion.at_ref, f32[384,512]{1,0:T(8,128)} %shard_map.77.update_ref, f32[16,8,32,128]{3,2,1,0:T(8,128)} %shard_map.74.mine_ref.one_ref, f32[16,8,32,128]{3,2,1,0:T(8,128)} %shard_map.76.mine_ref.two_ref, ...), custom_call_target="tpu_custom_call" | custom-call | flops 805306368 | bytes 2359296 | tf_op jit(solution)/shard_map/pallas_call | solution.py:203
  233.4 12.0 %all_to_all.30 = f32[16,40,128]{2,1,0:T(8,128)S(1)} all-to-all(f32[16,40,128]{2,1,0:T(8,128)S(1)} %bitcast.124), channel_id=1, replica_groups=mesh['row'=16,'col'=16] {'col'}, dimensions={0} | all-to-all | bytes 655360 | tf_op jit(solution)/shard_map/all_to_all | solution.py:231
  251.9 5.7 %collective-permute-start.22 = (f32[40,128]{1,0:T(8,128)S(1)}, f32[40,128]{1,0:T(8,128)S(1)}, u32[]{:S(2)}, u32[]{:S(2)}) collective-permute-start(f32[40,128]{1,0:T(8,128)S(1)} %add.22), channel_id=1, source_target_pairs={{0,128},{16,144},{32,160},{48,176},{64,192},{80,208},{96,224},{112... | collective-permute-start | bytes 61448 | tf_op jit(solution)/shard_map/ppermute | solution.py:377
  258.8 10.7 %all_to_all.31 = f32[16,40,128]{2,1,0:T(8,128)S(1)} all-to-all(f32[16,40,128]{2,1,0:T(8,128)S(1)} %broadcast_in_dim.5), channel_id=1, replica_groups=mesh['row'=16,'col'=16] {'col'}, dimensions={0} | all-to-all | bytes 655360 | tf_op jit(solution)/shard_map/all_to_all | solution.py:231
  269.5 5.7 %collective-permute-start.23 = (f32[5,128,128]{2,1,0:T(8,128)S(1)}, f32[5,128,128]{2,1,0:T(8,128)S(1)}, u32[]{:S(2)}, u32[]{:S(2)}) collective-permute-start(f32[5,128,128]{2,1,0:T(8,128)S(1)} %bitcast.115), channel_id=1, source_target_pairs={{0,16},{16,0},{32,48},{48,32},{64,80},{80,64},{96,112},{112,96},{1... | collective-permute-start | bytes 983048 | tf_op jit(solution)/shard_map/ppermute | solution.py:380
  276.9 25.4 %shard_map.79 = f32[512,512]{1,0:T(8,128)S(1)} custom-call(s32[1]{0:T(128)} %bitcast.2.core_ref, f32[5,128,128]{2,1,0:T(8,128)S(1)} %bitcast.116, f32[5,128,128]{2,1,0:T(8,128)S(1)} %collective-permute-done.23.other_ref), custom_call_target="tpu_custom_call" | custom-call | tf_op jit(solution)/shard_map/pallas_call | solution.py:116
  (131 shorter events, 101.2 us)
Async XLA Ops:
  7.2 64.3 %all-gather.5.cloned.1.call-start = ((), (), s32[]{:S(2)}) async-start(), calls=%async_computation.6 | async-start | bytes 2228224 | tf_op jit(solution)/shard_map/all_gather | solution.py:338
  12.7 6.1 %collective-permute-start = (f32[8,512]{1,0:T(8,128)}, f32[8,512]{1,0:T(8,128)S(1)}, u32[]{:S(2)}, u32[]{:S(2)}) collective-permute-start(f32[8,512]{1,0:T(8,128)} %shard_map.68), channel_id=1, source_target_pairs={{0,0},{1,16},{2,32},{3,48},{4,64},{5,80},{6,96},{7,112},{8,128},{9... | collective-permute-start | bytes 49160 | tf_op jit(solution)/shard_map/ppermute | solution.py:340
  18.8 15.3 %collective-permute-start.1 = (f32[8,512]{1,0:T(8,128)S(1)}, f32[8,512]{1,0:T(8,128)S(1)}, u32[]{:S(2)}, u32[]{:S(2)}) collective-permute-start(f32[8,512]{1,0:T(8,128)S(1)} %collective-permute-done), channel_id=1, source_target_pairs={{0,128},{16,144},{32,160},{48,176},{64,192},{80,208},{96,224},{112... | collective-permute-start | bytes 49160 | tf_op jit(solution)/shard_map/ppermute | solution.py:244
  34.2 3.8 %collective-permute-start.2 = (f32[2,8,512]{2,1,0:T(8,128)S(1)}, f32[2,8,512]{2,1,0:T(8,128)S(1)}, u32[]{:S(2)}, u32[]{:S(2)}) collective-permute-start(f32[2,8,512]{2,1,0:T(8,128)S(1)} %pad_maximum_fusion.14), channel_id=1, source_target_pairs={{0,64},{16,80},{32,96},{48,112},{64,0},{80,16},{96,32},{112,48},{1... | collective-permute-start | bytes 98312 | tf_op jit(solution)/shard_map/ppermute | solution.py:244
  41.2 5.1 %collective-permute-start.4 = (f32[2,2,2,8,512]{4,3,0,1,2:T(8,128)S(1)}, f32[2,2,2,8,512]{4,3,0,1,2:T(8,128)S(1)}, u32[]{:S(2)}, u32[]{:S(2)}) collective-permute-start(f32[2,2,2,8,512]{4,3,0,1,2:T(8,128)S(1)} %pad_maximum_fusion.6), channel_id=1, source_target_pairs={{0,16},{16,0},{32,48},{48,32},{64,80},{80,64},{96,112},{112,96},{1... | collective-permute-start | bytes 393224 | tf_op jit(solution)/shard_map/ppermute | solution.py:244
  48.4 17.8 %all-to-all-start.1 = ((f32[16,40,128]{2,1,0:T(8,128)}), f32[16,40,128]{2,1,0:T(8,128)S(1)}, u32[]{:S(2)}, u32[]{:S(2)}) async-start(f32[16,40,128]{2,1,0:T(8,128)} %select_maximum_fusion), calls=%async_computation.1 | async-start | bytes 655360 | tf_op jit(solution)/shard_map/all_to_all | solution.py:231
  66.3 47.3 %all-to-all-start = ((f32[16,47,8,128]{3,2,1,0:T(8,128)}), f32[16,47,8,128]{3,2,1,0:T(8,128)}, u32[]{:S(2)}, u32[]{:S(2)}) async-start(f32[16,47,8,128]{3,2,1,0:T(8,128)} %copy_bitcast_fusion), calls=%async_computation | async-start | bytes 6160384 | tf_op jit(solution)/shard_map/all_to_all | solution.py:231
  70.8 99.4 %all-gather.7.cloned.1.call-start = ((), (), s32[]{:S(2)}) async-start(), calls=%async_computation.7 | async-start | bytes 2228224 | tf_op jit(solution)/shard_map/all_gather | solution.py:362
  72.8 6.7 %collective-permute-start.5 = (f32[32,128]{1,0:T(8,128)}, f32[32,128]{1,0:T(8,128)S(1)}, u32[]{:S(2)}, u32[]{:S(2)}) collective-permute-start(f32[32,128]{1,0:T(8,128)} %shard_map.69), channel_id=1, source_target_pairs={{0,128},{16,144},{32,160},{48,176},{64,192},{80,208},{96,224},{112... | collective-permute-start | bytes 49160 | tf_op jit(solution)/shard_map/ppermute | solution.py:244
  80.2 4.1 %collective-permute-start.6 = (f32[2,32,128]{2,1,0:T(8,128)S(1)}, f32[2,32,128]{2,1,0:T(8,128)S(1)}, u32[]{:S(2)}, u32[]{:S(2)}) collective-permute-start(f32[2,32,128]{2,1,0:T(8,128)S(1)} %pad_maximum_fusion.15), channel_id=1, source_target_pairs={{0,64},{16,80},{32,96},{48,112},{64,0},{80,16},{96,32},{112,48},{1... | collective-permute-start | bytes 98312 | tf_op jit(solution)/shard_map/ppermute | solution.py:244
  88.6 6.4 %collective-permute-start.8 = (f32[2,2,2,32,128]{4,3,0,1,2:T(8,128)}, f32[2,2,2,32,128]{4,3,0,1,2:T(8,128)}, u32[]{:S(2)}, u32[]{:S(2)}) collective-permute-start(f32[2,2,2,32,128]{4,3,0,1,2:T(8,128)} %pad_maximum_fusion.7), channel_id=1, source_target_pairs={{0,16},{16,0},{32,48},{48,32},{64,80},{80,64},{96,112},{112,96},{1... | collective-permute-start | bytes 393224 | tf_op jit(solution)/shard_map/ppermute | solution.py:244
  102.9 6.6 %collective-permute-start.9 = (f32[32,128]{1,0:T(8,128)S(1)}, f32[32,128]{1,0:T(8,128)S(1)}, u32[]{:S(2)}, u32[]{:S(2)}) collective-permute-start(f32[32,128]{1,0:T(8,128)S(1)} %sub.8), channel_id=1, source_target_pairs={{0,128},{16,144},{32,160},{48,176},{64,192},{80,208},{96,224},{112... | collective-permute-start | bytes 49160 | tf_op jit(solution)/shard_map/ppermute | solution.py:244
  109.5 10.9 %collective-permute-start.10 = (f32[2,32,128]{2,1,0:T(8,128)S(1)}, f32[2,32,128]{2,1,0:T(8,128)S(1)}, u32[]{:S(2)}, u32[]{:S(2)}) collective-permute-start(f32[2,32,128]{2,1,0:T(8,128)S(1)} %pad_maximum_fusion.16), channel_id=1, source_target_pairs={{0,64},{16,80},{32,96},{48,112},{64,0},{80,16},{96,32},{112,48},{1... | collective-permute-start | bytes 98312 | tf_op jit(solution)/shard_map/ppermute | solution.py:244
  113.6 48.4 %all-to-all-start.2 = ((f32[16,46,8,128]{3,2,1,0:T(8,128)}), f32[16,46,8,128]{3,2,1,0:T(8,128)}, u32[]{:S(2)}, u32[]{:S(2)}) async-start(f32[16,46,8,128]{3,2,1,0:T(8,128)} %copy_bitcast_fusion.1), calls=%async_computation.2 | async-start | bytes 6029312 | tf_op jit(solution)/shard_map/all_to_all | solution.py:231
  124.1 3.9 %collective-permute-start.12 = (f32[2,2,2,32,128]{4,3,0,1,2:T(8,128)S(1)}, f32[2,2,2,32,128]{4,3,0,1,2:T(8,128)S(1)}, u32[]{:S(2)}, u32[]{:S(2)}) collective-permute-start(f32[2,2,2,32,128]{4,3,0,1,2:T(8,128)S(1)} %pad_maximum_fusion.8), channel_id=1, source_target_pairs={{0,16},{16,0},{32,48},{48,32},{64,80},{80,64},{96,112},{112,96},{1... | collective-permute-start | bytes 393224 | tf_op jit(solution)/shard_map/ppermute | solution.py:244
  131.8 6.8 %collective-permute-start.13 = (f32[32,128]{1,0:T(8,128)}, f32[32,128]{1,0:T(8,128)S(1)}, u32[]{:S(2)}, u32[]{:S(2)}) collective-permute-start(f32[32,128]{1,0:T(8,128)} %shard_map.72), channel_id=1, source_target_pairs={{0,128},{16,144},{32,160},{48,176},{64,192},{80,208},{96,224},{112... | collective-permute-start | bytes 49160 | tf_op jit(solution)/shard_map/ppermute | solution.py:244
  139.4 4.1 %collective-permute-start.14 = (f32[2,32,128]{2,1,0:T(8,128)S(1)}, f32[2,32,128]{2,1,0:T(8,128)S(1)}, u32[]{:S(2)}, u32[]{:S(2)}) collective-permute-start(f32[2,32,128]{2,1,0:T(8,128)S(1)} %pad_maximum_fusion.17), channel_id=1, source_target_pairs={{0,64},{16,80},{32,96},{48,112},{64,0},{80,16},{96,32},{112,48},{1... | collective-permute-start | bytes 98312 | tf_op jit(solution)/shard_map/ppermute | solution.py:244
  147.1 4.3 %collective-permute-start.16 = (f32[2,2,2,32,128]{4,3,0,1,2:T(8,128)S(1)}, f32[2,2,2,32,128]{4,3,0,1,2:T(8,128)S(1)}, u32[]{:S(2)}, u32[]{:S(2)}) collective-permute-start(f32[2,2,2,32,128]{4,3,0,1,2:T(8,128)S(1)} %pad_maximum_fusion.9), channel_id=1, source_target_pairs={{0,16},{16,0},{32,48},{48,32},{64,80},{80,64},{96,112},{112,96},{1... | collective-permute-start | bytes 393224 | tf_op jit(solution)/shard_map/ppermute | solution.py:244
  170.2 10.0 %collective-permute-start.17 = (f32[16,8,32,128]{3,2,1,0:T(8,128)}, f32[16,8,32,128]{3,2,1,0:T(8,128)}, u32[]{:S(2)}, u32[]{:S(2)}) collective-permute-start(f32[16,8,32,128]{3,2,1,0:T(8,128)} %shard_map.74.mine_ref.one_ref), channel_id=1, source_target_pairs={{0,16},{16,0},{32,48},{48,32},{64,80},{80,64},{96,112},{112,96},{1... | collective-permute-start | bytes 6291464 | tf_op jit(solution)/shard_map/ppermute | solution.py:367
  172.5 38.4 %all-to-all-start.3 = ((f32[16,8,32,128]{3,2,1,0:T(8,128)}), f32[16,8,32,128]{3,2,1,0:T(8,128)}, u32[]{:S(2)}, u32[]{:S(2)}) async-start(f32[16,8,32,128]{3,2,1,0:T(8,128)} %broadcast_in_dim.4), calls=%async_computation.3 | async-start | bytes 4194304 | tf_op jit(solution)/shard_map/all_to_all | solution.py:231
  211.0 5.3 %collective-permute-start.18 = (f32[16,8,32,128]{3,2,1,0:T(8,128)}, f32[16,8,32,128]{3,2,1,0:T(8,128)}, u32[]{:S(2)}, u32[]{:S(2)}) collective-permute-start(f32[16,8,32,128]{3,2,1,0:T(8,128)} %shard_map.76.mine_ref.two_ref), channel_id=1, source_target_pairs={{0,16},{16,0},{32,48},{48,32},{64,80},{80,64},{96,112},{112,96},{1... | collective-permute-start | bytes 6291464 | tf_op jit(solution)/shard_map/ppermute | solution.py:369
  248.2 3.8 %collective-permute-start.21 = (f32[40,128]{1,0:T(8,128)S(1)}, f32[40,128]{1,0:T(8,128)S(1)}, u32[]{:S(2)}, u32[]{:S(2)}) collective-permute-start(f32[40,128]{1,0:T(8,128)S(1)} %add.21), channel_id=1, source_target_pairs={{0,64},{16,80},{32,96},{48,112},{64,0},{80,16},{96,32},{112,48},{1... | collective-permute-start | bytes 61448 | tf_op jit(solution)/shard_map/ppermute | solution.py:377
  251.9 6.9 %collective-permute-start.22 = (f32[40,128]{1,0:T(8,128)S(1)}, f32[40,128]{1,0:T(8,128)S(1)}, u32[]{:S(2)}, u32[]{:S(2)}) collective-permute-start(f32[40,128]{1,0:T(8,128)S(1)} %add.22), channel_id=1, source_target_pairs={{0,128},{16,144},{32,160},{48,176},{64,192},{80,208},{96,224},{112... | collective-permute-start | bytes 61448 | tf_op jit(solution)/shard_map/ppermute | solution.py:377
  269.5 7.3 %collective-permute-start.23 = (f32[5,128,128]{2,1,0:T(8,128)S(1)}, f32[5,128,128]{2,1,0:T(8,128)S(1)}, u32[]{:S(2)}, u32[]{:S(2)}) collective-permute-start(f32[5,128,128]{2,1,0:T(8,128)S(1)} %bitcast.115), channel_id=1, source_target_pairs={{0,16},{16,0},{32,48},{48,32},{64,80},{80,64},{96,112},{112,96},{1... | collective-permute-start | bytes 983048 | tf_op jit(solution)/shard_map/ppermute | solution.py:380
  (10 other events, 182.0 us)
Sparse Core Ops, SparseCore 0:
  11.0 56.3 all-gather.4
  99.1 71.0 all-gather.6
